TPU v7x, 32 devices: a whole 2x2x4 slice. The times are simulated.
32 devices in a mesh: param: 8 (over y, x, core), walker: 4 (over z).
Axes of the slice: x: 2, y: 2, z: 4, core: 2. Of those that a mesh axis runs over, the one named last changes fastest.
Arguments:
- derivs: float32 [32, 4980736], P('walker', 'param'), may hold values from -1.7 to 1.7
- gradient: float32 [4980736], P('param'), may hold values from -0.01171875 to 0.01171875
Outputs:
- solution: float32 [4980736], P(('param', 'walker'))
All inputs are finite; a program needn't handle non-finite values.
Results may differ from a plain program's by a relative error of at most 0.0003.
Values sent between devices are 32-bit elements; how exact they have to be, the bound alone decides.
No kernel may reach another device: no remote copies, remote signals or barrier semaphores. Data moves between devices by JAX's collectives and lax.ppermute only.
A program may use at most 64 MiB of HBM per device.

v0:
```python
import jax
import jax.numpy as jnp
from jax import lax
from jax.sharding import PartitionSpec as P

ITERS = 3


DAMPING = 0.001


def body(derivs, gradient):
    walkers = lax.axis_size("walker")
    rows_all = derivs.shape[0] * walkers
    share_len = gradient.shape[0] // walkers
    offset = lax.axis_index("walker") * share_len

    def own_share(vector):
        return lax.dynamic_slice_in_dim(vector, offset, share_len, 0)

    def local_view(vector):
        return own_share(vector)

    def squares(vector):
        return lax.psum(jnp.sum(vector * vector), ("param", "walker"))

    solution = jnp.zeros_like(gradient)
    residual = gradient
    direction = gradient
    norm_now = squares(local_view(gradient))
    for step_idx in range(ITERS):
        row_part = jnp.dot(derivs, direction, precision=lax.Precision.HIGHEST)
        row_vals = lax.psum(row_part, "param")
        back_vals = lax.psum(jnp.dot(row_vals, derivs, precision=lax.Precision.HIGHEST), "walker")
        image = back_vals / rows_all + DAMPING * direction
        advance_solution = solution
        advance_residual = residual
        dir_view = local_view(direction)
        img_view = local_view(image)
        curv_pq = lax.psum(jnp.sum(dir_view * img_view), ("param", "walker"))
        step_len = norm_now / curv_pq
        advance_residual = advance_residual - step_len * image
        norm_next = squares(local_view(advance_residual))
        advance_solution = advance_solution + step_len * direction
        solution, residual, norm_next = (advance_solution, advance_residual, norm_next)
        direction = residual + norm_next / norm_now * direction
        norm_now = norm_next
    return own_share(solution)


def solution(mesh):
    in_specs = (P("walker", "param"), P("param"))
    out_specs = P(("param", "walker"))
    return jax.shard_map(body, mesh=mesh, in_specs=in_specs, out_specs=out_specs, check_vma=False)
```

profile of v0, /device:TPU:0, one launch (start us, length us, event | category | flops | bytes accessed | tf_op | source)
XLA Modules:
  0.0 797.7 jit_solution(4806930503922329819)
XLA Ops:
  6.5 0.0 all-reduce.5.cloned.1.call-start
  6.5 45.5 %convolution_bitcast_fusion.2 = f32[8]{0:T(128)S(1)} fusion(f32[8,622592]{1,0:T(8,128)} %param.2, f32[622592,1]{0,1:T(1,128)} %bitcast.30), kind=kOutput, calls=%fused_computation.8 | convolution fusion | flops 59768832 | bytes 22413344 | tf_op jit(solution)/shard_map/dot_general | solution.py:32
  52.0 15.1 %psum.85 = f32[8]{0:T(128)S(1)} all-reduce(f32[8]{0:T(128)S(1)} %convolution_bitcast_fusion.2), channel_id=1, replica_groups=mesh['param'=8,'walker'=4] {'param'}, use_global_device_ids=true, to_apply=%region_2.0 | all-reduce | flops 8 | bytes 64 | tf_op jit(solution)/shard_map/psum | solution.py:33
  67.1 22.2 %fusion.7 = f32[1,622592]{1,0:T(1,128)} fusion(f32[8,622592]{1,0:T(8,128)} %param.2, f32[8]{0:T(128)S(1)} %psum.85), kind=kOutput, calls=%fused_computation.23 | convolution fusion | flops 59768832 | bytes 22413344 | tf_op jit(solution)/shard_map/dot_general | solution.py:34
  89.3 0.0 copy-start
  89.3 0.0 all-reduce.5.cloned.1.call-update
  89.3 0.0 all-reduce.7.cloned.1.call-start
  89.4 99.3 %all-reduce.5.cloned.1.call-done = f32[622592]{0:T(1024)} async-done(((f32[622592]{0:T(1024)}), f32[622592]{0:T(1024)}) %all-reduce.5.cloned.1.call-update) | async-done | bytes 2490384 | tf_op jit(solution)/shard_map/psum | solution.py:34
  188.7 0.0 copy-done
  188.7 2.0 multiply_add_fusion.3
  190.8 0.9 multiply_reduce_fusion.3
  191.6 39.8 %all-reduce = (f32[]{:T(128)}, f32[]{:T(128)}) all-reduce(f32[]{:T(128)} %get-tuple-element.6, f32[]{:T(128)} %get-tuple-element.5), channel_id=1, replica_groups=mesh['param'=8,'walker'=4] {'param','walker'}, use_global_device_ids=true, to_apply=%region_1.0 | all-reduce | flops 2 | bytes 16 | tf_op jit(solution)/shard_map/psum | solution.py:25
  232.7 2.1 multiply_subtract_fusion.1
  234.8 0.0 copy-start.2
  234.8 1.4 copy-done.2
  236.3 0.8 multiply_reduce_fusion.2
  237.0 40.3 %psum.88 = f32[]{:T(128)} all-reduce(f32[]{:T(128)} %multiply_reduce_fusion.2), channel_id=1, replica_groups=mesh['param'=8,'walker'=4] {'param','walker'}, use_global_device_ids=true, to_apply=%region_7.0 | all-reduce | flops 1 | bytes 8 | tf_op jit(solution)/shard_map/psum | solution.py:25
  278.6 1.9 multiply_add_fusion.2
  280.6 0.0 copy-start.1
  280.6 1.4 copy-done.1
  282.0 45.5 %convolution_bitcast_fusion.1 = f32[8]{0:T(128)S(1)} fusion(f32[622592,1]{0,1:T(1,128)S(1)} %bitcast.31, f32[8,622592]{1,0:T(8,128)} %param.2), kind=kOutput, calls=%fused_computation.7 | convolution fusion | flops 59768832 | bytes 22413344 | tf_op jit(solution)/shard_map/dot_general | solution.py:32
  327.6 12.9 %psum.89 = f32[8]{0:T(128)S(1)} all-reduce(f32[8]{0:T(128)S(1)} %convolution_bitcast_fusion.1), channel_id=1, replica_groups=mesh['param'=8,'walker'=4] {'param'}, use_global_device_ids=true, to_apply=%region_8.0 | all-reduce | flops 8 | bytes 64 | tf_op jit(solution)/shard_map/psum | solution.py:33
  340.4 22.2 %fusion.5 = f32[1,622592]{1,0:T(1,128)} fusion(f32[8,622592]{1,0:T(8,128)} %param.2, f32[8]{0:T(128)S(1)} %psum.89), kind=kOutput, calls=%fused_computation.21 | convolution fusion | flops 59768832 | bytes 22413344 | tf_op jit(solution)/shard_map/dot_general | solution.py:34
  362.6 0.0 all-reduce.7.cloned.1.call-update
  362.6 0.0 all-reduce.9.cloned.1.call-start
  362.7 98.2 %all-reduce.7.cloned.1.call-done = f32[622592]{0:T(1024)} async-done(((f32[622592]{0:T(1024)}), f32[622592]{0:T(1024)}) %all-reduce.7.cloned.1.call-update) | async-done | bytes 2490384 | tf_op jit(solution)/shard_map/psum | solution.py:34
  460.9 2.8 multiply_add_fusion.1
  463.7 0.0 copy-start.4
  463.7 1.5 copy-done.4
  465.2 1.9 multiply_reduce_fusion.1
  467.1 39.5 %psum.91 = f32[]{:T(128)} all-reduce(f32[]{:T(128)} %multiply_reduce_fusion.1), channel_id=1, replica_groups=mesh['param'=8,'walker'=4] {'param','walker'}, use_global_device_ids=true, to_apply=%region_11.0 | all-reduce | flops 1 | bytes 8 | tf_op jit(solution)/shard_map/psum | solution.py:40
  507.9 2.7 multiply_subtract_fusion
  510.6 0.0 copy-start.5
  510.6 1.4 copy-done.5
  512.1 0.7 multiply_reduce_fusion
  512.8 49.0 %psum.92 = f32[]{:T(128)} all-reduce(f32[]{:T(128)} %multiply_reduce_fusion), channel_id=1, replica_groups=mesh['param'=8,'walker'=4] {'param','walker'}, use_global_device_ids=true, to_apply=%region_13.0 | all-reduce | flops 1 | bytes 8 | tf_op jit(solution)/shard_map/psum | solution.py:25
  563.1 2.7 multiply_add_fusion
  565.8 0.0 copy-start.3
  565.8 1.4 copy-done.3
  567.2 45.5 %convolution_bitcast_fusion = f32[8]{0:T(128)S(1)} fusion(f32[622592,1]{0,1:T(1,128)S(1)} %bitcast.32, f32[8,622592]{1,0:T(8,128)} %param.2), kind=kOutput, calls=%fused_computation.6 | convolution fusion | flops 59768832 | bytes 22413344 | tf_op jit(solution)/shard_map/dot_general | solution.py:32
  612.8 12.8 %psum.93 = f32[8]{0:T(128)S(1)} all-reduce(f32[8]{0:T(128)S(1)} %convolution_bitcast_fusion), channel_id=1, replica_groups=mesh['param'=8,'walker'=4] {'param'}, use_global_device_ids=true, to_apply=%region_14.0 | all-reduce | flops 8 | bytes 64 | tf_op jit(solution)/shard_map/psum | solution.py:33
  625.6 22.2 %fusion.3 = f32[1,622592]{1,0:T(1,128)} fusion(f32[8,622592]{1,0:T(8,128)} %param.2, f32[8]{0:T(128)S(1)} %psum.93), kind=kOutput, calls=%fused_computation.19 | convolution fusion | flops 59768832 | bytes 22413344 | tf_op jit(solution)/shard_map/dot_general | solution.py:34
  647.8 0.0 all-reduce.9.cloned.1.call-update
  647.8 98.2 %all-reduce.9.cloned.1.call-done = f32[622592]{0:T(1024)} async-done(((f32[622592]{0:T(1024)}), f32[622592]{0:T(1024)}) %all-reduce.9.cloned.1.call-update) | async-done | bytes 2490384 | tf_op jit(solution)/shard_map/psum | solution.py:34
  746.0 2.0 fusion.2
  748.1 39.5 %psum.95 = f32[]{:T(128)} all-reduce(f32[]{:T(128)} %fusion.2), channel_id=1, replica_groups=mesh['param'=8,'walker'=4] {'param','walker'}, use_global_device_ids=true, to_apply=%region_17.0 | all-reduce | flops 1 | bytes 8 | tf_op jit(solution)/shard_map/psum | solution.py:40
  788.8 2.2 multiply_add_fusion.4
Async XLA Ops:
  6.5 182.2 %all-reduce.5.cloned.1.call-start = ((), (), s32[]{:S(2)}) async-start(), calls=%async_computation | async-start | bytes 4980736 | tf_op jit(solution)/shard_map/psum | solution.py:34
  89.3 99.4 %copy-start = (f32[622592]{0:T(1024)S(1)}, f32[622592]{0:T(1024)}, u32[]{:S(2)}) copy-start(f32[622592]{0:T(1024)} %param.3) | copy-start | bytes 7471108
  89.3 371.6 %all-reduce.7.cloned.1.call-start = ((), (), s32[]{:S(2)}) async-start(), calls=%async_computation.1 | async-start | bytes 4980736 | tf_op jit(solution)/shard_map/psum | solution.py:34
  234.8 1.5 copy-start.2
  280.6 1.4 copy-start.1
  362.6 383.4 %all-reduce.9.cloned.1.call-start = ((), (), s32[]{:S(2)}) async-start(), calls=%async_computation.2 | async-start | bytes 4980736 | tf_op jit(solution)/shard_map/psum | solution.py:34
  463.7 1.5 copy-start.4
  510.6 1.5 copy-start.5
  565.8 1.5 copy-start.3
Sparse Core Ops, SparseCore 0:
  89.5 99.2 all-reduce.4
  362.8 98.1 all-reduce.6
  647.9 98.0 all-reduce.8
where the time goes:
time: 807 us; the launch traced here: 798 us
  waiting for transfers between devices  296 us (37%)
  blocking collectives  249 us (31%)
  matrix products  203 us (25%)
  other arithmetic  22.8 us (3%)
  between operations  19.8 us (2%)
    psum x3, waiting for transfers between devices, body(): lax.psum(jnp.dot(row_vals, derivs, precision=lax.Precision.HIGHEST), 'wal...  296 us
    dot_general x3, matrix products, body(): row_part = jnp.dot(derivs, direction, precision=lax.Precision.HIGHEST)  136 us
    psum x3, blocking collectives, squares(): return lax.psum(jnp.sum(vector * vector), ('param', 'walker'))  129 us
    psum x2, blocking collectives, body(): curv_pq = lax.psum(jnp.sum(dir_view * img_view), ('param', 'walker'))  78.9 us
    dot_general x3, matrix products, body(): jnp.dot(row_vals, derivs, precision=lax.Precision.HIGHEST)  66.5 us
    psum x3, blocking collectives, body(): row_vals = lax.psum(row_part, 'param')  40.8 us
  transfers between devices with their start and end apart: 3, of which 3 were waited for; matrix products, arithmetic and copies ran while one was open for 0% of the time, Pallas kernels for 0%

commit v1 on v0

v1 whole, which is shorter than its diff:
```python
import functools

import jax
import jax.numpy as jnp
from jax import lax
from jax.experimental import pallas as pl
from jax.experimental.pallas import tpu as pltpu
from jax.sharding import PartitionSpec as P

DAMPING = 0.001
LANES = 128
SUBLANES = 8
BLOCK_ROWS_MAX = 320
GROUP = 8


def block_rows(rows):
    return max(b for b in range(SUBLANES, BLOCK_ROWS_MAX + 1, SUBLANES) if rows % b == 0)


def lane_total(tile):
    return jnp.broadcast_to(jnp.sum(tile, axis=1, keepdims=True), tile.shape)


def all_total(tile):
    return jnp.broadcast_to(jnp.sum(jnp.sum(tile, axis=0, keepdims=True), axis=1, keepdims=True), tile.shape)


def tile_of(derivs_ref, row):
    return derivs_ref[:, pl.ds(pl.multiple_of(row * LANES, LANES), LANES)]


def products(derivs_ref, vec_ref, rows):
    def step(i, accs):
        accs = list(accs)
        base = i * GROUP
        for s in range(GROUP):
            row = base + s
            lane_vals = jnp.broadcast_to(vec_ref[pl.ds(row, 1), :], (SUBLANES, LANES))
            accs[s % 4] = accs[s % 4] + tile_of(derivs_ref, row) * lane_vals
        return tuple(accs)

    zero = jnp.zeros((SUBLANES, LANES), jnp.float32)
    accs = lax.fori_loop(0, rows // GROUP, step, (zero,) * 4)
    return (accs[0] + accs[1]) + (accs[2] + accs[3])


def tile_sum(block):
    return jnp.sum(block.reshape(-1, SUBLANES, LANES), axis=0)


def start_kernel(steps, derivs_ref, grad_ref, stats_ref):
    step = pl.program_id(0)

    @pl.when(step == 0)
    def _():
        stats_ref[...] = jnp.zeros_like(stats_ref)

    stats_ref[0:8, :] += products(derivs_ref, grad_ref, grad_ref.shape[0])
    grad = grad_ref[...]
    stats_ref[8:16, :] += tile_sum(grad * grad)

    @pl.when(step == steps - 1)
    def _():
        stats_ref[0:8, :] = lane_total(stats_ref[0:8, :])
        stats_ref[8:16, :] = all_total(stats_ref[8:16, :])


def start_call(derivs, grad):
    rows = grad.shape[0]
    blk = block_rows(rows)
    steps = rows // blk
    return pl.pallas_call(
        functools.partial(start_kernel, steps),
        grid=(steps,),
        in_specs=[
            pl.BlockSpec((SUBLANES, blk * LANES), lambda i: (0, i)),
            pl.BlockSpec((blk, LANES), lambda i: (i, 0)),
        ],
        out_specs=pl.BlockSpec((24, LANES), lambda i: (0, 0)),
        out_shape=jax.ShapeDtypeStruct((24, LANES), jnp.float32),
        name="start_products",
    )(derivs, grad)


def back_kernel(derivs_ref, vals_ref, out_ref):
    vals = vals_ref[...]

    def step(i, carry):
        base = i * GROUP
        for s in range(GROUP):
            row = base + s
            out_ref[pl.ds(row, 1), :] = jnp.sum(tile_of(derivs_ref, row) * vals, axis=0, keepdims=True)
        return carry

    lax.fori_loop(0, out_ref.shape[0] // GROUP, step, 0)


def back_call(derivs, vals, rows):
    blk = block_rows(rows)
    return pl.pallas_call(
        back_kernel,
        grid=(rows // blk,),
        in_specs=[
            pl.BlockSpec((SUBLANES, blk * LANES), lambda i: (0, i)),
            pl.BlockSpec((SUBLANES, LANES), lambda i: (0, 0)),
        ],
        out_specs=pl.BlockSpec((blk, LANES), lambda i: (i, 0)),
        out_shape=jax.ShapeDtypeStruct((rows, LANES), jnp.float32),
        name="back_products",
    )(derivs, vals)


def advance_kernel(steps, scale, derivs_ref, res_ref, back_ref, dir_ref, step_ref, new_ref, stats_ref):
    step = pl.program_id(0)

    @pl.when(step == 0)
    def _():
        stats_ref[...] = jnp.zeros_like(stats_ref)

    step_len = step_ref[0:1, :]
    beta = step_ref[1:2, :]
    direction = res_ref[...] + beta * dir_ref[...]
    new = res_ref[...] - step_len * (back_ref[...] * scale + DAMPING * direction)
    new_ref[...] = new
    stats_ref[8:16, :] += tile_sum(new * new)
    stats_ref[16:24, :] += tile_sum(new * direction)
    stats_ref[0:8, :] += products(derivs_ref, new_ref, new_ref.shape[0])

    @pl.when(step == steps - 1)
    def _():
        stats_ref[0:8, :] = lane_total(stats_ref[0:8, :])
        stats_ref[8:16, :] = all_total(stats_ref[8:16, :])
        stats_ref[16:24, :] = all_total(stats_ref[16:24, :])


def advance_call(derivs, residual, back, prev_direction, step_len, beta, rows_all):
    rows = residual.shape[0]
    blk = block_rows(rows)
    steps = rows // blk
    scalars = jnp.concatenate([step_len, beta, jnp.zeros((6, LANES), jnp.float32)])
    vec = pl.BlockSpec((blk, LANES), lambda i: (i, 0))
    return pl.pallas_call(
        functools.partial(advance_kernel, steps, 1.0 / rows_all),
        grid=(steps,),
        in_specs=[
            pl.BlockSpec((SUBLANES, blk * LANES), lambda i: (0, i)),
            vec,
            vec,
            vec,
            pl.BlockSpec((SUBLANES, LANES), lambda i: (0, 0)),
        ],
        out_specs=[vec, pl.BlockSpec((24, LANES), lambda i: (0, 0))],
        out_shape=[
            jax.ShapeDtypeStruct((rows, LANES), jnp.float32),
            jax.ShapeDtypeStruct((24, LANES), jnp.float32),
        ],
        name="advance_residual",
    )(derivs, residual, back, prev_direction, scalars)


def last_kernel(share_ref, grad_ref, res1_ref, res2_ref, coef_ref, out_ref):
    c0, c1, c2 = coef_ref[0:1, :], coef_ref[1:2, :], coef_ref[2:3, :]
    out_ref[...] = c0 * grad_ref[...] + c1 * res1_ref[...] + c2 * res2_ref[...]


def last_call(share, grad, res1, res2, coefs, share_rows):
    vec = pl.BlockSpec((share_rows, LANES), lambda i, share_ref: (share_ref[0], 0))
    return pl.pallas_call(
        last_kernel,
        grid_spec=pltpu.PrefetchScalarGridSpec(
            num_scalar_prefetch=1,
            grid=(1,),
            in_specs=[vec, vec, vec, pl.BlockSpec((SUBLANES, LANES), lambda i, share_ref: (0, 0))],
            out_specs=pl.BlockSpec((share_rows, LANES), lambda i, share_ref: (0, 0)),
        ),
        out_shape=jax.ShapeDtypeStruct((share_rows, LANES), jnp.float32),
        name="last_combination",
    )(share, grad, res1, res2, coefs)


def small_sum(value, axis):
    size = lax.axis_size(axis)
    if size & (size - 1):
        return lax.psum(value, axis)
    bit = 1
    while bit < size:
        value = value + lax.ppermute(value, axis, [(i, i ^ bit) for i in range(size)])
        bit *= 2
    return value


def big_sum(value):
    return lax.psum(value, "walker")


def body(derivs, gradient):
    walkers = lax.axis_size("walker")
    rows_all = derivs.shape[0] * walkers
    rows = gradient.shape[0] // LANES
    grad = gradient.reshape(rows, LANES)

    def walker_squares(vals):
        return small_sum(jnp.sum(vals * vals, axis=0, keepdims=True), "walker")

    stats = small_sum(start_call(derivs, grad), "param")
    vals0, norm0 = stats[0:8], stats[8:9]
    back0 = big_sum(back_call(derivs, vals0, rows))
    dir_sq0 = norm0
    step0 = norm0 / (walker_squares(vals0) / rows_all + DAMPING * dir_sq0)
    zero = jnp.zeros_like(norm0)
    res1, stats = advance_call(derivs, grad, back0, grad, step0, zero, rows_all)

    stats = small_sum(stats, "param")
    norm1, cross1 = stats[8:9], stats[16:17]
    beta1 = norm1 / norm0
    vals1 = stats[0:8] + beta1 * vals0
    back1 = big_sum(back_call(derivs, vals1, rows))
    dir_sq1 = norm1 + 2.0 * beta1 * cross1 + beta1 * beta1 * dir_sq0
    step1 = norm1 / (walker_squares(vals1) / rows_all + DAMPING * dir_sq1)
    res2, stats = advance_call(derivs, res1, back1, grad, step1, beta1, rows_all)

    stats = small_sum(stats, "param")
    norm2, cross2 = stats[8:9], stats[16:17]
    beta2 = norm2 / norm1
    vals2 = stats[0:8] + beta2 * vals1
    dir_sq2 = norm2 + 2.0 * beta2 * cross2 + beta2 * beta2 * dir_sq1
    step2 = norm2 / (walker_squares(vals2) / rows_all + DAMPING * dir_sq2)

    along1 = step1 + step2 * beta2
    coefs = jnp.concatenate([step0 + along1 * beta1, along1, step2, jnp.zeros((5, LANES), jnp.float32)])
    share = lax.axis_index("walker").astype(jnp.int32).reshape(1)
    out = last_call(share, grad, res1, res2, coefs, rows // walkers)
    return out.reshape(-1)


def solution(mesh):
    in_specs = (P("walker", "param"), P("param"))
    out_specs = P(("param", "walker"))
    return jax.shard_map(body, mesh=mesh, in_specs=in_specs, out_specs=out_specs, check_vma=False)
```

time: 807 us -> 350 us (0.43)
  blocking collectives: 249 us -> 0 us
  matrix products: 203 us -> 0 us
  Pallas kernels: 0 us -> 94.1 us
  waiting for transfers between devices: 296 us -> 215 us
  starting transfers between devices: 0.09 us -> 19.5 us
  other arithmetic: 22.8 us -> 5.43 us
    psum x8 -> x0, blocking collectives: 249 us -> none  [the longest x3 129 us: squares(): return lax.psum(jnp.sum(vector * vector), ('param', 'walker'))]
    dot_general x6 -> x0, matrix products: 203 us -> none  [the longest x3 136 us: body(): row_part = jnp.dot(derivs, direction, precision=lax.Precision.HIGHEST)]
    psum x3 -> x2, waiting for transfers between devices: 296 us -> 183 us  [big_sum(): return lax.psum(value, 'walker')]
    pallas_call x0 -> x6, Pallas kernels: none -> 94.1 us  [the longest x2 37.8 us: advance_call(): pl.pallas_call(functools.partial(advance_kernel, steps, 1.0 / rows_all),...]
    ppermute x0 -> x15, waiting for transfers between devices: none -> 32 us  [small_sum(): lax.ppermute(value, axis, [(i, i ^ bit) for i in range(size)])]
    ppermute x0 -> x15, starting transfers between devices: none -> 19.4 us  [small_sum(): lax.ppermute(value, axis, [(i, i ^ bit) for i in range(size)])]
    add x5 -> x13, other arithmetic: 11.6 us -> 2.18 us  [the longest x12 2.16 us: small_sum(): value + lax.ppermute(value, axis, [(i, i ^ bit) for i in range(size)])]
  transfers between devices with their start and end apart: 3 -> 17, of which waited for: 3 -> 17; matrix products, arithmetic and copies ran while one was open for 0% -> 0% of each run, Pallas kernels for 0% -> 0%
where the time goes in v1:
time: 350 us; the launch traced here: 348 us
  waiting for transfers between devices  215 us (61%)
  Pallas kernels  94.1 us (27%)
  starting transfers between devices  19.5 us (6%)
  between operations  13.4 us (4%)
  other arithmetic  5.43 us (2%)
    psum x2, waiting for transfers between devices, big_sum(): return lax.psum(value, 'walker')  183 us
    pallas_call x2, Pallas kernels, advance_call(): pl.pallas_call(functools.partial(advance_kernel, steps, 1.0 / rows_all),...  37.8 us
    pallas_call x2, Pallas kernels, back_call(): pl.pallas_call(back_kernel, grid=(rows // blk,), in_specs=[pl.BlockSpec((...  36.9 us
    ppermute x15, waiting for transfers between devices, small_sum(): lax.ppermute(value, axis, [(i, i ^ bit) for i in range(size)])  32 us
    ppermute x15, starting transfers between devices, small_sum(): lax.ppermute(value, axis, [(i, i ^ bit) for i in range(size)])  19.4 us
    pallas_call x1, Pallas kernels, start_call(): pl.pallas_call(functools.partial(start_kernel, steps), grid=(steps,), in_...  17 us
  transfers between devices with their start and end apart: 17, of which 17 were waited for; matrix products, arithmetic and copies ran while one was open for 0% of the time, Pallas kernels for 0%

profile of v1, /device:TPU:0, one launch (start us, length us, event | category | flops | bytes accessed | tf_op | source)
XLA Modules:
  0.0 347.7 jit_solution(9720857721745740806)
XLA Ops:
  6.5 17.0 %start_products.1 = f32[24,128]{1,0:T(8,128)} custom-call(f32[8,622592]{1,0:T(8,128)} %derivs_ref.9, f32[4864,128]{1,0:T(8,128)} %bitcast.12), custom_call_target="tpu_custom_call" | custom-call | tf_op jit(solution)/shard_map/start_products/pallas_call | solution.py:73
  23.5 0.5 collective-permute-start
  24.0 1.0 collective-permute-done
  25.0 0.7 add.82
  25.7 2.8 collective-permute-start.1
  28.6 1.7 collective-permute-done.1
  30.2 2.1 collective-permute-start.2
  32.3 1.7 collective-permute-done.2
  34.0 0.6 multiply_reduce_fusion.1
  34.6 18.4 %back_products.2 = f32[4864,128]{1,0:T(8,128)} custom-call(f32[8,622592]{1,0:T(8,128)} %derivs_ref.9, f32[8,128]{1,0:T(8,128)} %get-tuple-element.21.vals_ref), custom_call_target="tpu_custom_call" | custom-call | tf_op jit(solution)/shard_map/back_products/pallas_call | solution.py:101
  53.0 0.0 all-reduce.5.cloned.1.call-start
  53.1 2.1 collective-permute-start.3
  55.2 1.5 collective-permute-done.3
  56.7 3.0 collective-permute-start.4
  59.8 0.1 pad.9.clone
  59.8 0.1 pad.8.clone
  59.9 1.4 collective-permute-done.4
  61.3 0.7 maximum_maximum_fusion.step_ref
  62.0 92.8 %all-reduce.3.cloned.1.call-done.back_ref = f32[4864,128]{1,0:T(8,128)} async-done(((f32[4864,128]{1,0:T(8,128)}), f32[4864,128]{1,0:T(8,128)}) %all-reduce.3.cloned.1.call-update) | async-done | bytes 2490384 | tf_op jit(solution)/shard_map/psum | solution.py:194
  154.8 19.1 %advance_residual.2 = (f32[4864,128]{1,0:T(8,128)}, f32[24,128]{1,0:T(8,128)}) custom-call(f32[8,622592]{1,0:T(8,128)} %derivs_ref.9, f32[4864,128]{1,0:T(8,128)} %bitcast.13, f32[4864,128]{1,0:T(8,128)} %all-reduce.3.cloned.1.call-done.back_ref, f32[4864,128]{1,0:T(8,128)} %bitcast.14, f32[8,128]{1,0:T(8,128)} %maximum_maximum_fusion.step_ref), custom_call_target="tpu_custom_call" | custom-call | tf_op jit(solution)/shard_map/advance_residual/pallas_call | solution.py:143
  173.9 1.4 collective-permute-done.5
  175.3 0.7 add.88
  176.0 1.5 collective-permute-start.6
  177.5 2.2 collective-permute-done.6
  179.7 1.5 collective-permute-start.7
  181.2 2.2 collective-permute-done.7
  183.4 0.6 multiply_reduce_fusion
  184.0 18.4 %back_products.3 = f32[4864,128]{1,0:T(8,128)} custom-call(f32[8,622592]{1,0:T(8,128)} %derivs_ref.9, f32[8,128]{1,0:T(8,128)} %get-tuple-element.19.vals_ref), custom_call_target="tpu_custom_call" | custom-call | tf_op jit(solution)/shard_map/back_products/pallas_call | solution.py:101
  202.5 0.1 collective-permute-start.8
  202.6 3.5 %collective-permute-done.8 = f32[1,128]{1,0:T(1,128)S(1)} collective-permute-done((f32[1,128]{1,0:T(1,128)S(1)}, f32[1,128]{1,0:T(1,128)S(1)}, u32[]{:S(2)}, u32[]{:S(2)}) %collective-permute-start.8) | collective-permute-done | bytes 544 | tf_op jit(solution)/shard_map/ppermute | solution.py:188
  206.1 1.4 collective-permute-start.9
  207.5 3.1 collective-permute-done.9
  210.6 0.7 maximum_maximum_fusion.1.step_ref
  211.3 90.2 %all-reduce.5.cloned.1.call-done.back_ref = f32[4864,128]{1,0:T(8,128)} async-done(((f32[4864,128]{1,0:T(8,128)}), f32[4864,128]{1,0:T(8,128)}) %all-reduce.5.cloned.1.call-update) | async-done | bytes 2490384 | tf_op jit(solution)/shard_map/psum | solution.py:194
  301.5 18.7 %advance_residual.3 = (f32[4864,128]{1,0:T(8,128)}, f32[24,128]{1,0:T(8,128)}) custom-call(f32[8,622592]{1,0:T(8,128)} %derivs_ref.9, f32[4864,128]{1,0:T(8,128)} %get-tuple-element.9.res_ref.res1_ref, f32[4864,128]{1,0:T(8,128)} %all-reduce.5.cloned.1.call-done.back_ref, f32[4864,128]{1,0:T(8,128)} %bitcast.15, f32[8,128]{1,0:T(8,128)} %maximum_maximum_fusion.1.step_ref), custom_call_target="tpu_custom_call" | custom-call | tf_op jit(solution)/shard_map/advance_residual/pallas_call | solution.py:143
  320.3 1.4 collective-permute-done.10
  321.7 0.7 add.97
  322.4 1.5 collective-permute-start.11
  323.8 2.2 collective-permute-done.11
  326.1 1.5 collective-permute-start.12
  327.5 2.2 collective-permute-done.12
  329.8 0.1 collective-permute-start.13
  329.9 3.5 %collective-permute-done.13 = f32[1,128]{1,0:T(1,128)S(1)} collective-permute-done((f32[1,128]{1,0:T(1,128)S(1)}, f32[1,128]{1,0:T(1,128)S(1)}, u32[]{:S(2)}, u32[]{:S(2)}) %collective-permute-start.13) | collective-permute-done | bytes 544 | tf_op jit(solution)/shard_map/ppermute | solution.py:188
  333.4 1.4 collective-permute-start.14
  334.9 0.1 pad.3.clone
  334.9 2.9 collective-permute-done.14
  337.9 0.7 maximum_maximum_fusion.2.coef_ref
  338.5 2.4 last_combination.1
  (24 shorter events, 0.1 us)
Async XLA Ops:
  6.5 148.3 %all-reduce.3.cloned.1.call-start = ((), (), s32[]{:S(2)}) async-start(), calls=%async_computation | async-start | bytes 4980736 | tf_op jit(solution)/shard_map/psum | solution.py:194
  23.5 1.5 collective-permute-start
  25.7 4.5 %collective-permute-start.1 = (f32[24,128]{1,0:T(8,128)S(1)}, f32[24,128]{1,0:T(8,128)S(1)}, u32[]{:S(2)}, u32[]{:S(2)}) collective-permute-start(f32[24,128]{1,0:T(8,128)S(1)} %add.82), channel_id=1, source_target_pairs={{0,8},{4,12},{8,0},{12,4},{16,24},{20,28},{24,16},{28,20},{1,9},{5... | collective-permute-start | bytes 36872 | tf_op jit(solution)/shard_map/ppermute | solution.py:188
  30.2 3.7 %collective-permute-start.2 = (f32[24,128]{1,0:T(8,128)S(1)}, f32[24,128]{1,0:T(8,128)S(1)}, u32[]{:S(2)}, u32[]{:S(2)}) collective-permute-start(f32[24,128]{1,0:T(8,128)S(1)} %add.83), channel_id=1, source_target_pairs={{0,16},{4,20},{8,24},{12,28},{16,0},{20,4},{24,8},{28,12},{1,17},{... | collective-permute-start | bytes 36872 | tf_op jit(solution)/shard_map/ppermute | solution.py:188
  53.0 248.5 %all-reduce.5.cloned.1.call-start = ((), (), s32[]{:S(2)}) async-start(), calls=%async_computation.1 | async-start | bytes 4980736 | tf_op jit(solution)/shard_map/psum | solution.py:194
  53.1 3.7 %collective-permute-start.3 = (f32[1,128]{1,0:T(1,128)S(1)}, f32[1,128]{1,0:T(1,128)S(1)}, u32[]{:S(2)}, u32[]{:S(2)}) collective-permute-start(f32[1,128]{1,0:T(1,128)S(1)} %bitcast.19), channel_id=1, source_target_pairs={{0,1},{1,0},{2,3},{3,2},{4,5},{5,4},{6,7},{7,6},{8,9},{9,8},{10,11... | collective-permute-start | bytes 1544 | tf_op jit(solution)/shard_map/ppermute | solution.py:188
  56.7 4.5 %collective-permute-start.4 = (f32[1,128]{1,0:T(1,128)S(1)}, f32[1,128]{1,0:T(1,128)S(1)}, u32[]{:S(2)}, u32[]{:S(2)}) collective-permute-start(f32[1,128]{1,0:T(1,128)S(1)} %bitcast_add_fusion.2), channel_id=1, source_target_pairs={{0,2},{1,3},{2,0},{3,1},{4,6},{5,7},{6,4},{7,5},{8,10},{9,11},{10,... | collective-permute-start | bytes 1544 | tf_op jit(solution)/shard_map/ppermute | solution.py:188
  173.9 1.4 collective-permute-start.5
  176.0 3.7 %collective-permute-start.6 = (f32[24,128]{1,0:T(8,128)S(1)}, f32[24,128]{1,0:T(8,128)S(1)}, u32[]{:S(2)}, u32[]{:S(2)}) collective-permute-start(f32[24,128]{1,0:T(8,128)S(1)} %add.88), channel_id=1, source_target_pairs={{0,8},{4,12},{8,0},{12,4},{16,24},{20,28},{24,16},{28,20},{1,9},{5... | collective-permute-start | bytes 36872 | tf_op jit(solution)/shard_map/ppermute | solution.py:188
  179.7 3.7 %collective-permute-start.7 = (f32[24,128]{1,0:T(8,128)S(1)}, f32[24,128]{1,0:T(8,128)S(1)}, u32[]{:S(2)}, u32[]{:S(2)}) collective-permute-start(f32[24,128]{1,0:T(8,128)S(1)} %add.89), channel_id=1, source_target_pairs={{0,16},{4,20},{8,24},{12,28},{16,0},{20,4},{24,8},{28,12},{1,17},{... | collective-permute-start | bytes 36872 | tf_op jit(solution)/shard_map/ppermute | solution.py:188
  202.5 3.6 %collective-permute-start.8 = (f32[1,128]{1,0:T(1,128)S(1)}, f32[1,128]{1,0:T(1,128)S(1)}, u32[]{:S(2)}, u32[]{:S(2)}) collective-permute-start(f32[1,128]{1,0:T(1,128)S(1)} %bitcast.21), channel_id=1, source_target_pairs={{0,1},{1,0},{2,3},{3,2},{4,5},{5,4},{6,7},{7,6},{8,9},{9,8},{10,11... | collective-permute-start | bytes 1544 | tf_op jit(solution)/shard_map/ppermute | solution.py:188
  206.1 4.5 %collective-permute-start.9 = (f32[1,128]{1,0:T(1,128)S(1)}, f32[1,128]{1,0:T(1,128)S(1)}, u32[]{:S(2)}, u32[]{:S(2)}) collective-permute-start(f32[1,128]{1,0:T(1,128)S(1)} %bitcast_add_fusion.1), channel_id=1, source_target_pairs={{0,2},{1,3},{2,0},{3,1},{4,6},{5,7},{6,4},{7,5},{8,10},{9,11},{10,... | collective-permute-start | bytes 1544 | tf_op jit(solution)/shard_map/ppermute | solution.py:188
  301.5 28.2 %copy-start = (f32[8,128]{1,0:T(8,128)S(1)}, f32[8,128]{1,0:T(8,128)}, u32[]{:S(2)}) copy-start(f32[8,128]{1,0:T(8,128)} %get-tuple-element.19.vals_ref) | copy-start | bytes 12292
  320.3 1.4 collective-permute-start.10
  322.4 3.7 %collective-permute-start.11 = (f32[24,128]{1,0:T(8,128)S(1)}, f32[24,128]{1,0:T(8,128)S(1)}, u32[]{:S(2)}, u32[]{:S(2)}) collective-permute-start(f32[24,128]{1,0:T(8,128)S(1)} %add.97), channel_id=1, source_target_pairs={{0,8},{4,12},{8,0},{12,4},{16,24},{20,28},{24,16},{28,20},{1,9},{5... | collective-permute-start | bytes 36872 | tf_op jit(solution)/shard_map/ppermute | solution.py:188
  326.1 3.7 %collective-permute-start.12 = (f32[24,128]{1,0:T(8,128)S(1)}, f32[24,128]{1,0:T(8,128)S(1)}, u32[]{:S(2)}, u32[]{:S(2)}) collective-permute-start(f32[24,128]{1,0:T(8,128)S(1)} %add.98), channel_id=1, source_target_pairs={{0,16},{4,20},{8,24},{12,28},{16,0},{20,4},{24,8},{28,12},{1,17},{... | collective-permute-start | bytes 36872 | tf_op jit(solution)/shard_map/ppermute | solution.py:188
  329.8 3.6 %collective-permute-start.13 = (f32[1,128]{1,0:T(1,128)S(1)}, f32[1,128]{1,0:T(1,128)S(1)}, u32[]{:S(2)}, u32[]{:S(2)}) collective-permute-start(f32[1,128]{1,0:T(1,128)S(1)} %bitcast.20), channel_id=1, source_target_pairs={{0,1},{1,0},{2,3},{3,2},{4,5},{5,4},{6,7},{7,6},{8,9},{9,8},{10,11... | collective-permute-start | bytes 1544 | tf_op jit(solution)/shard_map/ppermute | solution.py:188
  333.4 4.4 %collective-permute-start.14 = (f32[1,128]{1,0:T(1,128)S(1)}, f32[1,128]{1,0:T(1,128)S(1)}, u32[]{:S(2)}, u32[]{:S(2)}) collective-permute-start(f32[1,128]{1,0:T(1,128)S(1)} %bitcast_add_fusion), channel_id=1, source_target_pairs={{0,2},{1,3},{2,0},{3,1},{4,6},{5,7},{6,4},{7,5},{8,10},{9,11},{10,... | collective-permute-start | bytes 1544 | tf_op jit(solution)/shard_map/ppermute | solution.py:188
Sparse Core Ops, SparseCore 0:
  53.1 101.6 all-reduce.2
  202.6 98.8 all-reduce.4

commit v2 on v0

v2 whole, which is shorter than its diff:
```python
import functools

import jax
import jax.numpy as jnp
from jax import lax
from jax.experimental import pallas as pl
from jax.experimental.pallas import tpu as pltpu
from jax.sharding import PartitionSpec as P

DAMPING = 0.001
LANES = 128
SUBLANES = 8
CHUNKS = 8
COPIES = 8
CHUNK_VMEM = 8 * 2**20
EXTRA = 8


def whole_tiles(rows, parts):
    return max(n for n in range(1, parts + 1) if rows % (n * SUBLANES) == 0)


def unroll_of(groups):
    return max(u for u in (1, 2, 4) if groups % u == 0)


def lane_total(tile):
    return jnp.broadcast_to(jnp.sum(tile, axis=1, keepdims=True), tile.shape)


def all_total(tile):
    return lane_total(jnp.broadcast_to(jnp.sum(tile, axis=0, keepdims=True), tile.shape))


def tile_sum(block):
    return jnp.sum(block.reshape(-1, SUBLANES, LANES), axis=0)


def eight_tiles(derivs, row):
    width = SUBLANES * LANES
    block = derivs[:, pl.ds(pl.multiple_of(row * LANES, width), width)]
    return [block[:, s * LANES : (s + 1) * LANES] for s in range(SUBLANES)]


def products(derivs, vec, first, rows, offset=0):
    unroll = unroll_of(rows // SUBLANES)

    def step(i, accs):
        accs = list(accs)
        for u in range(unroll):
            row = first + (i * unroll + u) * SUBLANES
            vals = vec[pl.ds(pl.multiple_of(row, SUBLANES), SUBLANES), :]
            tiles = eight_tiles(derivs, offset + row)
            for s in range(SUBLANES):
                accs[s] = accs[s] + tiles[s] * jnp.broadcast_to(vals[s : s + 1, :], (SUBLANES, LANES))
        return tuple(accs)

    zero = jnp.zeros((SUBLANES, LANES), jnp.float32)
    a = lax.fori_loop(0, rows // SUBLANES // unroll, step, (zero,) * SUBLANES)
    return ((a[0] + a[1]) + (a[2] + a[3])) + ((a[4] + a[5]) + (a[6] + a[7]))


def sublane_sums(tiles):
    index = lax.broadcasted_iota(jnp.int32, (SUBLANES, LANES), 0)
    half = SUBLANES // 2
    while half >= 1:
        low = (index & half) == 0
        merged = []
        for s in range(half):
            a, b = tiles[s], tiles[s + half]
            keep, move = jnp.where(low, a, b), jnp.where(low, b, a)
            if half == SUBLANES // 2:
                moved = pltpu.roll(move, half, 0)
            else:
                moved = jnp.where(low, pltpu.roll(move, SUBLANES - half, 0), pltpu.roll(move, half, 0))
            merged.append(keep + moved)
        tiles = merged
        half //= 2
    return tiles[0]


def vmem():
    return pl.BlockSpec(memory_space=pltpu.VMEM)


def hbm():
    return pl.BlockSpec(memory_space=pltpu.HBM)


def start_kernel(copies, derivs_hbm, grad_hbm, stats, derivs, sems, grad, grad_sems):
    rows = grad.shape[0] // copies
    waits = []
    grad_copies = []
    for c in range(copies):
        part = pl.ds(c * rows, rows)
        grad_copies.append(pltpu.make_async_copy(grad_hbm.at[part, :], grad.at[part, :], grad_sems.at[c]))
        grad_copies[-1].start()
        cols = pl.ds(c * rows * LANES, rows * LANES)
        waits.append(pltpu.make_async_copy(derivs_hbm.at[:, cols], derivs.at[:, cols], sems.at[c]))
        waits[-1].start()
    total = jnp.zeros((SUBLANES, LANES), jnp.float32)
    squares = total
    for c in range(copies):
        grad_copies[c].wait()
        waits[c].wait()
        total = total + products(derivs, grad, c * rows, rows)
        part = grad[c * rows : (c + 1) * rows, :]
        squares = squares + tile_sum(part * part)
    stats[0:8, :] = lane_total(total)
    stats[8:16, :] = all_total(squares)
    stats[16:24, :] = jnp.zeros((SUBLANES, LANES), jnp.float32)


def start_call(derivs, grad):
    rows = grad.shape[0]
    copies = whole_tiles(rows, COPIES)
    return pl.pallas_call(
        functools.partial(start_kernel, copies),
        in_specs=[hbm(), hbm()],
        out_specs=[vmem(), vmem()],
        out_shape=[jax.ShapeDtypeStruct((24, LANES), jnp.float32), pltpu.VMEM(derivs.shape, jnp.float32)],
        scratch_shapes=[
            pltpu.SemaphoreType.DMA((copies,)),
            pltpu.VMEM((rows, LANES), jnp.float32),
            pltpu.SemaphoreType.DMA((copies,)),
        ],
        compiler_params=pltpu.CompilerParams(vmem_limit_bytes=CHUNK_VMEM),
        cost_estimate=pl.CostEstimate(flops=16 * rows * LANES, bytes_accessed=36 * rows * LANES, transcendentals=0),
        name="start_products",
    )(pltpu.with_memory_space_constraint(derivs, pltpu.HBM), pltpu.with_memory_space_constraint(grad, pltpu.HBM))


def back_kernel(offset, derivs, vals_ref, out):
    vals = vals_ref[...]
    rows = out.shape[0] - EXTRA
    out[rows : rows + EXTRA, :] = jnp.broadcast_to(jnp.sum(vals * vals, axis=0, keepdims=True), (EXTRA, LANES))
    unroll = unroll_of(rows // SUBLANES)

    def step(i, carry):
        for u in range(unroll):
            row = (i * unroll + u) * SUBLANES
            tiles = [tile * vals for tile in eight_tiles(derivs, offset + row)]
            out[pl.ds(pl.multiple_of(row, SUBLANES), SUBLANES), :] = sublane_sums(tiles)
        return carry

    lax.fori_loop(0, rows // SUBLANES // unroll, step, 0)


def back_call(derivs, vals, chunk, rows):
    return pl.pallas_call(
        functools.partial(back_kernel, chunk * rows),
        in_specs=[vmem(), vmem()],
        out_specs=vmem(),
        out_shape=jax.ShapeDtypeStruct((rows + EXTRA, LANES), jnp.float32),
        compiler_params=pltpu.CompilerParams(vmem_limit_bytes=CHUNK_VMEM),
        cost_estimate=pl.CostEstimate(flops=16 * rows * LANES, bytes_accessed=36 * rows * LANES, transcendentals=0),
        name="back_products",
    )(pltpu.with_memory_space_constraint(derivs, pltpu.VMEM), vals)


def step_length(norm, squares, rows_all, dir_sq):
    return norm / (squares / rows_all + DAMPING * dir_sq)


def advance_kernel(offset, rows_all, last, derivs, back, squares, known, res, prev, stats_in, new, stats):
    rows = new.shape[0]
    norm, dir_sq, beta = known[0:1, :], known[1:2, :], known[2:3, :]
    step_len = step_length(norm, squares[0:1, :], rows_all, dir_sq)
    old = res[...]
    direction = old + beta * prev[...]
    fresh = old - step_len * (back[0:rows, :] * (1.0 / rows_all) + DAMPING * direction)
    new[...] = fresh
    norms = stats_in[8:16, :] + tile_sum(fresh * fresh)
    cross = stats_in[16:24, :] + tile_sum(fresh * direction)
    total = stats_in[0:8, :] + products(derivs, new, 0, rows, offset)
    if last:
        total, norms, cross = lane_total(total), all_total(norms), all_total(cross)
    stats[0:8, :] = total
    stats[8:16, :] = norms
    stats[16:24, :] = cross


def advance_call(derivs, back, first_back, known, residual, prev, stats, chunk, rows, rows_all, last):
    here = pl.BlockSpec((rows, LANES), lambda i: (0, 0))
    part = pl.BlockSpec((rows, LANES), lambda i: (chunk, 0))
    rest = pl.BlockSpec((EXTRA, LANES), lambda i: (rows // EXTRA, 0))
    tile = pl.BlockSpec((SUBLANES, LANES), lambda i: (0, 0))
    sums = pl.BlockSpec((24, LANES), lambda i: (0, 0))
    return pl.pallas_call(
        functools.partial(advance_kernel, chunk * rows, rows_all, last),
        grid=(1,),
        in_specs=[vmem(), here, rest, tile, here if residual.shape[0] == rows else part, part, sums],
        out_specs=[here, sums],
        out_shape=[
            jax.ShapeDtypeStruct((rows, LANES), jnp.float32),
            jax.ShapeDtypeStruct((24, LANES), jnp.float32),
        ],
        compiler_params=pltpu.CompilerParams(vmem_limit_bytes=CHUNK_VMEM),
        cost_estimate=pl.CostEstimate(flops=24 * rows * LANES, bytes_accessed=48 * rows * LANES, transcendentals=0),
        name="advance_residual",
    )(pltpu.with_memory_space_constraint(derivs, pltpu.VMEM), back, first_back, known, residual, prev, stats)


def last_kernel(share_ref, grad_ref, res1_ref, res2_ref, coef_ref, out_ref):
    c0, c1, c2 = coef_ref[0:1, :], coef_ref[1:2, :], coef_ref[2:3, :]
    out_ref[...] = c0 * grad_ref[...] + c1 * res1_ref[...] + c2 * res2_ref[...]


def last_call(share, grad, res1, res2, coefs, share_rows):
    vec = pl.BlockSpec((share_rows, LANES), lambda i, share_ref: (share_ref[0], 0))
    return pl.pallas_call(
        last_kernel,
        grid_spec=pltpu.PrefetchScalarGridSpec(
            num_scalar_prefetch=1,
            grid=(1,),
            in_specs=[vec, vec, vec, pl.BlockSpec((SUBLANES, LANES), lambda i, share_ref: (0, 0))],
            out_specs=pl.BlockSpec((share_rows, LANES), lambda i, share_ref: (0, 0)),
        ),
        out_shape=jax.ShapeDtypeStruct((share_rows, LANES), jnp.float32),
        name="last_combination",
    )(share, grad, res1, res2, coefs)


def small_sum(value, axis):
    size = lax.axis_size(axis)
    if size & (size - 1):
        return lax.psum(value, axis)
    bit = 1
    while bit < size:
        value = value + lax.ppermute(value, axis, [(i, i ^ bit) for i in range(size)])
        bit *= 2
    return value


def chain(chunks, produce, consume, state, gate):
    count = lax.axis_size("walker")
    me = lax.axis_index("walker")
    gaps = (1, 2)
    up, down = [0], [0]
    for link in range(count - 2):
        up.append(up[-1] + gaps[link % 2])
    for link in range(count - 2, 0, -1):
        down.insert(0, down[0] + gaps[link % 2])

    def links(parity):
        partner, send, recv = {}, {}, {}
        for w in range(count):
            other = w + 1 if w % 2 == parity else w - 1
            if 0 <= other < count:
                link = min(w, other)
                partner[w] = other
                send[w], recv[w] = (up[link], down[link]) if other > w else (down[link], up[link])
        return partner, send, recv

    def pick(items, at, delays):
        found = None
        for delay in sorted(set(delays.values())):
            if not 0 <= at - delay < len(items) or items[at - delay] is None:
                continue
            if found is None:
                found = items[at - delay]
            else:
                mine = functools.reduce(jnp.logical_or, [me == w for w in delays if delays[w] == delay])
                found = jnp.where(mine, items[at - delay], found)
        return found

    both = (links(0), links(1))
    made = [produce(0, gate)]
    got = ([], [])

    def complete(chunk):
        total = made[chunk]
        for parity, (_, _, recv) in enumerate(both):
            arrived = pick(got[parity], chunk, {w: -delay for w, delay in recv.items()})
            if arrived is not None:
                total = total + arrived
        return total

    def exchange(parity, step, before, gate, state):
        partner, send, _ = both[parity]
        pairs = [(w, partner[w]) for w in partner if 0 <= step - send[w] < chunks]
        own = pick(made, step, send) if pairs else None
        if own is None:
            got[parity].append(None)
            return gate, state
        if 0 <= before < step and got[1 - parity][before] is not None:
            own = own + got[1 - parity][before]
        own, gate, *state = lax.optimization_barrier((own, gate, *state))
        got[parity].append(lax.ppermute(own, "walker", pairs))
        return gate, tuple(state)

    late = [max(recv.values(), default=-1) for _, _, recv in both]
    lag = 1 + max(late[0], late[1] + 1)
    steps = chunks + max(late)
    for step in range(steps):
        gate, state = exchange(0, step, step - gaps[1], gate, state)
        if step + 1 < chunks:
            made.append(produce(step + 1, gate))
            made[-1], gate, *state = lax.optimization_barrier((made[-1], gate, *state))
            state = tuple(state)
        gate, state = exchange(1, step, step - gaps[0], gate, state)
        if step - lag >= 0:
            state = consume(step - lag, complete(step - lag), state)
    for chunk in range(max(steps - lag, 0), chunks):
        state = consume(chunk, complete(chunk), state)
    return state


def body(derivs, gradient):
    walkers = lax.axis_size("walker")
    rows_all = derivs.shape[0] * walkers
    rows = gradient.shape[0] // LANES
    grad = gradient.reshape(rows, LANES)
    chunks = whole_tiles(rows, CHUNKS)
    part = rows // chunks

    def advance(residual, prev, vals, norm, dir_sq, beta):
        known = jnp.concatenate([norm, dir_sq, beta, jnp.zeros((5, LANES), jnp.float32)])
        first = []
        fresh = []

        def consume(chunk, total, state):
            if not first:
                first.append(total)
            last = chunk == chunks - 1
            old = residual[chunk] if isinstance(residual, list) else residual
            new, stats = advance_call(
                derivs, total, first[0], known, old, prev, state[0], chunk, part, rows_all, last
            )
            fresh.append(new)
            return (stats,)

        def produce(chunk, gate):
            return back_call(derivs, gate, chunk, part)

        state = (jnp.zeros((24, LANES), jnp.float32),)
        (stats,) = chain(chunks, produce, consume, state, vals)
        step = step_length(norm, first[0][part : part + 1], rows_all, dir_sq)
        return fresh, step, small_sum(stats, "param")

    stats, derivs = start_call(derivs, grad)
    stats = small_sum(stats, "param")
    vals0, norm0 = stats[0:8], stats[8:9]
    dir_sq0 = norm0
    res1, step0, stats = advance(grad, grad, vals0, norm0, dir_sq0, jnp.zeros_like(norm0))

    norm1, cross1 = stats[8:9], stats[16:17]
    beta1 = norm1 / norm0
    vals1 = stats[0:8] + beta1 * vals0
    dir_sq1 = norm1 + 2.0 * beta1 * cross1 + beta1 * beta1 * dir_sq0
    res2, step1, stats = advance(res1, grad, vals1, norm1, dir_sq1, beta1)

    norm2, cross2 = stats[8:9], stats[16:17]
    beta2 = norm2 / norm1
    vals2 = stats[0:8] + beta2 * vals1
    dir_sq2 = norm2 + 2.0 * beta2 * cross2 + beta2 * beta2 * dir_sq1
    squares = small_sum(jnp.sum(vals2 * vals2, axis=0, keepdims=True), "walker")
    step2 = step_length(norm2, squares, rows_all, dir_sq2)

    along1 = step1 + step2 * beta2
    coefs = jnp.concatenate([step0 + along1 * beta1, along1, step2, jnp.zeros((5, LANES), jnp.float32)])
    share = lax.axis_index("walker").astype(jnp.int32).reshape(1)
    out = last_call(share, grad, jnp.concatenate(res1), jnp.concatenate(res2), coefs, rows // walkers)
    return out.reshape(-1)


def solution(mesh):
    in_specs = (P("walker", "param"), P("param"))
    out_specs = P(("param", "walker"))
    return jax.shard_map(body, mesh=mesh, in_specs=in_specs, out_specs=out_specs, check_vma=False)
```

time: 807 us -> 232 us (0.29); the launches traced: 798 us -> 231 us
  blocking collectives: 249 us -> 0 us
  matrix products: 203 us -> 0 us
  waiting for transfers between devices: 296 us -> 93.8 us
  starting transfers between devices: 0.09 us -> 97.5 us
  Pallas kernels: 0 us -> 27.2 us
  other arithmetic: 22.8 us -> 3.67 us
  between operations: 19.8 us -> 0.93 us
    psum x3 -> x0, waiting for transfers between devices: 296 us -> none  [body(): lax.psum(jnp.dot(row_vals, derivs, precision=lax.Precision.HIGHEST), 'wal...]
    psum x8 -> x0, blocking collectives: 249 us -> none  [the longest x3 129 us: squares(): return lax.psum(jnp.sum(vector * vector), ('param', 'walker'))]
    dot_general x6 -> x0, matrix products: 203 us -> none  [the longest x3 136 us: body(): row_part = jnp.dot(derivs, direction, precision=lax.Precision.HIGHEST)]
    ppermute x0 -> x49, starting transfers between devices: none -> 97.5 us  [the longest x38 85.2 us: exchange(): got[parity].append(lax.ppermute(own, 'walker', pairs))]
    ppermute x0 -> x49, waiting for transfers between devices: none -> 93.8 us  [the longest x38 71.5 us: exchange(): got[parity].append(lax.ppermute(own, 'walker', pairs))]
    pallas_call x0 -> x34, Pallas kernels: none -> 27.2 us  [the longest x16 9.58 us: back_call(): pl.pallas_call(functools.partial(back_kernel, chunk * rows), in_specs=[vm...]
    add x5 -> x50, other arithmetic: 11.6 us -> 2.83 us  [the longest x32 2.19 us: exchange(): own = own + got[1 - parity][before]]
  transfers between devices with their start and end apart: 3 -> 49, of which waited for: 3 -> 28; matrix products, arithmetic and copies ran while one was open for 0% -> 1% of each run, Pallas kernels for 0% -> 6%
where the time goes in v2:
time: 232 us; the launch traced here: 231 us
  starting transfers between devices  97.5 us (42%)
  waiting for transfers between devices  93.8 us (40%)
  Pallas kernels  27.2 us (12%)
  local copies, waits for them, and re-layouts  8.21 us (4%)
  other arithmetic  3.67 us (2%)
    ppermute x38, starting transfers between devices, exchange(): got[parity].append(lax.ppermute(own, 'walker', pairs))  85.2 us
    ppermute x38, waiting for transfers between devices, exchange(): got[parity].append(lax.ppermute(own, 'walker', pairs))  71.5 us
    ppermute x11, waiting for transfers between devices, small_sum(): lax.ppermute(value, axis, [(i, i ^ bit) for i in range(size)])  22.3 us
    ppermute x11, starting transfers between devices, small_sum(): lax.ppermute(value, axis, [(i, i ^ bit) for i in range(size)])  12.3 us
    pallas_call x16, Pallas kernels, back_call(): pl.pallas_call(functools.partial(back_kernel, chunk * rows), in_specs=[vm...  9.58 us
    pallas_call x1, Pallas kernels, start_call(): pl.pallas_call(functools.partial(start_kernel, copies), in_specs=[hbm(),...  8.09 us
    unnamed x42, local copies, waits for them, and re-layouts  8 us
    pallas_call x16, Pallas kernels, advance_call(): pl.pallas_call(functools.partial(advance_kernel, chunk * rows, rows_all,...  7.14 us
  transfers between devices with their start and end apart: 49, of which 28 were waited for; matrix products, arithmetic and copies ran while one was open for 1% of the time, Pallas kernels for 6%

profile of v2, /device:TPU:0, one launch (start us, length us, event | category | flops | bytes accessed | tf_op | source)
XLA Modules:
  0.0 231.3 jit_solution(16973194649758242783)
XLA Ops:
  0.0 8.1 %start_products.1 = (f32[24,128]{1,0:T(8,128)S(1)}, f32[8,622592]{1,0:T(8,128)S(1)}) custom-call(f32[8,622592]{1,0:T(8,128)} %derivs_hbm.1, f32[4864,128]{1,0:T(8,128)} %bitcast.8), custom_call_target="tpu_custom_call" | custom-call | flops 9961472 | bytes 22413312 | tf_op jit(solution)/shard_map/start_products/pallas_call | solution.py:117
  9.5 2.8 %collective-permute-start.1 = (f32[24,128]{1,0:T(8,128)S(1)}, f32[24,128]{1,0:T(8,128)S(1)}, u32[]{:S(2)}, u32[]{:S(2)}) collective-permute-start(f32[24,128]{1,0:T(8,128)S(1)} %add.258), channel_id=1, source_target_pairs={{0,8},{4,12},{8,0},{12,4},{16,24},{20,28},{24,16},{28,20},{1,9},{5... | collective-permute-start | bytes 36872 | tf_op jit(solution)/shard_map/ppermute | solution.py:230
  12.3 1.7 collective-permute-done.1
  14.0 2.1 collective-permute-start.2
  16.0 1.7 collective-permute-done.2
  18.3 4.0 %collective-permute-start.3 = (f32[616,128]{1,0:T(8,128)S(1)}, f32[616,128]{1,0:T(8,128)S(1)}, u32[]{:S(2)}, u32[]{:S(2)}) collective-permute-start(f32[616,128]{1,0:T(8,128)S(1)} %back_products.16), channel_id=1, source_target_pairs={{0,1},{3,2},{4,5},{7,6},{8,9},{11,10},{12,13},{15,14},{16,17},{19,... | collective-permute-start | bytes 946184 | tf_op jit(solution)/shard_map/ppermute | solution.py:289
  23.6 1.3 collective-permute-start.5
  24.9 5.3 %collective-permute-done.3 = f32[616,128]{1,0:T(8,128)S(1)} collective-permute-done((f32[616,128]{1,0:T(8,128)S(1)}, f32[616,128]{1,0:T(8,128)S(1)}, u32[]{:S(2)}, u32[]{:S(2)}) %collective-permute-start.3) | collective-permute-done | bytes 315424 | tf_op jit(solution)/shard_map/ppermute | solution.py:289
  31.1 6.7 %copy-done.1 = f32[8,622592]{1,0:T(8,128)S(1)} copy-done((f32[8,622592]{1,0:T(8,128)S(1)}, f32[8,622592]{1,0:T(8,128)}, u32[]{:S(2)}) %copy-start.1) | copy-done | bytes 19922968
  39.3 9.4 %collective-permute-start.8 = (f32[616,128]{1,0:T(8,128)S(1)}, f32[616,128]{1,0:T(8,128)S(1)}, u32[]{:S(2)}, u32[]{:S(2)}) collective-permute-start(f32[616,128]{1,0:T(8,128)S(1)} %back_products.18), channel_id=1, source_target_pairs={{0,1},{3,2},{4,5},{7,6},{8,9},{11,10},{12,13},{15,14},{16,17},{19,... | collective-permute-start | bytes 946184 | tf_op jit(solution)/shard_map/ppermute | solution.py:289
  49.6 4.8 %collective-permute-done.8 = f32[616,128]{1,0:T(8,128)S(1)} collective-permute-done((f32[616,128]{1,0:T(8,128)S(1)}, f32[616,128]{1,0:T(8,128)S(1)}, u32[]{:S(2)}, u32[]{:S(2)}) %collective-permute-start.8) | collective-permute-done | bytes 315424 | tf_op jit(solution)/shard_map/ppermute | solution.py:289
  55.8 6.6 %collective-permute-start.9 = (f32[616,128]{1,0:T(8,128)S(1)}, f32[616,128]{1,0:T(8,128)S(1)}, u32[]{:S(2)}, u32[]{:S(2)}) collective-permute-start(f32[616,128]{1,0:T(8,128)S(1)} %select_add_fusion.8), channel_id=1, source_target_pairs={{0,1},{1,0},{2,3},{3,2},{4,5},{5,4},{6,7},{7,6},{8,9},{9,8},{10,11... | collective-permute-start | bytes 946184 | tf_op jit(solution)/shard_map/ppermute | solution.py:289
  63.8 5.3 %collective-permute-start.11 = (f32[616,128]{1,0:T(8,128)S(1)}, f32[616,128]{1,0:T(8,128)S(1)}, u32[]{:S(2)}, u32[]{:S(2)}) collective-permute-start(f32[616,128]{1,0:T(8,128)S(1)} %select_add_fusion.7), channel_id=1, source_target_pairs={{0,1},{1,0},{2,3},{3,2},{4,5},{5,4},{6,7},{7,6},{8,9},{9,8},{10,11... | collective-permute-start | bytes 946184 | tf_op jit(solution)/shard_map/ppermute | solution.py:289
  71.2 4.6 %collective-permute-start.13 = (f32[616,128]{1,0:T(8,128)S(1)}, f32[616,128]{1,0:T(8,128)S(1)}, u32[]{:S(2)}, u32[]{:S(2)}) collective-permute-start(f32[616,128]{1,0:T(8,128)S(1)} %select_add_fusion.6), channel_id=1, source_target_pairs={{0,1},{1,0},{2,3},{3,2},{4,5},{5,4},{6,7},{7,6},{8,9},{9,8},{10,11... | collective-permute-start | bytes 946184 | tf_op jit(solution)/shard_map/ppermute | solution.py:289
  75.8 1.4 collective-permute-done.11
  78.4 6.4 %collective-permute-start.15 = (f32[616,128]{1,0:T(8,128)S(1)}, f32[616,128]{1,0:T(8,128)S(1)}, u32[]{:S(2)}, u32[]{:S(2)}) collective-permute-start(f32[616,128]{1,0:T(8,128)S(1)} %select_add_fusion.5), channel_id=1, source_target_pairs={{0,1},{1,0},{2,3},{3,2},{4,5},{5,4},{6,7},{7,6},{8,9},{9,8},{10,11... | collective-permute-start | bytes 946184 | tf_op jit(solution)/shard_map/ppermute | solution.py:289
  86.7 6.3 %collective-permute-done.15 = f32[616,128]{1,0:T(8,128)S(1)} collective-permute-done((f32[616,128]{1,0:T(8,128)S(1)}, f32[616,128]{1,0:T(8,128)S(1)}, u32[]{:S(2)}, u32[]{:S(2)}) %collective-permute-start.15) | collective-permute-done | bytes 315424 | tf_op jit(solution)/shard_map/ppermute | solution.py:289
  97.0 6.5 %collective-permute-done.17 = f32[616,128]{1,0:T(8,128)S(1)} collective-permute-done((f32[616,128]{1,0:T(8,128)S(1)}, f32[616,128]{1,0:T(8,128)S(1)}, u32[]{:S(2)}, u32[]{:S(2)}) %collective-permute-start.17) | collective-permute-done | bytes 315424 | tf_op jit(solution)/shard_map/ppermute | solution.py:289
  105.4 1.5 collective-permute-done.19
  107.5 5.4 %collective-permute-done.21 = f32[616,128]{1,0:T(8,128)S(1)} collective-permute-done((f32[616,128]{1,0:T(8,128)S(1)}, f32[616,128]{1,0:T(8,128)S(1)}, u32[]{:S(2)}, u32[]{:S(2)}) %collective-permute-start.21) | collective-permute-done | bytes 315424 | tf_op jit(solution)/shard_map/ppermute | solution.py:289
  114.7 1.5 collective-permute-start.23
  116.2 2.2 collective-permute-done.23
  118.4 1.5 collective-permute-start.24
  119.9 2.2 collective-permute-done.24
  122.7 1.5 collective-permute-start.25
  125.5 1.3 collective-permute-start.27
  126.8 5.2 %collective-permute-done.25 = f32[616,128]{1,0:T(8,128)S(1)} collective-permute-done((f32[616,128]{1,0:T(8,128)S(1)}, f32[616,128]{1,0:T(8,128)S(1)}, u32[]{:S(2)}, u32[]{:S(2)}) %collective-permute-start.25) | collective-permute-done | bytes 315424 | tf_op jit(solution)/shard_map/ppermute | solution.py:289
  133.5 2.3 collective-permute-done.27
  136.5 6.6 %collective-permute-start.30 = (f32[616,128]{1,0:T(8,128)S(1)}, f32[616,128]{1,0:T(8,128)S(1)}, u32[]{:S(2)}, u32[]{:S(2)}) collective-permute-start(f32[616,128]{1,0:T(8,128)S(1)} %back_products.26), channel_id=1, source_target_pairs={{0,1},{3,2},{4,5},{7,6},{8,9},{11,10},{12,13},{15,14},{16,17},{19,... | collective-permute-start | bytes 946184 | tf_op jit(solution)/shard_map/ppermute | solution.py:289
  143.2 3.5 %collective-permute-start.28 = (f32[616,128]{1,0:T(8,128)S(1)}, f32[616,128]{1,0:T(8,128)S(1)}, u32[]{:S(2)}, u32[]{:S(2)}) collective-permute-start(f32[616,128]{1,0:T(8,128)S(1)} %select_add_fusion.4), channel_id=1, source_target_pairs={{0,1},{1,0},{2,3},{3,2},{4,5},{5,4},{6,7},{7,6},{8,9},{9,8},{10,11... | collective-permute-start | bytes 946184 | tf_op jit(solution)/shard_map/ppermute | solution.py:289
  147.4 2.0 collective-permute-done.30
  150.8 6.4 %collective-permute-start.31 = (f32[616,128]{1,0:T(8,128)S(1)}, f32[616,128]{1,0:T(8,128)S(1)}, u32[]{:S(2)}, u32[]{:S(2)}) collective-permute-start(f32[616,128]{1,0:T(8,128)S(1)} %select_add_fusion.3), channel_id=1, source_target_pairs={{0,1},{1,0},{2,3},{3,2},{4,5},{5,4},{6,7},{7,6},{8,9},{9,8},{10,11... | collective-permute-start | bytes 946184 | tf_op jit(solution)/shard_map/ppermute | solution.py:289
  158.5 5.4 %collective-permute-start.33 = (f32[616,128]{1,0:T(8,128)S(1)}, f32[616,128]{1,0:T(8,128)S(1)}, u32[]{:S(2)}, u32[]{:S(2)}) collective-permute-start(f32[616,128]{1,0:T(8,128)S(1)} %select_add_fusion.2), channel_id=1, source_target_pairs={{0,1},{1,0},{2,3},{3,2},{4,5},{5,4},{6,7},{7,6},{8,9},{9,8},{10,11... | collective-permute-start | bytes 946184 | tf_op jit(solution)/shard_map/ppermute | solution.py:289
  166.4 4.8 %collective-permute-done.33 = f32[616,128]{1,0:T(8,128)S(1)} collective-permute-done((f32[616,128]{1,0:T(8,128)S(1)}, f32[616,128]{1,0:T(8,128)S(1)}, u32[]{:S(2)}, u32[]{:S(2)}) %collective-permute-start.33) | collective-permute-done | bytes 315424 | tf_op jit(solution)/shard_map/ppermute | solution.py:289
  171.4 1.8 collective-permute-start.35
  173.7 2.4 %collective-permute-start.37 = (f32[616,128]{1,0:T(8,128)S(1)}, f32[616,128]{1,0:T(8,128)S(1)}, u32[]{:S(2)}, u32[]{:S(2)}) collective-permute-start(f32[616,128]{1,0:T(8,128)S(1)} %select_add_fusion), channel_id=1, source_target_pairs={{0,1},{1,0},{2,3},{3,2},{4,5},{5,4},{6,7},{7,6},{8,9},{9,8},{10,11... | collective-permute-start | bytes 946184 | tf_op jit(solution)/shard_map/ppermute | solution.py:289
  176.7 1.6 collective-permute-done.35
  181.0 1.3 collective-permute-done.37
  184.6 7.9 %collective-permute-done.39 = f32[616,128]{1,0:T(8,128)S(1)} collective-permute-done((f32[616,128]{1,0:T(8,128)S(1)}, f32[616,128]{1,0:T(8,128)S(1)}, u32[]{:S(2)}, u32[]{:S(2)}) %collective-permute-start.39) | collective-permute-done | bytes 315424 | tf_op jit(solution)/shard_map/ppermute | solution.py:289
  195.8 11.3 %collective-permute-done.43 = f32[616,128]{1,0:T(8,128)S(1)} collective-permute-done((f32[616,128]{1,0:T(8,128)S(1)}, f32[616,128]{1,0:T(8,128)S(1)}, u32[]{:S(2)}, u32[]{:S(2)}) %collective-permute-start.43) | collective-permute-done | bytes 315424 | tf_op jit(solution)/shard_map/ppermute | solution.py:289
  207.1 3.4 %collective-permute-done.41 = f32[616,128]{1,0:T(8,128)S(1)} collective-permute-done((f32[616,128]{1,0:T(8,128)S(1)}, f32[616,128]{1,0:T(8,128)S(1)}, u32[]{:S(2)}, u32[]{:S(2)}) %collective-permute-start.41) | collective-permute-done | bytes 315424 | tf_op jit(solution)/shard_map/ppermute | solution.py:289
  212.8 1.5 collective-permute-start.45
  214.3 2.2 collective-permute-done.45
  216.5 1.5 collective-permute-start.46
  218.0 2.2 collective-permute-done.46
  220.3 3.5 %collective-permute-done.47 = f32[1,128]{1,0:T(1,128)S(1)} collective-permute-done((f32[1,128]{1,0:T(1,128)S(1)}, f32[1,128]{1,0:T(1,128)S(1)}, u32[]{:S(2)}, u32[]{:S(2)}) %collective-permute-start.47) | collective-permute-done | bytes 544 | tf_op jit(solution)/shard_map/ppermute | solution.py:230
  224.7 3.6 %collective-permute-done.48 = f32[1,128]{1,0:T(1,128)S(1)} collective-permute-done((f32[1,128]{1,0:T(1,128)S(1)}, f32[1,128]{1,0:T(1,128)S(1)}, u32[]{:S(2)}, u32[]{:S(2)}) %collective-permute-start.48) | collective-permute-done | bytes 544 | tf_op jit(solution)/shard_map/ppermute | solution.py:230
  229.0 2.4 %last_combination.1 = f32[1216,128]{1,0:T(8,128)} custom-call(s32[1]{0:T(128)} %bitcast.share_ref, f32[4864,128]{1,0:T(8,128)} %bitcast.9, f32[4864,128]{1,0:T(8,128)} %copy-done.5, f32[4864,128]{1,0:T(8,128)} %copy-done.4, f32[8,128]{1,0:T(8,128)} %maximum_maximum_fusion.2.coef_ref), custom_call_target="tpu_custom_call" | custom-call | tf_op jit(solution)/shard_map/last_combination/pallas_call | solution.py:211
  (190 shorter events, 45.5 us)
Async XLA Ops:
  8.1 1.4 collective-permute-start
  9.5 4.5 %collective-permute-start.1 = (f32[24,128]{1,0:T(8,128)S(1)}, f32[24,128]{1,0:T(8,128)S(1)}, u32[]{:S(2)}, u32[]{:S(2)}) collective-permute-start(f32[24,128]{1,0:T(8,128)S(1)} %add.258), channel_id=1, source_target_pairs={{0,8},{4,12},{8,0},{12,4},{16,24},{20,28},{24,16},{28,20},{1,9},{5... | collective-permute-start | bytes 36872 | tf_op jit(solution)/shard_map/ppermute | solution.py:230
  14.0 3.7 %collective-permute-start.2 = (f32[24,128]{1,0:T(8,128)S(1)}, f32[24,128]{1,0:T(8,128)S(1)}, u32[]{:S(2)}, u32[]{:S(2)}) collective-permute-start(f32[24,128]{1,0:T(8,128)S(1)} %add.259), channel_id=1, source_target_pairs={{0,16},{4,20},{8,24},{12,28},{16,0},{20,4},{24,8},{28,12},{1,17},{... | collective-permute-start | bytes 36872 | tf_op jit(solution)/shard_map/ppermute | solution.py:230
  18.3 11.9 %collective-permute-start.3 = (f32[616,128]{1,0:T(8,128)S(1)}, f32[616,128]{1,0:T(8,128)S(1)}, u32[]{:S(2)}, u32[]{:S(2)}) collective-permute-start(f32[616,128]{1,0:T(8,128)S(1)} %back_products.16), channel_id=1, source_target_pairs={{0,1},{3,2},{4,5},{7,6},{8,9},{11,10},{12,13},{15,14},{16,17},{19,... | collective-permute-start | bytes 946184 | tf_op jit(solution)/shard_map/ppermute | solution.py:289
  23.6 14.8 %collective-permute-start.5 = (f32[616,128]{1,0:T(8,128)S(1)}, f32[616,128]{1,0:T(8,128)S(1)}, u32[]{:S(2)}, u32[]{:S(2)}) collective-permute-start(f32[616,128]{1,0:T(8,128)S(1)} %back_products.17), channel_id=1, source_target_pairs={{0,1},{3,2},{4,5},{7,6},{8,9},{11,10},{12,13},{15,14},{16,17},{19,... | collective-permute-start | bytes 946184 | tf_op jit(solution)/shard_map/ppermute | solution.py:289
  30.2 18.4 %collective-permute-start.4 = (f32[616,128]{1,0:T(8,128)S(1)}, f32[616,128]{1,0:T(8,128)S(1)}, u32[]{:S(2)}, u32[]{:S(2)}) collective-permute-start(f32[616,128]{1,0:T(8,128)S(1)} %add.261), channel_id=1, source_target_pairs={{1,2},{2,1},{5,6},{6,5},{9,10},{10,9},{13,14},{14,13},{17,18},{18,... | collective-permute-start | bytes 946184 | tf_op jit(solution)/shard_map/ppermute | solution.py:289
  38.4 16.7 %collective-permute-start.7 = (f32[616,128]{1,0:T(8,128)S(1)}, f32[616,128]{1,0:T(8,128)S(1)}, u32[]{:S(2)}, u32[]{:S(2)}) collective-permute-start(f32[616,128]{1,0:T(8,128)S(1)} %add.263), channel_id=1, source_target_pairs={{1,2},{2,1},{5,6},{6,5},{9,10},{10,9},{13,14},{14,13},{17,18},{18,... | collective-permute-start | bytes 946184 | tf_op jit(solution)/shard_map/ppermute | solution.py:289
  39.3 15.1 %collective-permute-start.8 = (f32[616,128]{1,0:T(8,128)S(1)}, f32[616,128]{1,0:T(8,128)S(1)}, u32[]{:S(2)}, u32[]{:S(2)}) collective-permute-start(f32[616,128]{1,0:T(8,128)S(1)} %back_products.18), channel_id=1, source_target_pairs={{0,1},{3,2},{4,5},{7,6},{8,9},{11,10},{12,13},{15,14},{16,17},{19,... | collective-permute-start | bytes 946184 | tf_op jit(solution)/shard_map/ppermute | solution.py:289
  48.8 13.6 %collective-permute-start.6 = (f32[616,128]{1,0:T(8,128)S(1)}, f32[616,128]{1,0:T(8,128)S(1)}, u32[]{:S(2)}, u32[]{:S(2)}) collective-permute-start(f32[616,128]{1,0:T(8,128)S(1)} %select_add_fusion.9), channel_id=1, source_target_pairs={{0,1},{1,0},{2,3},{3,2},{4,5},{5,4},{6,7},{7,6},{8,9},{9,8},{10,11... | collective-permute-start | bytes 946184 | tf_op jit(solution)/shard_map/ppermute | solution.py:289
  54.4 8.8 %collective-permute-start.10 = (f32[616,128]{1,0:T(8,128)S(1)}, f32[616,128]{1,0:T(8,128)S(1)}, u32[]{:S(2)}, u32[]{:S(2)}) collective-permute-start(f32[616,128]{1,0:T(8,128)S(1)} %add.268), channel_id=1, source_target_pairs={{1,2},{2,1},{5,6},{6,5},{9,10},{10,9},{13,14},{14,13},{17,18},{18,... | collective-permute-start | bytes 946184 | tf_op jit(solution)/shard_map/ppermute | solution.py:289
  55.8 13.4 %collective-permute-start.9 = (f32[616,128]{1,0:T(8,128)S(1)}, f32[616,128]{1,0:T(8,128)S(1)}, u32[]{:S(2)}, u32[]{:S(2)}) collective-permute-start(f32[616,128]{1,0:T(8,128)S(1)} %select_add_fusion.8), channel_id=1, source_target_pairs={{0,1},{1,0},{2,3},{3,2},{4,5},{5,4},{6,7},{7,6},{8,9},{9,8},{10,11... | collective-permute-start | bytes 946184 | tf_op jit(solution)/shard_map/ppermute | solution.py:289
  62.5 8.6 %collective-permute-start.12 = (f32[616,128]{1,0:T(8,128)S(1)}, f32[616,128]{1,0:T(8,128)S(1)}, u32[]{:S(2)}, u32[]{:S(2)}) collective-permute-start(f32[616,128]{1,0:T(8,128)S(1)} %get-tuple-element.226), channel_id=1, source_target_pairs={{1,2},{2,1},{5,6},{6,5},{9,10},{10,9},{13,14},{14,13},{17,18},{18,... | collective-permute-start | bytes 946184 | tf_op jit(solution)/shard_map/ppermute | solution.py:289
  63.8 13.4 %collective-permute-start.11 = (f32[616,128]{1,0:T(8,128)S(1)}, f32[616,128]{1,0:T(8,128)S(1)}, u32[]{:S(2)}, u32[]{:S(2)}) collective-permute-start(f32[616,128]{1,0:T(8,128)S(1)} %select_add_fusion.7), channel_id=1, source_target_pairs={{0,1},{1,0},{2,3},{3,2},{4,5},{5,4},{6,7},{7,6},{8,9},{9,8},{10,11... | collective-permute-start | bytes 946184 | tf_op jit(solution)/shard_map/ppermute | solution.py:289
  70.0 8.3 %collective-permute-start.14 = (f32[616,128]{1,0:T(8,128)S(1)}, f32[616,128]{1,0:T(8,128)S(1)}, u32[]{:S(2)}, u32[]{:S(2)}) collective-permute-start(f32[616,128]{1,0:T(8,128)S(1)} %get-tuple-element.236), channel_id=1, source_target_pairs={{1,2},{2,1},{5,6},{6,5},{9,10},{10,9},{13,14},{14,13},{17,18},{18,... | collective-permute-start | bytes 946184 | tf_op jit(solution)/shard_map/ppermute | solution.py:289
  71.2 14.2 %collective-permute-start.13 = (f32[616,128]{1,0:T(8,128)S(1)}, f32[616,128]{1,0:T(8,128)S(1)}, u32[]{:S(2)}, u32[]{:S(2)}) collective-permute-start(f32[616,128]{1,0:T(8,128)S(1)} %select_add_fusion.6), channel_id=1, source_target_pairs={{0,1},{1,0},{2,3},{3,2},{4,5},{5,4},{6,7},{7,6},{8,9},{9,8},{10,11... | collective-permute-start | bytes 946184 | tf_op jit(solution)/shard_map/ppermute | solution.py:289
  78.4 14.6 %collective-permute-start.15 = (f32[616,128]{1,0:T(8,128)S(1)}, f32[616,128]{1,0:T(8,128)S(1)}, u32[]{:S(2)}, u32[]{:S(2)}) collective-permute-start(f32[616,128]{1,0:T(8,128)S(1)} %select_add_fusion.5), channel_id=1, source_target_pairs={{0,1},{1,0},{2,3},{3,2},{4,5},{5,4},{6,7},{7,6},{8,9},{9,8},{10,11... | collective-permute-start | bytes 946184 | tf_op jit(solution)/shard_map/ppermute | solution.py:289
  84.8 8.4 %collective-permute-start.16 = (f32[616,128]{1,0:T(8,128)S(1)}, f32[616,128]{1,0:T(8,128)S(1)}, u32[]{:S(2)}, u32[]{:S(2)}) collective-permute-start(f32[616,128]{1,0:T(8,128)S(1)} %get-tuple-element.242), channel_id=1, source_target_pairs={{1,2},{2,1},{5,6},{6,5},{9,10},{10,9},{13,14},{14,13},{17,18},{18,... | collective-permute-start | bytes 946184 | tf_op jit(solution)/shard_map/ppermute | solution.py:289
  85.6 10.1 %collective-permute-start.18 = (f32[616,128]{1,0:T(8,128)S(1)}, f32[616,128]{1,0:T(8,128)S(1)}, u32[]{:S(2)}, u32[]{:S(2)}) collective-permute-start(f32[616,128]{1,0:T(8,128)S(1)} %get-tuple-element.248), channel_id=1, source_target_pairs={{1,2},{2,1},{5,6},{6,5},{9,10},{10,9},{13,14},{14,13},{17,18},{18,... | collective-permute-start | bytes 946184 | tf_op jit(solution)/shard_map/ppermute | solution.py:289
  93.2 3.8 %collective-permute-start.20 = (f32[616,128]{1,0:T(8,128)S(1)}, f32[616,128]{1,0:T(8,128)S(1)}, u32[]{:S(2)}, u32[]{:S(2)}) collective-permute-start(f32[616,128]{1,0:T(8,128)S(1)} %get-tuple-element.253), channel_id=1, source_target_pairs={{1,2},{2,1},{5,6},{6,5},{9,10},{10,9},{13,14},{14,13},{17,18},{18,... | collective-permute-start | bytes 946184 | tf_op jit(solution)/shard_map/ppermute | solution.py:289
  93.9 9.6 %collective-permute-start.17 = (f32[616,128]{1,0:T(8,128)S(1)}, f32[616,128]{1,0:T(8,128)S(1)}, u32[]{:S(2)}, u32[]{:S(2)}) collective-permute-start(f32[616,128]{1,0:T(8,128)S(1)} %add.284), channel_id=1, source_target_pairs={{1,0},{2,3},{5,4},{6,7},{9,8},{10,11},{13,12},{14,15},{17,16},{18,... | collective-permute-start | bytes 946184 | tf_op jit(solution)/shard_map/ppermute | solution.py:289
  95.7 11.2 %collective-permute-start.19 = (f32[616,128]{1,0:T(8,128)S(1)}, f32[616,128]{1,0:T(8,128)S(1)}, u32[]{:S(2)}, u32[]{:S(2)}) collective-permute-start(f32[616,128]{1,0:T(8,128)S(1)} %add.287), channel_id=1, source_target_pairs={{1,0},{2,3},{5,4},{6,7},{9,8},{10,11},{13,12},{14,15},{17,16},{18,... | collective-permute-start | bytes 946184 | tf_op jit(solution)/shard_map/ppermute | solution.py:289
  104.1 8.8 %collective-permute-start.21 = (f32[616,128]{1,0:T(8,128)S(1)}, f32[616,128]{1,0:T(8,128)S(1)}, u32[]{:S(2)}, u32[]{:S(2)}) collective-permute-start(f32[616,128]{1,0:T(8,128)S(1)} %add.290), channel_id=1, source_target_pairs={{1,0},{2,3},{5,4},{6,7},{9,8},{10,11},{13,12},{14,15},{17,16},{18,... | collective-permute-start | bytes 946184 | tf_op jit(solution)/shard_map/ppermute | solution.py:289
  113.5 1.2 collective-permute-start.22
  114.7 3.7 %collective-permute-start.23 = (f32[24,128]{1,0:T(8,128)S(1)}, f32[24,128]{1,0:T(8,128)S(1)}, u32[]{:S(2)}, u32[]{:S(2)}) collective-permute-start(f32[24,128]{1,0:T(8,128)S(1)} %add.293), channel_id=1, source_target_pairs={{0,8},{4,12},{8,0},{12,4},{16,24},{20,28},{24,16},{28,20},{1,9},{5... | collective-permute-start | bytes 36872 | tf_op jit(solution)/shard_map/ppermute | solution.py:230
  118.4 3.7 %collective-permute-start.24 = (f32[24,128]{1,0:T(8,128)S(1)}, f32[24,128]{1,0:T(8,128)S(1)}, u32[]{:S(2)}, u32[]{:S(2)}) collective-permute-start(f32[24,128]{1,0:T(8,128)S(1)} %add.294), channel_id=1, source_target_pairs={{0,16},{4,20},{8,24},{12,28},{16,0},{20,4},{24,8},{28,12},{1,17},{... | collective-permute-start | bytes 36872 | tf_op jit(solution)/shard_map/ppermute | solution.py:230
  122.7 9.3 %collective-permute-start.25 = (f32[616,128]{1,0:T(8,128)S(1)}, f32[616,128]{1,0:T(8,128)S(1)}, u32[]{:S(2)}, u32[]{:S(2)}) collective-permute-start(f32[616,128]{1,0:T(8,128)S(1)} %back_products.24), channel_id=1, source_target_pairs={{0,1},{3,2},{4,5},{7,6},{8,9},{11,10},{12,13},{15,14},{16,17},{19,... | collective-permute-start | bytes 946184 | tf_op jit(solution)/shard_map/ppermute | solution.py:289
  125.5 10.3 %collective-permute-start.27 = (f32[616,128]{1,0:T(8,128)S(1)}, f32[616,128]{1,0:T(8,128)S(1)}, u32[]{:S(2)}, u32[]{:S(2)}) collective-permute-start(f32[616,128]{1,0:T(8,128)S(1)} %back_products.25), channel_id=1, source_target_pairs={{0,1},{3,2},{4,5},{7,6},{8,9},{11,10},{12,13},{15,14},{16,17},{19,... | collective-permute-start | bytes 946184 | tf_op jit(solution)/shard_map/ppermute | solution.py:289
  132.1 11.0 %collective-permute-start.26 = (f32[616,128]{1,0:T(8,128)S(1)}, f32[616,128]{1,0:T(8,128)S(1)}, u32[]{:S(2)}, u32[]{:S(2)}) collective-permute-start(f32[616,128]{1,0:T(8,128)S(1)} %add.297), channel_id=1, source_target_pairs={{1,2},{2,1},{5,6},{6,5},{9,10},{10,9},{13,14},{14,13},{17,18},{18,... | collective-permute-start | bytes 946184 | tf_op jit(solution)/shard_map/ppermute | solution.py:289
  135.8 14.3 %collective-permute-start.29 = (f32[616,128]{1,0:T(8,128)S(1)}, f32[616,128]{1,0:T(8,128)S(1)}, u32[]{:S(2)}, u32[]{:S(2)}) collective-permute-start(f32[616,128]{1,0:T(8,128)S(1)} %add.299), channel_id=1, source_target_pairs={{1,2},{2,1},{5,6},{6,5},{9,10},{10,9},{13,14},{14,13},{17,18},{18,... | collective-permute-start | bytes 946184 | tf_op jit(solution)/shard_map/ppermute | solution.py:289
  136.5 12.9 %collective-permute-start.30 = (f32[616,128]{1,0:T(8,128)S(1)}, f32[616,128]{1,0:T(8,128)S(1)}, u32[]{:S(2)}, u32[]{:S(2)}) collective-permute-start(f32[616,128]{1,0:T(8,128)S(1)} %back_products.26), channel_id=1, source_target_pairs={{0,1},{3,2},{4,5},{7,6},{8,9},{11,10},{12,13},{15,14},{16,17},{19,... | collective-permute-start | bytes 946184 | tf_op jit(solution)/shard_map/ppermute | solution.py:289
  143.2 14.0 %collective-permute-start.28 = (f32[616,128]{1,0:T(8,128)S(1)}, f32[616,128]{1,0:T(8,128)S(1)}, u32[]{:S(2)}, u32[]{:S(2)}) collective-permute-start(f32[616,128]{1,0:T(8,128)S(1)} %select_add_fusion.4), channel_id=1, source_target_pairs={{0,1},{1,0},{2,3},{3,2},{4,5},{5,4},{6,7},{7,6},{8,9},{9,8},{10,11... | collective-permute-start | bytes 946184 | tf_op jit(solution)/shard_map/ppermute | solution.py:289
  149.5 8.5 %collective-permute-start.32 = (f32[616,128]{1,0:T(8,128)S(1)}, f32[616,128]{1,0:T(8,128)S(1)}, u32[]{:S(2)}, u32[]{:S(2)}) collective-permute-start(f32[616,128]{1,0:T(8,128)S(1)} %add.306), channel_id=1, source_target_pairs={{1,2},{2,1},{5,6},{6,5},{9,10},{10,9},{13,14},{14,13},{17,18},{18,... | collective-permute-start | bytes 946184 | tf_op jit(solution)/shard_map/ppermute | solution.py:289
  150.8 13.0 %collective-permute-start.31 = (f32[616,128]{1,0:T(8,128)S(1)}, f32[616,128]{1,0:T(8,128)S(1)}, u32[]{:S(2)}, u32[]{:S(2)}) collective-permute-start(f32[616,128]{1,0:T(8,128)S(1)} %select_add_fusion.3), channel_id=1, source_target_pairs={{0,1},{1,0},{2,3},{3,2},{4,5},{5,4},{6,7},{7,6},{8,9},{9,8},{10,11... | collective-permute-start | bytes 946184 | tf_op jit(solution)/shard_map/ppermute | solution.py:289
  157.3 8.4 %collective-permute-start.34 = (f32[616,128]{1,0:T(8,128)S(1)}, f32[616,128]{1,0:T(8,128)S(1)}, u32[]{:S(2)}, u32[]{:S(2)}) collective-permute-start(f32[616,128]{1,0:T(8,128)S(1)} %get-tuple-element.310), channel_id=1, source_target_pairs={{1,2},{2,1},{5,6},{6,5},{9,10},{10,9},{13,14},{14,13},{17,18},{18,... | collective-permute-start | bytes 946184 | tf_op jit(solution)/shard_map/ppermute | solution.py:289
  158.5 12.7 %collective-permute-start.33 = (f32[616,128]{1,0:T(8,128)S(1)}, f32[616,128]{1,0:T(8,128)S(1)}, u32[]{:S(2)}, u32[]{:S(2)}) collective-permute-start(f32[616,128]{1,0:T(8,128)S(1)} %select_add_fusion.2), channel_id=1, source_target_pairs={{0,1},{1,0},{2,3},{3,2},{4,5},{5,4},{6,7},{7,6},{8,9},{9,8},{10,11... | collective-permute-start | bytes 946184 | tf_op jit(solution)/shard_map/ppermute | solution.py:289
  164.6 9.0 %collective-permute-start.36 = (f32[616,128]{1,0:T(8,128)S(1)}, f32[616,128]{1,0:T(8,128)S(1)}, u32[]{:S(2)}, u32[]{:S(2)}) collective-permute-start(f32[616,128]{1,0:T(8,128)S(1)} %get-tuple-element.320), channel_id=1, source_target_pairs={{1,2},{2,1},{5,6},{6,5},{9,10},{10,9},{13,14},{14,13},{17,18},{18,... | collective-permute-start | bytes 946184 | tf_op jit(solution)/shard_map/ppermute | solution.py:289
  171.4 7.0 %collective-permute-start.35 = (f32[616,128]{1,0:T(8,128)S(1)}, f32[616,128]{1,0:T(8,128)S(1)}, u32[]{:S(2)}, u32[]{:S(2)}) collective-permute-start(f32[616,128]{1,0:T(8,128)S(1)} %select_add_fusion.1), channel_id=1, source_target_pairs={{0,1},{1,0},{2,3},{3,2},{4,5},{5,4},{6,7},{7,6},{8,9},{9,8},{10,11... | collective-permute-start | bytes 946184 | tf_op jit(solution)/shard_map/ppermute | solution.py:289
  173.7 8.6 %collective-permute-start.37 = (f32[616,128]{1,0:T(8,128)S(1)}, f32[616,128]{1,0:T(8,128)S(1)}, u32[]{:S(2)}, u32[]{:S(2)}) collective-permute-start(f32[616,128]{1,0:T(8,128)S(1)} %select_add_fusion), channel_id=1, source_target_pairs={{0,1},{1,0},{2,3},{3,2},{4,5},{5,4},{6,7},{7,6},{8,9},{9,8},{10,11... | collective-permute-start | bytes 946184 | tf_op jit(solution)/shard_map/ppermute | solution.py:289
  176.0 2.5 %collective-permute-start.38 = (f32[616,128]{1,0:T(8,128)S(1)}, f32[616,128]{1,0:T(8,128)S(1)}, u32[]{:S(2)}, u32[]{:S(2)}) collective-permute-start(f32[616,128]{1,0:T(8,128)S(1)} %get-tuple-element.326), channel_id=1, source_target_pairs={{1,2},{2,1},{5,6},{6,5},{9,10},{10,9},{13,14},{14,13},{17,18},{18,... | collective-permute-start | bytes 946184 | tf_op jit(solution)/shard_map/ppermute | solution.py:289
  179.0 13.5 %collective-permute-start.39 = (f32[616,128]{1,0:T(8,128)S(1)}, f32[616,128]{1,0:T(8,128)S(1)}, u32[]{:S(2)}, u32[]{:S(2)}) collective-permute-start(f32[616,128]{1,0:T(8,128)S(1)} %add.322), channel_id=1, source_target_pairs={{1,0},{2,3},{5,4},{6,7},{9,8},{10,11},{13,12},{14,15},{17,16},{18,... | collective-permute-start | bytes 946184 | tf_op jit(solution)/shard_map/ppermute | solution.py:289
  180.3 4.3 %collective-permute-start.40 = (f32[616,128]{1,0:T(8,128)S(1)}, f32[616,128]{1,0:T(8,128)S(1)}, u32[]{:S(2)}, u32[]{:S(2)}) collective-permute-start(f32[616,128]{1,0:T(8,128)S(1)} %get-tuple-element.332), channel_id=1, source_target_pairs={{1,2},{2,1},{5,6},{6,5},{9,10},{10,9},{13,14},{14,13},{17,18},{18,... | collective-permute-start | bytes 946184 | tf_op jit(solution)/shard_map/ppermute | solution.py:289
  182.4 10.6 %collective-permute-start.42 = (f32[616,128]{1,0:T(8,128)S(1)}, f32[616,128]{1,0:T(8,128)S(1)}, u32[]{:S(2)}, u32[]{:S(2)}) collective-permute-start(f32[616,128]{1,0:T(8,128)S(1)} %get-tuple-element.337), channel_id=1, source_target_pairs={{1,2},{2,1},{5,6},{6,5},{9,10},{10,9},{13,14},{14,13},{17,18},{18,... | collective-permute-start | bytes 946184 | tf_op jit(solution)/shard_map/ppermute | solution.py:289
  193.1 13.9 %collective-permute-start.43 = (f32[616,128]{1,0:T(8,128)S(1)}, f32[616,128]{1,0:T(8,128)S(1)}, u32[]{:S(2)}, u32[]{:S(2)}) collective-permute-start(f32[616,128]{1,0:T(8,128)S(1)} %add.328), channel_id=1, source_target_pairs={{1,0},{2,3},{5,4},{6,7},{9,8},{10,11},{13,12},{14,15},{17,16},{18,... | collective-permute-start | bytes 946184 | tf_op jit(solution)/shard_map/ppermute | solution.py:289
  194.4 16.0 %collective-permute-start.41 = (f32[616,128]{1,0:T(8,128)S(1)}, f32[616,128]{1,0:T(8,128)S(1)}, u32[]{:S(2)}, u32[]{:S(2)}) collective-permute-start(f32[616,128]{1,0:T(8,128)S(1)} %add.325), channel_id=1, source_target_pairs={{1,0},{2,3},{5,4},{6,7},{9,8},{10,11},{13,12},{14,15},{17,16},{18,... | collective-permute-start | bytes 946184 | tf_op jit(solution)/shard_map/ppermute | solution.py:289
  212.8 3.7 %collective-permute-start.45 = (f32[24,128]{1,0:T(8,128)S(1)}, f32[24,128]{1,0:T(8,128)S(1)}, u32[]{:S(2)}, u32[]{:S(2)}) collective-permute-start(f32[24,128]{1,0:T(8,128)S(1)} %add.333), channel_id=1, source_target_pairs={{0,8},{4,12},{8,0},{12,4},{16,24},{20,28},{24,16},{28,20},{1,9},{5... | collective-permute-start | bytes 36872 | tf_op jit(solution)/shard_map/ppermute | solution.py:230
  216.5 3.7 %collective-permute-start.46 = (f32[24,128]{1,0:T(8,128)S(1)}, f32[24,128]{1,0:T(8,128)S(1)}, u32[]{:S(2)}, u32[]{:S(2)}) collective-permute-start(f32[24,128]{1,0:T(8,128)S(1)} %add.334), channel_id=1, source_target_pairs={{0,16},{4,20},{8,24},{12,28},{16,0},{20,4},{24,8},{28,12},{1,17},{... | collective-permute-start | bytes 36872 | tf_op jit(solution)/shard_map/ppermute | solution.py:230
  220.2 3.6 %collective-permute-start.47 = (f32[1,128]{1,0:T(1,128)S(1)}, f32[1,128]{1,0:T(1,128)S(1)}, u32[]{:S(2)}, u32[]{:S(2)}) collective-permute-start(f32[1,128]{1,0:T(1,128)S(1)} %bitcast.36), channel_id=1, source_target_pairs={{0,1},{1,0},{2,3},{3,2},{4,5},{5,4},{6,7},{7,6},{8,9},{9,8},{10,11... | collective-permute-start | bytes 1544 | tf_op jit(solution)/shard_map/ppermute | solution.py:230
  223.8 4.4 %collective-permute-start.48 = (f32[1,128]{1,0:T(1,128)S(1)}, f32[1,128]{1,0:T(1,128)S(1)}, u32[]{:S(2)}, u32[]{:S(2)}) collective-permute-start(f32[1,128]{1,0:T(1,128)S(1)} %bitcast_add_fusion), channel_id=1, source_target_pairs={{0,2},{1,3},{2,0},{3,1},{4,6},{5,7},{6,4},{7,5},{8,10},{9,11},{10,... | collective-permute-start | bytes 1544 | tf_op jit(solution)/shard_map/ppermute | solution.py:230
  (16 other events, 120.5 us)

commit v3 on v2

--- a/solution.py
+++ b/solution.py
@@ -12,7 +12,9 @@
 SUBLANES = 8
 CHUNKS = 8
 COPIES = 8
-CHUNK_VMEM = 8 * 2**20
+START_VMEM = 3 * 2**20
+BACK_VMEM = 1 * 2**20
+ADVANCE_VMEM = 3 * 2**20
 EXTRA = 8
 
 
@@ -124,8 +126,8 @@
             pltpu.VMEM((rows, LANES), jnp.float32),
             pltpu.SemaphoreType.DMA((copies,)),
         ],
-        compiler_params=pltpu.CompilerParams(vmem_limit_bytes=CHUNK_VMEM),
-        cost_estimate=pl.CostEstimate(flops=16 * rows * LANES, bytes_accessed=36 * rows * LANES, transcendentals=0),
+        compiler_params=pltpu.CompilerParams(vmem_limit_bytes=START_VMEM),
+        cost_estimate=pl.CostEstimate(flops=0, bytes_accessed=0, transcendentals=0),
         name="start_products",
     )(pltpu.with_memory_space_constraint(derivs, pltpu.HBM), pltpu.with_memory_space_constraint(grad, pltpu.HBM))
 
@@ -152,8 +154,8 @@
         in_specs=[vmem(), vmem()],
         out_specs=vmem(),
         out_shape=jax.ShapeDtypeStruct((rows + EXTRA, LANES), jnp.float32),
-        compiler_params=pltpu.CompilerParams(vmem_limit_bytes=CHUNK_VMEM),
-        cost_estimate=pl.CostEstimate(flops=16 * rows * LANES, bytes_accessed=36 * rows * LANES, transcendentals=0),
+        compiler_params=pltpu.CompilerParams(vmem_limit_bytes=BACK_VMEM),
+        cost_estimate=pl.CostEstimate(flops=0, bytes_accessed=0, transcendentals=0),
         name="back_products",
     )(pltpu.with_memory_space_constraint(derivs, pltpu.VMEM), vals)
 
@@ -195,47 +197,60 @@
             jax.ShapeDtypeStruct((rows, LANES), jnp.float32),
             jax.ShapeDtypeStruct((24, LANES), jnp.float32),
         ],
-        compiler_params=pltpu.CompilerParams(vmem_limit_bytes=CHUNK_VMEM),
-        cost_estimate=pl.CostEstimate(flops=24 * rows * LANES, bytes_accessed=48 * rows * LANES, transcendentals=0),
+        compiler_params=pltpu.CompilerParams(vmem_limit_bytes=ADVANCE_VMEM),
+        cost_estimate=pl.CostEstimate(flops=0, bytes_accessed=0, transcendentals=0),
         name="advance_residual",
     )(pltpu.with_memory_space_constraint(derivs, pltpu.VMEM), back, first_back, known, residual, prev, stats)
 
 
-def last_kernel(share_ref, grad_ref, res1_ref, res2_ref, coef_ref, out_ref):
-    c0, c1, c2 = coef_ref[0:1, :], coef_ref[1:2, :], coef_ref[2:3, :]
-    out_ref[...] = c0 * grad_ref[...] + c1 * res1_ref[...] + c2 * res2_ref[...]
-
-
-def last_call(share, grad, res1, res2, coefs, share_rows):
+def share_kernel(share_ref, grad_ref, res1_ref, res2_ref, coef_ref, base_ref, dir_ref, last_ref):
+    step0, step1, beta1 = (coef_ref[i : i + 1, :] for i in range(3))
+    direction1 = res1_ref[...] + beta1 * grad_ref[...]
+    base_ref[...] = step0 * grad_ref[...] + step1 * direction1
+    dir_ref[...] = direction1
+    last_ref[...] = res2_ref[...]
+
+
+def share_call(share, grad, res1, res2, coefs, share_rows):
     vec = pl.BlockSpec((share_rows, LANES), lambda i, share_ref: (share_ref[0], 0))
+    out = pl.BlockSpec((share_rows, LANES), lambda i, share_ref: (0, 0))
     return pl.pallas_call(
-        last_kernel,
+        share_kernel,
         grid_spec=pltpu.PrefetchScalarGridSpec(
             num_scalar_prefetch=1,
             grid=(1,),
             in_specs=[vec, vec, vec, pl.BlockSpec((SUBLANES, LANES), lambda i, share_ref: (0, 0))],
-            out_specs=pl.BlockSpec((share_rows, LANES), lambda i, share_ref: (0, 0)),
+            out_specs=[out] * 3,
         ),
-        out_shape=jax.ShapeDtypeStruct((share_rows, LANES), jnp.float32),
-        name="last_combination",
+        out_shape=[pltpu.VMEM((share_rows, LANES), jnp.float32)] * 3,
+        cost_estimate=pl.CostEstimate(flops=0, bytes_accessed=24 * share_rows * LANES, transcendentals=0),
+        name="share_parts",
     )(share, grad, res1, res2, coefs)
 
 
-def small_sum(value, axis):
+def small_sum(value, axis, beside=()):
     size = lax.axis_size(axis)
     if size & (size - 1):
-        return lax.psum(value, axis)
+        return lax.psum(value, axis), beside
     bit = 1
     while bit < size:
-        value = value + lax.ppermute(value, axis, [(i, i ^ bit) for i in range(size)])
-        bit *= 2
-    return value
+        if bit > 1 and beside:
+            value, *beside = lax.optimization_barrier((value, *beside))
+        fan = 2 if bit * 4 > size or (bit == 1 and size not in (4, 16)) else 4
+        got = [lax.ppermute(value, axis, [(i, i ^ (bit * j)) for i in range(size)]) for j in range(1, fan)]
+        if fan == 4:
+            first = value + got[0]
+            value = first + (got[1] + got[2])
+        else:
+            value = value + got[0]
+        bit *= fan
+    return value, tuple(beside)
 
 
 def chain(chunks, produce, consume, state, gate):
     count = lax.axis_size("walker")
     me = lax.axis_index("walker")
-    gaps = (1, 2)
+    gaps = (2, 2)
     up, down = [0], [0]
     for link in range(count - 2):
         up.append(up[-1] + gaps[link % 2])
@@ -336,13 +351,15 @@
         state = (jnp.zeros((24, LANES), jnp.float32),)
         (stats,) = chain(chunks, produce, consume, state, vals)
         step = step_length(norm, first[0][part : part + 1], rows_all, dir_sq)
-        return fresh, step, small_sum(stats, "param")
+        return fresh, step, stats
 
     stats, derivs = start_call(derivs, grad)
-    stats = small_sum(stats, "param")
+    stats, _ = small_sum(stats, "param")
     vals0, norm0 = stats[0:8], stats[8:9]
     dir_sq0 = norm0
     res1, step0, stats = advance(grad, grad, vals0, norm0, dir_sq0, jnp.zeros_like(norm0))
+
+    stats, _ = small_sum(stats, "param")
 
     norm1, cross1 = stats[8:9], stats[16:17]
     beta1 = norm1 / norm0
@@ -350,18 +367,19 @@
     dir_sq1 = norm1 + 2.0 * beta1 * cross1 + beta1 * beta1 * dir_sq0
     res2, step1, stats = advance(res1, grad, vals1, norm1, dir_sq1, beta1)
 
+    coefs = jnp.concatenate([step0, step1, beta1, jnp.zeros((5, LANES), jnp.float32)])
+    whole1, whole2 = jnp.concatenate(res1), jnp.concatenate(res2)
+    stats, (whole1, whole2, coefs) = small_sum(stats, "param", (whole1, whole2, coefs))
+    share = lax.axis_index("walker").astype(jnp.int32).reshape(1)
+    base, direction1, res = share_call(share, grad, whole1, whole2, coefs, rows // walkers)
+
     norm2, cross2 = stats[8:9], stats[16:17]
     beta2 = norm2 / norm1
     vals2 = stats[0:8] + beta2 * vals1
     dir_sq2 = norm2 + 2.0 * beta2 * cross2 + beta2 * beta2 * dir_sq1
-    squares = small_sum(jnp.sum(vals2 * vals2, axis=0, keepdims=True), "walker")
+    squares, _ = small_sum(jnp.sum(vals2 * vals2, axis=0, keepdims=True), "walker")
     step2 = step_length(norm2, squares, rows_all, dir_sq2)
-
-    along1 = step1 + step2 * beta2
-    coefs = jnp.concatenate([step0 + along1 * beta1, along1, step2, jnp.zeros((5, LANES), jnp.float32)])
-    share = lax.axis_index("walker").astype(jnp.int32).reshape(1)
-    out = last_call(share, grad, jnp.concatenate(res1), jnp.concatenate(res2), coefs, rows // walkers)
-    return out.reshape(-1)
+    return (base + step2 * (res + beta2 * direction1)).reshape(-1)
 
 
 def solution(mesh):

time: 232 us -> 213 us (0.918)
  waiting for transfers between devices: 93.8 us -> 80.9 us
  starting transfers between devices: 97.5 us -> 87.5 us
  local copies, waits for them, and re-layouts: 8.21 us -> 11.6 us
    ppermute x38 -> x40, starting transfers between devices: 85.2 us -> 72 us  [exchange(): got[parity].append(lax.ppermute(own, 'walker', pairs))]
    ppermute x11 -> x15, waiting for transfers between devices: 22.3 us -> 12.8 us  [small_sum(): lax.ppermute(value, axis, [(i, i ^ bit * j) for i in range(size)])]
    ppermute x38 -> x40, waiting for transfers between devices: 71.5 us -> 68.1 us  [exchange(): got[parity].append(lax.ppermute(own, 'walker', pairs))]
    unnamed x42 -> x30, local copies, waits for them, and re-layouts: 8 us -> 11.4 us
    ppermute x11 -> x15, starting transfers between devices: 12.3 us -> 15.4 us  [small_sum(): lax.ppermute(value, axis, [(i, i ^ bit * j) for i in range(size)])]
  transfers between devices with their start and end apart: 49 -> 55, of which waited for: 28 -> 32; matrix products, arithmetic and copies ran while one was open for 1% -> 2% of each run, Pallas kernels for 6% -> 7%
where the time goes in v3:
time: 213 us; the launch traced here: 212 us
  starting transfers between devices  87.5 us (41%)
  waiting for transfers between devices  80.9 us (38%)
  Pallas kernels  26.4 us (12%)
  local copies, waits for them, and re-layouts  11.6 us (5%)
  other arithmetic  4.54 us (2%)
    ppermute x40, starting transfers between devices, exchange(): got[parity].append(lax.ppermute(own, 'walker', pairs))  72 us
    ppermute x40, waiting for transfers between devices, exchange(): got[parity].append(lax.ppermute(own, 'walker', pairs))  68.1 us
    ppermute x15, starting transfers between devices, small_sum(): lax.ppermute(value, axis, [(i, i ^ bit * j) for i in range(size)])  15.4 us
    ppermute x15, waiting for transfers between devices, small_sum(): lax.ppermute(value, axis, [(i, i ^ bit * j) for i in range(size)])  12.8 us
    unnamed x30, local copies, waits for them, and re-layouts  11.4 us
    pallas_call x16, Pallas kernels, back_call(): pl.pallas_call(functools.partial(back_kernel, chunk * rows), in_specs=[vm...  9.58 us
    pallas_call x1, Pallas kernels, start_call(): pl.pallas_call(functools.partial(start_kernel, copies), in_specs=[hbm(),...  8.09 us
    pallas_call x16, Pallas kernels, advance_call(): pl.pallas_call(functools.partial(advance_kernel, chunk * rows, rows_all,...  7.16 us
  transfers between devices with their start and end apart: 55, of which 32 were waited for; matrix products, arithmetic and copies ran while one was open for 2% of the time, Pallas kernels for 7%

profile of v3, /device:TPU:0, one launch (start us, length us, event | category | flops | bytes accessed | tf_op | source)
XLA Modules:
  0.0 211.8 jit_solution(5524377362648620920)
XLA Ops:
  0.0 8.1 %start_products.1 = (f32[24,128]{1,0:T(8,128)S(1)}, f32[8,622592]{1,0:T(8,128)S(1)}) custom-call(f32[8,622592]{1,0:T(8,128)} %derivs_hbm.1, f32[4864,128]{1,0:T(8,128)} %bitcast.11), custom_call_target="tpu_custom_call" | custom-call | tf_op jit(solution)/shard_map/start_products/pallas_call | solution.py:119
  9.5 2.9 %collective-permute-start.2 = (f32[24,128]{1,0:T(8,128)S(1)}, f32[24,128]{1,0:T(8,128)S(1)}, u32[]{:S(2)}, u32[]{:S(2)}) collective-permute-start(f32[24,128]{1,0:T(8,128)S(1)} %add.270), channel_id=1, source_target_pairs={{0,16},{4,20},{8,24},{12,28},{16,0},{20,4},{24,8},{28,12},{1,17},{... | collective-permute-start | bytes 36872 | tf_op jit(solution)/shard_map/ppermute | solution.py:240
  12.3 1.4 collective-permute-start.3
  14.0 2.9 %collective-permute-done.3 = f32[24,128]{1,0:T(8,128)S(1)} collective-permute-done((f32[24,128]{1,0:T(8,128)S(1)}, f32[24,128]{1,0:T(8,128)S(1)}, u32[]{:S(2)}, u32[]{:S(2)}) %collective-permute-start.3) | collective-permute-done | bytes 12320 | tf_op jit(solution)/shard_map/ppermute | solution.py:240
  18.1 3.5 %collective-permute-start.4 = (f32[616,128]{1,0:T(8,128)S(1)}, f32[616,128]{1,0:T(8,128)S(1)}, u32[]{:S(2)}, u32[]{:S(2)}) collective-permute-start(f32[616,128]{1,0:T(8,128)S(1)} %back_products.16), channel_id=1, source_target_pairs={{0,1},{3,2},{4,5},{7,6},{8,9},{11,10},{12,13},{15,14},{16,17},{19,... | collective-permute-start | bytes 946184 | tf_op jit(solution)/shard_map/ppermute | solution.py:304
  23.4 1.3 collective-permute-start.6
  24.7 4.7 %collective-permute-done.4 = f32[616,128]{1,0:T(8,128)S(1)} collective-permute-done((f32[616,128]{1,0:T(8,128)S(1)}, f32[616,128]{1,0:T(8,128)S(1)}, u32[]{:S(2)}, u32[]{:S(2)}) %collective-permute-start.4) | collective-permute-done | bytes 315424 | tf_op jit(solution)/shard_map/ppermute | solution.py:304
  30.3 7.2 %collective-permute-start.8 = (f32[616,128]{1,0:T(8,128)S(1)}, f32[616,128]{1,0:T(8,128)S(1)}, u32[]{:S(2)}, u32[]{:S(2)}) collective-permute-start(f32[616,128]{1,0:T(8,128)S(1)} %back_products.18), channel_id=1, source_target_pairs={{0,1},{3,2},{4,5},{7,6},{8,9},{11,10},{12,13},{15,14},{16,17},{19,... | collective-permute-start | bytes 946184 | tf_op jit(solution)/shard_map/ppermute | solution.py:304
  37.5 1.3 collective-permute-start.10
  38.9 6.7 %copy-done.1 = f32[8,622592]{1,0:T(8,128)S(1)} copy-done((f32[8,622592]{1,0:T(8,128)S(1)}, f32[8,622592]{1,0:T(8,128)}, u32[]{:S(2)}) %copy-start.1) | copy-done | bytes 19922968
  47.1 1.4 collective-permute-start.11
  48.6 3.6 %copy-done.2 = f32[8,622592]{1,0:T(8,128)S(1)} copy-done((f32[8,622592]{1,0:T(8,128)S(1)}, f32[8,622592]{1,0:T(8,128)}, u32[]{:S(2)}) %copy-start.2) | copy-done | bytes 19922968
  55.1 6.4 %collective-permute-start.13 = (f32[616,128]{1,0:T(8,128)S(1)}, f32[616,128]{1,0:T(8,128)S(1)}, u32[]{:S(2)}, u32[]{:S(2)}) collective-permute-start(f32[616,128]{1,0:T(8,128)S(1)} %select_add_fusion.6), channel_id=1, source_target_pairs={{0,1},{1,0},{2,3},{3,2},{4,5},{5,4},{6,7},{7,6},{8,9},{9,8},{10,11... | collective-permute-start | bytes 946184 | tf_op jit(solution)/shard_map/ppermute | solution.py:304
  62.7 3.4 %collective-permute-start.16 = (f32[616,128]{1,0:T(8,128)S(1)}, f32[616,128]{1,0:T(8,128)S(1)}, u32[]{:S(2)}, u32[]{:S(2)}) collective-permute-start(f32[616,128]{1,0:T(8,128)S(1)} %select_add_fusion.5), channel_id=1, source_target_pairs={{0,1},{1,0},{2,3},{3,2},{4,5},{5,4},{6,7},{7,6},{8,9},{9,8},{10,11... | collective-permute-start | bytes 946184 | tf_op jit(solution)/shard_map/ppermute | solution.py:304
  68.1 4.1 %collective-permute-start.14 = (f32[616,128]{1,0:T(8,128)S(1)}, f32[616,128]{1,0:T(8,128)S(1)}, u32[]{:S(2)}, u32[]{:S(2)}) collective-permute-start(f32[616,128]{1,0:T(8,128)S(1)} %select_add_fusion.4), channel_id=1, source_target_pairs={{0,1},{1,0},{2,3},{3,2},{4,5},{5,4},{6,7},{7,6},{8,9},{9,8},{10,11... | collective-permute-start | bytes 946184 | tf_op jit(solution)/shard_map/ppermute | solution.py:304
  75.0 1.3 collective-permute-start.21
  76.3 2.1 collective-permute-done.14
  81.0 6.4 %collective-permute-done.21 = f32[616,128]{1,0:T(8,128)S(1)} collective-permute-done((f32[616,128]{1,0:T(8,128)S(1)}, f32[616,128]{1,0:T(8,128)S(1)}, u32[]{:S(2)}, u32[]{:S(2)}) %collective-permute-start.21) | collective-permute-done | bytes 315424 | tf_op jit(solution)/shard_map/ppermute | solution.py:304
  87.9 1.3 collective-permute-start.23
  89.2 4.9 %collective-permute-done.19 = f32[616,128]{1,0:T(8,128)S(1)} collective-permute-done((f32[616,128]{1,0:T(8,128)S(1)}, f32[616,128]{1,0:T(8,128)S(1)}, u32[]{:S(2)}, u32[]{:S(2)}) %collective-permute-start.19) | collective-permute-done | bytes 315424 | tf_op jit(solution)/shard_map/ppermute | solution.py:304
  94.7 1.3 collective-permute-start.22
  96.0 4.9 %collective-permute-done.23 = f32[616,128]{1,0:T(8,128)S(1)} collective-permute-done((f32[616,128]{1,0:T(8,128)S(1)}, f32[616,128]{1,0:T(8,128)S(1)}, u32[]{:S(2)}, u32[]{:S(2)}) %collective-permute-start.23) | collective-permute-done | bytes 315424 | tf_op jit(solution)/shard_map/ppermute | solution.py:304
  101.4 2.9 %collective-permute-done.22 = f32[616,128]{1,0:T(8,128)S(1)} collective-permute-done((f32[616,128]{1,0:T(8,128)S(1)}, f32[616,128]{1,0:T(8,128)S(1)}, u32[]{:S(2)}, u32[]{:S(2)}) %collective-permute-start.22) | collective-permute-done | bytes 315424 | tf_op jit(solution)/shard_map/ppermute | solution.py:304
  106.1 1.8 collective-permute-start.26
  109.8 2.7 %collective-permute-done.27 = f32[24,128]{1,0:T(8,128)S(1)} collective-permute-done((f32[24,128]{1,0:T(8,128)S(1)}, f32[24,128]{1,0:T(8,128)S(1)}, u32[]{:S(2)}, u32[]{:S(2)}) %collective-permute-start.27) | collective-permute-done | bytes 12320 | tf_op jit(solution)/shard_map/ppermute | solution.py:240
  113.4 1.5 collective-permute-start.28
  116.7 1.3 collective-permute-start.30
  118.1 4.6 %collective-permute-done.28 = f32[616,128]{1,0:T(8,128)S(1)} collective-permute-done((f32[616,128]{1,0:T(8,128)S(1)}, f32[616,128]{1,0:T(8,128)S(1)}, u32[]{:S(2)}, u32[]{:S(2)}) %collective-permute-start.28) | collective-permute-done | bytes 315424 | tf_op jit(solution)/shard_map/ppermute | solution.py:304
  123.5 6.2 %collective-permute-start.32 = (f32[616,128]{1,0:T(8,128)S(1)}, f32[616,128]{1,0:T(8,128)S(1)}, u32[]{:S(2)}, u32[]{:S(2)}) collective-permute-start(f32[616,128]{1,0:T(8,128)S(1)} %back_products.26), channel_id=1, source_target_pairs={{0,1},{3,2},{4,5},{7,6},{8,9},{11,10},{12,13},{15,14},{16,17},{19,... | collective-permute-start | bytes 946184 | tf_op jit(solution)/shard_map/ppermute | solution.py:304
  131.0 4.7 %collective-permute-start.34 = (f32[616,128]{1,0:T(8,128)S(1)}, f32[616,128]{1,0:T(8,128)S(1)}, u32[]{:S(2)}, u32[]{:S(2)}) collective-permute-start(f32[616,128]{1,0:T(8,128)S(1)} %back_products.27), channel_id=1, source_target_pairs={{0,1},{3,2},{4,5},{7,6},{8,9},{11,10},{12,13},{15,14},{16,17},{19,... | collective-permute-start | bytes 946184 | tf_op jit(solution)/shard_map/ppermute | solution.py:304
  139.4 4.3 %collective-permute-done.34 = f32[616,128]{1,0:T(8,128)S(1)} collective-permute-done((f32[616,128]{1,0:T(8,128)S(1)}, f32[616,128]{1,0:T(8,128)S(1)}, u32[]{:S(2)}, u32[]{:S(2)}) %collective-permute-start.34) | collective-permute-done | bytes 315424 | tf_op jit(solution)/shard_map/ppermute | solution.py:304
  143.6 2.5 %collective-permute-start.37 = (f32[616,128]{1,0:T(8,128)S(1)}, f32[616,128]{1,0:T(8,128)S(1)}, u32[]{:S(2)}, u32[]{:S(2)}) collective-permute-start(f32[616,128]{1,0:T(8,128)S(1)} %select_add_fusion.2), channel_id=1, source_target_pairs={{0,1},{1,0},{2,3},{3,2},{4,5},{5,4},{6,7},{7,6},{8,9},{9,8},{10,11... | collective-permute-start | bytes 946184 | tf_op jit(solution)/shard_map/ppermute | solution.py:304
  146.9 3.5 %collective-permute-done.35 = f32[616,128]{1,0:T(8,128)S(1)} collective-permute-done((f32[616,128]{1,0:T(8,128)S(1)}, f32[616,128]{1,0:T(8,128)S(1)}, u32[]{:S(2)}, u32[]{:S(2)}) %collective-permute-start.35) | collective-permute-done | bytes 315424 | tf_op jit(solution)/shard_map/ppermute | solution.py:304
  151.7 2.5 %collective-permute-start.40 = (f32[616,128]{1,0:T(8,128)S(1)}, f32[616,128]{1,0:T(8,128)S(1)}, u32[]{:S(2)}, u32[]{:S(2)}) collective-permute-start(f32[616,128]{1,0:T(8,128)S(1)} %select_add_fusion.1), channel_id=1, source_target_pairs={{0,1},{1,0},{2,3},{3,2},{4,5},{5,4},{6,7},{7,6},{8,9},{9,8},{10,11... | collective-permute-start | bytes 946184 | tf_op jit(solution)/shard_map/ppermute | solution.py:304
  155.5 1.6 collective-permute-done.37
  157.8 2.5 %collective-permute-start.38 = (f32[616,128]{1,0:T(8,128)S(1)}, f32[616,128]{1,0:T(8,128)S(1)}, u32[]{:S(2)}, u32[]{:S(2)}) collective-permute-start(f32[616,128]{1,0:T(8,128)S(1)} %select_add_fusion), channel_id=1, source_target_pairs={{0,1},{1,0},{2,3},{3,2},{4,5},{5,4},{6,7},{7,6},{8,9},{9,8},{10,11... | collective-permute-start | bytes 946184 | tf_op jit(solution)/shard_map/ppermute | solution.py:304
  161.0 2.8 %collective-permute-done.40 = f32[616,128]{1,0:T(8,128)S(1)} collective-permute-done((f32[616,128]{1,0:T(8,128)S(1)}, f32[616,128]{1,0:T(8,128)S(1)}, u32[]{:S(2)}, u32[]{:S(2)}) %collective-permute-start.40) | collective-permute-done | bytes 315424 | tf_op jit(solution)/shard_map/ppermute | solution.py:304
  165.2 1.3 collective-permute-start.45
  166.5 1.4 collective-permute-done.38
  170.5 9.2 %collective-permute-done.45 = f32[616,128]{1,0:T(8,128)S(1)} collective-permute-done((f32[616,128]{1,0:T(8,128)S(1)}, f32[616,128]{1,0:T(8,128)S(1)}, u32[]{:S(2)}, u32[]{:S(2)}) %collective-permute-start.45) | collective-permute-done | bytes 315424 | tf_op jit(solution)/shard_map/ppermute | solution.py:304
  181.7 4.9 %collective-permute-done.43 = f32[616,128]{1,0:T(8,128)S(1)} collective-permute-done((f32[616,128]{1,0:T(8,128)S(1)}, f32[616,128]{1,0:T(8,128)S(1)}, u32[]{:S(2)}, u32[]{:S(2)}) %collective-permute-start.43) | collective-permute-done | bytes 315424 | tf_op jit(solution)/shard_map/ppermute | solution.py:304
  188.5 4.8 %collective-permute-done.47 = f32[616,128]{1,0:T(8,128)S(1)} collective-permute-done((f32[616,128]{1,0:T(8,128)S(1)}, f32[616,128]{1,0:T(8,128)S(1)}, u32[]{:S(2)}, u32[]{:S(2)}) %collective-permute-start.47) | collective-permute-done | bytes 315424 | tf_op jit(solution)/shard_map/ppermute | solution.py:304
  193.3 3.7 %collective-permute-done.46 = f32[616,128]{1,0:T(8,128)S(1)} collective-permute-done((f32[616,128]{1,0:T(8,128)S(1)}, f32[616,128]{1,0:T(8,128)S(1)}, u32[]{:S(2)}, u32[]{:S(2)}) %collective-permute-start.46) | collective-permute-done | bytes 315424 | tf_op jit(solution)/shard_map/ppermute | solution.py:304
  199.7 1.4 collective-permute-start.51
  201.1 1.6 collective-permute-start.49
  202.9 1.3 collective-permute-done.51
  205.4 2.0 collective-permute-start.54
  208.4 1.6 share_parts.1
  (189 shorter events, 51.3 us)
Async XLA Ops:
  9.5 4.5 %collective-permute-start.2 = (f32[24,128]{1,0:T(8,128)S(1)}, f32[24,128]{1,0:T(8,128)S(1)}, u32[]{:S(2)}, u32[]{:S(2)}) collective-permute-start(f32[24,128]{1,0:T(8,128)S(1)} %add.270), channel_id=1, source_target_pairs={{0,16},{4,20},{8,24},{12,28},{16,0},{20,4},{24,8},{28,12},{1,17},{... | collective-permute-start | bytes 36872 | tf_op jit(solution)/shard_map/ppermute | solution.py:240
  12.3 4.6 %collective-permute-start.3 = (f32[24,128]{1,0:T(8,128)S(1)}, f32[24,128]{1,0:T(8,128)S(1)}, u32[]{:S(2)}, u32[]{:S(2)}) collective-permute-start(f32[24,128]{1,0:T(8,128)S(1)} %add.270), channel_id=1, source_target_pairs={{0,24},{4,28},{8,16},{12,20},{16,8},{20,12},{24,0},{28,4},{1,25},{... | collective-permute-start | bytes 36872 | tf_op jit(solution)/shard_map/ppermute | solution.py:240
  13.8 3.7 %collective-permute-start.1 = (f32[24,128]{1,0:T(8,128)S(1)}, f32[24,128]{1,0:T(8,128)S(1)}, u32[]{:S(2)}, u32[]{:S(2)}) collective-permute-start(f32[24,128]{1,0:T(8,128)S(1)} %add.270), channel_id=1, source_target_pairs={{0,8},{4,12},{8,0},{12,4},{16,24},{20,28},{24,16},{28,20},{1,9},{5... | collective-permute-start | bytes 36872 | tf_op jit(solution)/shard_map/ppermute | solution.py:240
  18.1 11.4 %collective-permute-start.4 = (f32[616,128]{1,0:T(8,128)S(1)}, f32[616,128]{1,0:T(8,128)S(1)}, u32[]{:S(2)}, u32[]{:S(2)}) collective-permute-start(f32[616,128]{1,0:T(8,128)S(1)} %back_products.16), channel_id=1, source_target_pairs={{0,1},{3,2},{4,5},{7,6},{8,9},{11,10},{12,13},{15,14},{16,17},{19,... | collective-permute-start | bytes 946184 | tf_op jit(solution)/shard_map/ppermute | solution.py:304
  23.4 22.7 %collective-permute-start.6 = (f32[616,128]{1,0:T(8,128)S(1)}, f32[616,128]{1,0:T(8,128)S(1)}, u32[]{:S(2)}, u32[]{:S(2)}) collective-permute-start(f32[616,128]{1,0:T(8,128)S(1)} %back_products.17), channel_id=1, source_target_pairs={{0,1},{3,2},{4,5},{7,6},{8,9},{11,10},{12,13},{15,14},{16,17},{19,... | collective-permute-start | bytes 946184 | tf_op jit(solution)/shard_map/ppermute | solution.py:304
  29.5 17.5 %collective-permute-start.5 = (f32[616,128]{1,0:T(8,128)S(1)}, f32[616,128]{1,0:T(8,128)S(1)}, u32[]{:S(2)}, u32[]{:S(2)}) collective-permute-start(f32[616,128]{1,0:T(8,128)S(1)} %add.274), channel_id=1, source_target_pairs={{1,2},{2,1},{5,6},{6,5},{9,10},{10,9},{13,14},{14,13},{17,18},{18,... | collective-permute-start | bytes 946184 | tf_op jit(solution)/shard_map/ppermute | solution.py:304
  30.3 18.2 %collective-permute-start.8 = (f32[616,128]{1,0:T(8,128)S(1)}, f32[616,128]{1,0:T(8,128)S(1)}, u32[]{:S(2)}, u32[]{:S(2)}) collective-permute-start(f32[616,128]{1,0:T(8,128)S(1)} %back_products.18), channel_id=1, source_target_pairs={{0,1},{3,2},{4,5},{7,6},{8,9},{11,10},{12,13},{15,14},{16,17},{19,... | collective-permute-start | bytes 946184 | tf_op jit(solution)/shard_map/ppermute | solution.py:304
  37.5 16.6 %collective-permute-start.10 = (f32[616,128]{1,0:T(8,128)S(1)}, f32[616,128]{1,0:T(8,128)S(1)}, u32[]{:S(2)}, u32[]{:S(2)}) collective-permute-start(f32[616,128]{1,0:T(8,128)S(1)} %back_products.19), channel_id=1, source_target_pairs={{0,1},{3,2},{4,5},{7,6},{8,9},{11,10},{12,13},{15,14},{16,17},{19,... | collective-permute-start | bytes 946184 | tf_op jit(solution)/shard_map/ppermute | solution.py:304
  46.2 7.3 %collective-permute-start.7 = (f32[616,128]{1,0:T(8,128)S(1)}, f32[616,128]{1,0:T(8,128)S(1)}, u32[]{:S(2)}, u32[]{:S(2)}) collective-permute-start(f32[616,128]{1,0:T(8,128)S(1)} %add.276), channel_id=1, source_target_pairs={{1,2},{2,1},{5,6},{6,5},{9,10},{10,9},{13,14},{14,13},{17,18},{18,... | collective-permute-start | bytes 946184 | tf_op jit(solution)/shard_map/ppermute | solution.py:304
  47.1 14.4 %collective-permute-start.11 = (f32[616,128]{1,0:T(8,128)S(1)}, f32[616,128]{1,0:T(8,128)S(1)}, u32[]{:S(2)}, u32[]{:S(2)}) collective-permute-start(f32[616,128]{1,0:T(8,128)S(1)} %select_add_fusion.7), channel_id=1, source_target_pairs={{0,1},{1,0},{2,3},{3,2},{4,5},{5,4},{6,7},{7,6},{8,9},{9,8},{10,11... | collective-permute-start | bytes 946184 | tf_op jit(solution)/shard_map/ppermute | solution.py:304
  52.8 8.7 %collective-permute-start.9 = (f32[616,128]{1,0:T(8,128)S(1)}, f32[616,128]{1,0:T(8,128)S(1)}, u32[]{:S(2)}, u32[]{:S(2)}) collective-permute-start(f32[616,128]{1,0:T(8,128)S(1)} %add.278), channel_id=1, source_target_pairs={{1,2},{2,1},{5,6},{6,5},{9,10},{10,9},{13,14},{14,13},{17,18},{18,... | collective-permute-start | bytes 946184 | tf_op jit(solution)/shard_map/ppermute | solution.py:304
  54.2 13.3 %collective-permute-start.12 = (f32[616,128]{1,0:T(8,128)S(1)}, f32[616,128]{1,0:T(8,128)S(1)}, u32[]{:S(2)}, u32[]{:S(2)}) collective-permute-start(f32[616,128]{1,0:T(8,128)S(1)} %add.280), channel_id=1, source_target_pairs={{1,2},{2,1},{5,6},{6,5},{9,10},{10,9},{13,14},{14,13},{17,18},{18,... | collective-permute-start | bytes 946184 | tf_op jit(solution)/shard_map/ppermute | solution.py:304
  55.1 12.4 %collective-permute-start.13 = (f32[616,128]{1,0:T(8,128)S(1)}, f32[616,128]{1,0:T(8,128)S(1)}, u32[]{:S(2)}, u32[]{:S(2)}) collective-permute-start(f32[616,128]{1,0:T(8,128)S(1)} %select_add_fusion.6), channel_id=1, source_target_pairs={{0,1},{1,0},{2,3},{3,2},{4,5},{5,4},{6,7},{7,6},{8,9},{9,8},{10,11... | collective-permute-start | bytes 946184 | tf_op jit(solution)/shard_map/ppermute | solution.py:304
  62.7 11.0 %collective-permute-start.16 = (f32[616,128]{1,0:T(8,128)S(1)}, f32[616,128]{1,0:T(8,128)S(1)}, u32[]{:S(2)}, u32[]{:S(2)}) collective-permute-start(f32[616,128]{1,0:T(8,128)S(1)} %select_add_fusion.5), channel_id=1, source_target_pairs={{0,1},{1,0},{2,3},{3,2},{4,5},{5,4},{6,7},{7,6},{8,9},{9,8},{10,11... | collective-permute-start | bytes 946184 | tf_op jit(solution)/shard_map/ppermute | solution.py:304
  66.1 8.2 %collective-permute-start.17 = (f32[616,128]{1,0:T(8,128)S(1)}, f32[616,128]{1,0:T(8,128)S(1)}, u32[]{:S(2)}, u32[]{:S(2)}) collective-permute-start(f32[616,128]{1,0:T(8,128)S(1)} %get-tuple-element.237), channel_id=1, source_target_pairs={{1,2},{2,1},{5,6},{6,5},{9,10},{10,9},{13,14},{14,13},{17,18},{18,... | collective-permute-start | bytes 946184 | tf_op jit(solution)/shard_map/ppermute | solution.py:304
  68.1 10.2 %collective-permute-start.14 = (f32[616,128]{1,0:T(8,128)S(1)}, f32[616,128]{1,0:T(8,128)S(1)}, u32[]{:S(2)}, u32[]{:S(2)}) collective-permute-start(f32[616,128]{1,0:T(8,128)S(1)} %select_add_fusion.4), channel_id=1, source_target_pairs={{0,1},{1,0},{2,3},{3,2},{4,5},{5,4},{6,7},{7,6},{8,9},{9,8},{10,11... | collective-permute-start | bytes 946184 | tf_op jit(solution)/shard_map/ppermute | solution.py:304
  72.2 6.7 %collective-permute-start.15 = (f32[616,128]{1,0:T(8,128)S(1)}, f32[616,128]{1,0:T(8,128)S(1)}, u32[]{:S(2)}, u32[]{:S(2)}) collective-permute-start(f32[616,128]{1,0:T(8,128)S(1)} %get-tuple-element.235), channel_id=1, source_target_pairs={{1,2},{2,1},{5,6},{6,5},{9,10},{10,9},{13,14},{14,13},{17,18},{18,... | collective-permute-start | bytes 946184 | tf_op jit(solution)/shard_map/ppermute | solution.py:304
  74.3 13.6 %collective-permute-start.20 = (f32[616,128]{1,0:T(8,128)S(1)}, f32[616,128]{1,0:T(8,128)S(1)}, u32[]{:S(2)}, u32[]{:S(2)}) collective-permute-start(f32[616,128]{1,0:T(8,128)S(1)} %get-tuple-element.246), channel_id=1, source_target_pairs={{1,2},{2,1},{5,6},{6,5},{9,10},{10,9},{13,14},{14,13},{17,18},{18,... | collective-permute-start | bytes 946184 | tf_op jit(solution)/shard_map/ppermute | solution.py:304
  75.0 12.4 %collective-permute-start.21 = (f32[616,128]{1,0:T(8,128)S(1)}, f32[616,128]{1,0:T(8,128)S(1)}, u32[]{:S(2)}, u32[]{:S(2)}) collective-permute-start(f32[616,128]{1,0:T(8,128)S(1)} %add.293), channel_id=1, source_target_pairs={{1,0},{2,3},{5,4},{6,7},{9,8},{10,11},{13,12},{14,15},{17,16},{18,... | collective-permute-start | bytes 946184 | tf_op jit(solution)/shard_map/ppermute | solution.py:304
  79.0 15.1 %collective-permute-start.19 = (f32[616,128]{1,0:T(8,128)S(1)}, f32[616,128]{1,0:T(8,128)S(1)}, u32[]{:S(2)}, u32[]{:S(2)}) collective-permute-start(f32[616,128]{1,0:T(8,128)S(1)} %add.289), channel_id=1, source_target_pairs={{1,0},{2,3},{5,4},{6,7},{9,8},{10,11},{13,12},{14,15},{17,16},{18,... | collective-permute-start | bytes 946184 | tf_op jit(solution)/shard_map/ppermute | solution.py:304
  80.3 14.3 %collective-permute-start.18 = (f32[616,128]{1,0:T(8,128)S(1)}, f32[616,128]{1,0:T(8,128)S(1)}, u32[]{:S(2)}, u32[]{:S(2)}) collective-permute-start(f32[616,128]{1,0:T(8,128)S(1)} %get-tuple-element.244), channel_id=1, source_target_pairs={{1,2},{2,1},{5,6},{6,5},{9,10},{10,9},{13,14},{14,13},{17,18},{18,... | collective-permute-start | bytes 946184 | tf_op jit(solution)/shard_map/ppermute | solution.py:304
  87.9 12.9 %collective-permute-start.23 = (f32[616,128]{1,0:T(8,128)S(1)}, f32[616,128]{1,0:T(8,128)S(1)}, u32[]{:S(2)}, u32[]{:S(2)}) collective-permute-start(f32[616,128]{1,0:T(8,128)S(1)} %add.299), channel_id=1, source_target_pairs={{1,0},{2,3},{5,4},{6,7},{9,8},{10,11},{13,12},{14,15},{17,16},{18,... | collective-permute-start | bytes 946184 | tf_op jit(solution)/shard_map/ppermute | solution.py:304
  94.7 9.6 %collective-permute-start.22 = (f32[616,128]{1,0:T(8,128)S(1)}, f32[616,128]{1,0:T(8,128)S(1)}, u32[]{:S(2)}, u32[]{:S(2)}) collective-permute-start(f32[616,128]{1,0:T(8,128)S(1)} %add.296), channel_id=1, source_target_pairs={{1,0},{2,3},{5,4},{6,7},{9,8},{10,11},{13,12},{14,15},{17,16},{18,... | collective-permute-start | bytes 946184 | tf_op jit(solution)/shard_map/ppermute | solution.py:304
  106.1 3.7 %collective-permute-start.26 = (f32[24,128]{1,0:T(8,128)S(1)}, f32[24,128]{1,0:T(8,128)S(1)}, u32[]{:S(2)}, u32[]{:S(2)}) collective-permute-start(f32[24,128]{1,0:T(8,128)S(1)} %add.306), channel_id=1, source_target_pairs={{0,16},{4,20},{8,24},{12,28},{16,0},{20,4},{24,8},{28,12},{1,17},{... | collective-permute-start | bytes 36872 | tf_op jit(solution)/shard_map/ppermute | solution.py:240
  107.9 4.6 %collective-permute-start.27 = (f32[24,128]{1,0:T(8,128)S(1)}, f32[24,128]{1,0:T(8,128)S(1)}, u32[]{:S(2)}, u32[]{:S(2)}) collective-permute-start(f32[24,128]{1,0:T(8,128)S(1)} %add.306), channel_id=1, source_target_pairs={{0,24},{4,28},{8,16},{12,20},{16,8},{20,12},{24,0},{28,4},{1,25},{... | collective-permute-start | bytes 36872 | tf_op jit(solution)/shard_map/ppermute | solution.py:240
  113.4 9.3 %collective-permute-start.28 = (f32[616,128]{1,0:T(8,128)S(1)}, f32[616,128]{1,0:T(8,128)S(1)}, u32[]{:S(2)}, u32[]{:S(2)}) collective-permute-start(f32[616,128]{1,0:T(8,128)S(1)} %back_products.24), channel_id=1, source_target_pairs={{0,1},{3,2},{4,5},{7,6},{8,9},{11,10},{12,13},{15,14},{16,17},{19,... | collective-permute-start | bytes 946184 | tf_op jit(solution)/shard_map/ppermute | solution.py:304
  116.7 13.6 %collective-permute-start.30 = (f32[616,128]{1,0:T(8,128)S(1)}, f32[616,128]{1,0:T(8,128)S(1)}, u32[]{:S(2)}, u32[]{:S(2)}) collective-permute-start(f32[616,128]{1,0:T(8,128)S(1)} %back_products.25), channel_id=1, source_target_pairs={{0,1},{3,2},{4,5},{7,6},{8,9},{11,10},{12,13},{15,14},{16,17},{19,... | collective-permute-start | bytes 946184 | tf_op jit(solution)/shard_map/ppermute | solution.py:304
  122.7 13.0 %collective-permute-start.29 = (f32[616,128]{1,0:T(8,128)S(1)}, f32[616,128]{1,0:T(8,128)S(1)}, u32[]{:S(2)}, u32[]{:S(2)}) collective-permute-start(f32[616,128]{1,0:T(8,128)S(1)} %add.311), channel_id=1, source_target_pairs={{1,2},{2,1},{5,6},{6,5},{9,10},{10,9},{13,14},{14,13},{17,18},{18,... | collective-permute-start | bytes 946184 | tf_op jit(solution)/shard_map/ppermute | solution.py:304
  123.5 13.1 %collective-permute-start.32 = (f32[616,128]{1,0:T(8,128)S(1)}, f32[616,128]{1,0:T(8,128)S(1)}, u32[]{:S(2)}, u32[]{:S(2)}) collective-permute-start(f32[616,128]{1,0:T(8,128)S(1)} %back_products.26), channel_id=1, source_target_pairs={{0,1},{3,2},{4,5},{7,6},{8,9},{11,10},{12,13},{15,14},{16,17},{19,... | collective-permute-start | bytes 946184 | tf_op jit(solution)/shard_map/ppermute | solution.py:304
  130.4 8.3 %collective-permute-start.31 = (f32[616,128]{1,0:T(8,128)S(1)}, f32[616,128]{1,0:T(8,128)S(1)}, u32[]{:S(2)}, u32[]{:S(2)}) collective-permute-start(f32[616,128]{1,0:T(8,128)S(1)} %add.313), channel_id=1, source_target_pairs={{1,2},{2,1},{5,6},{6,5},{9,10},{10,9},{13,14},{14,13},{17,18},{18,... | collective-permute-start | bytes 946184 | tf_op jit(solution)/shard_map/ppermute | solution.py:304
  131.0 12.6 %collective-permute-start.34 = (f32[616,128]{1,0:T(8,128)S(1)}, f32[616,128]{1,0:T(8,128)S(1)}, u32[]{:S(2)}, u32[]{:S(2)}) collective-permute-start(f32[616,128]{1,0:T(8,128)S(1)} %back_products.27), channel_id=1, source_target_pairs={{0,1},{3,2},{4,5},{7,6},{8,9},{11,10},{12,13},{15,14},{16,17},{19,... | collective-permute-start | bytes 946184 | tf_op jit(solution)/shard_map/ppermute | solution.py:304
  135.8 14.6 %collective-permute-start.35 = (f32[616,128]{1,0:T(8,128)S(1)}, f32[616,128]{1,0:T(8,128)S(1)}, u32[]{:S(2)}, u32[]{:S(2)}) collective-permute-start(f32[616,128]{1,0:T(8,128)S(1)} %select_add_fusion.3), channel_id=1, source_target_pairs={{0,1},{1,0},{2,3},{3,2},{4,5},{5,4},{6,7},{7,6},{8,9},{9,8},{10,11... | collective-permute-start | bytes 946184 | tf_op jit(solution)/shard_map/ppermute | solution.py:304
  138.0 12.5 %collective-permute-start.33 = (f32[616,128]{1,0:T(8,128)S(1)}, f32[616,128]{1,0:T(8,128)S(1)}, u32[]{:S(2)}, u32[]{:S(2)}) collective-permute-start(f32[616,128]{1,0:T(8,128)S(1)} %add.315), channel_id=1, source_target_pairs={{1,2},{2,1},{5,6},{6,5},{9,10},{10,9},{13,14},{14,13},{17,18},{18,... | collective-permute-start | bytes 946184 | tf_op jit(solution)/shard_map/ppermute | solution.py:304
  143.6 13.5 %collective-permute-start.37 = (f32[616,128]{1,0:T(8,128)S(1)}, f32[616,128]{1,0:T(8,128)S(1)}, u32[]{:S(2)}, u32[]{:S(2)}) collective-permute-start(f32[616,128]{1,0:T(8,128)S(1)} %select_add_fusion.2), channel_id=1, source_target_pairs={{0,1},{1,0},{2,3},{3,2},{4,5},{5,4},{6,7},{7,6},{8,9},{9,8},{10,11... | collective-permute-start | bytes 946184 | tf_op jit(solution)/shard_map/ppermute | solution.py:304
  146.2 11.1 %collective-permute-start.36 = (f32[616,128]{1,0:T(8,128)S(1)}, f32[616,128]{1,0:T(8,128)S(1)}, u32[]{:S(2)}, u32[]{:S(2)}) collective-permute-start(f32[616,128]{1,0:T(8,128)S(1)} %add.317), channel_id=1, source_target_pairs={{1,2},{2,1},{5,6},{6,5},{9,10},{10,9},{13,14},{14,13},{17,18},{18,... | collective-permute-start | bytes 946184 | tf_op jit(solution)/shard_map/ppermute | solution.py:304
  151.7 12.2 %collective-permute-start.40 = (f32[616,128]{1,0:T(8,128)S(1)}, f32[616,128]{1,0:T(8,128)S(1)}, u32[]{:S(2)}, u32[]{:S(2)}) collective-permute-start(f32[616,128]{1,0:T(8,128)S(1)} %select_add_fusion.1), channel_id=1, source_target_pairs={{0,1},{1,0},{2,3},{3,2},{4,5},{5,4},{6,7},{7,6},{8,9},{9,8},{10,11... | collective-permute-start | bytes 946184 | tf_op jit(solution)/shard_map/ppermute | solution.py:304
  154.8 9.6 %collective-permute-start.41 = (f32[616,128]{1,0:T(8,128)S(1)}, f32[616,128]{1,0:T(8,128)S(1)}, u32[]{:S(2)}, u32[]{:S(2)}) collective-permute-start(f32[616,128]{1,0:T(8,128)S(1)} %get-tuple-element.315), channel_id=1, source_target_pairs={{1,2},{2,1},{5,6},{6,5},{9,10},{10,9},{13,14},{14,13},{17,18},{18,... | collective-permute-start | bytes 946184 | tf_op jit(solution)/shard_map/ppermute | solution.py:304
  157.8 10.2 %collective-permute-start.38 = (f32[616,128]{1,0:T(8,128)S(1)}, f32[616,128]{1,0:T(8,128)S(1)}, u32[]{:S(2)}, u32[]{:S(2)}) collective-permute-start(f32[616,128]{1,0:T(8,128)S(1)} %select_add_fusion), channel_id=1, source_target_pairs={{0,1},{1,0},{2,3},{3,2},{4,5},{5,4},{6,7},{7,6},{8,9},{9,8},{10,11... | collective-permute-start | bytes 946184 | tf_op jit(solution)/shard_map/ppermute | solution.py:304
  160.3 8.2 %collective-permute-start.39 = (f32[616,128]{1,0:T(8,128)S(1)}, f32[616,128]{1,0:T(8,128)S(1)}, u32[]{:S(2)}, u32[]{:S(2)}) collective-permute-start(f32[616,128]{1,0:T(8,128)S(1)} %get-tuple-element.312), channel_id=1, source_target_pairs={{1,2},{2,1},{5,6},{6,5},{9,10},{10,9},{13,14},{14,13},{17,18},{18,... | collective-permute-start | bytes 946184 | tf_op jit(solution)/shard_map/ppermute | solution.py:304
  164.5 15.8 %collective-permute-start.44 = (f32[616,128]{1,0:T(8,128)S(1)}, f32[616,128]{1,0:T(8,128)S(1)}, u32[]{:S(2)}, u32[]{:S(2)}) collective-permute-start(f32[616,128]{1,0:T(8,128)S(1)} %get-tuple-element.326), channel_id=1, source_target_pairs={{1,2},{2,1},{5,6},{6,5},{9,10},{10,9},{13,14},{14,13},{17,18},{18,... | collective-permute-start | bytes 946184 | tf_op jit(solution)/shard_map/ppermute | solution.py:304
  165.2 14.6 %collective-permute-start.45 = (f32[616,128]{1,0:T(8,128)S(1)}, f32[616,128]{1,0:T(8,128)S(1)}, u32[]{:S(2)}, u32[]{:S(2)}) collective-permute-start(f32[616,128]{1,0:T(8,128)S(1)} %add.332), channel_id=1, source_target_pairs={{1,0},{2,3},{5,4},{6,7},{9,8},{10,11},{13,12},{14,15},{17,16},{18,... | collective-permute-start | bytes 946184 | tf_op jit(solution)/shard_map/ppermute | solution.py:304
  168.5 18.5 %collective-permute-start.42 = (f32[616,128]{1,0:T(8,128)S(1)}, f32[616,128]{1,0:T(8,128)S(1)}, u32[]{:S(2)}, u32[]{:S(2)}) collective-permute-start(f32[616,128]{1,0:T(8,128)S(1)} %get-tuple-element.323), channel_id=1, source_target_pairs={{1,2},{2,1},{5,6},{6,5},{9,10},{10,9},{13,14},{14,13},{17,18},{18,... | collective-permute-start | bytes 946184 | tf_op jit(solution)/shard_map/ppermute | solution.py:304
  169.2 17.3 %collective-permute-start.43 = (f32[616,128]{1,0:T(8,128)S(1)}, f32[616,128]{1,0:T(8,128)S(1)}, u32[]{:S(2)}, u32[]{:S(2)}) collective-permute-start(f32[616,128]{1,0:T(8,128)S(1)} %add.328), channel_id=1, source_target_pairs={{1,0},{2,3},{5,4},{6,7},{9,8},{10,11},{13,12},{14,15},{17,16},{18,... | collective-permute-start | bytes 946184 | tf_op jit(solution)/shard_map/ppermute | solution.py:304
  180.4 12.9 %collective-permute-start.47 = (f32[616,128]{1,0:T(8,128)S(1)}, f32[616,128]{1,0:T(8,128)S(1)}, u32[]{:S(2)}, u32[]{:S(2)}) collective-permute-start(f32[616,128]{1,0:T(8,128)S(1)} %add.338), channel_id=1, source_target_pairs={{1,0},{2,3},{5,4},{6,7},{9,8},{10,11},{13,12},{14,15},{17,16},{18,... | collective-permute-start | bytes 946184 | tf_op jit(solution)/shard_map/ppermute | solution.py:304
  187.1 9.8 %collective-permute-start.46 = (f32[616,128]{1,0:T(8,128)S(1)}, f32[616,128]{1,0:T(8,128)S(1)}, u32[]{:S(2)}, u32[]{:S(2)}) collective-permute-start(f32[616,128]{1,0:T(8,128)S(1)} %add.335), channel_id=1, source_target_pairs={{1,0},{2,3},{5,4},{6,7},{9,8},{10,11},{13,12},{14,15},{17,16},{18,... | collective-permute-start | bytes 946184 | tf_op jit(solution)/shard_map/ppermute | solution.py:304
  199.7 4.6 %collective-permute-start.51 = (f32[24,128]{1,0:T(8,128)S(1)}, f32[24,128]{1,0:T(8,128)S(1)}, u32[]{:S(2)}, u32[]{:S(2)}) collective-permute-start(f32[24,128]{1,0:T(8,128)S(1)} %add.345), channel_id=1, source_target_pairs={{0,24},{4,28},{8,16},{12,20},{16,8},{20,12},{24,0},{28,4},{1,25},{... | collective-permute-start | bytes 36872 | tf_op jit(solution)/shard_map/ppermute | solution.py:240
  204.9 5.2 %collective-permute-start.53 = (f32[1,128]{1,0:T(1,128)S(1)}, f32[1,128]{1,0:T(1,128)S(1)}, u32[]{:S(2)}, u32[]{:S(2)}) collective-permute-start(f32[1,128]{1,0:T(1,128)S(1)} %bitcast.40), channel_id=1, source_target_pairs={{0,2},{1,3},{2,0},{3,1},{4,6},{5,7},{6,4},{7,5},{8,10},{9,11},{10,... | collective-permute-start | bytes 1544 | tf_op jit(solution)/shard_map/ppermute | solution.py:240
  205.4 5.3 %collective-permute-start.54 = (f32[1,128]{1,0:T(1,128)S(1)}, f32[1,128]{1,0:T(1,128)S(1)}, u32[]{:S(2)}, u32[]{:S(2)}) collective-permute-start(f32[1,128]{1,0:T(1,128)S(1)} %bitcast.41), channel_id=1, source_target_pairs={{0,3},{1,2},{2,1},{3,0},{4,7},{5,6},{6,5},{7,4},{8,11},{9,10},{10,... | collective-permute-start | bytes 1544 | tf_op jit(solution)/shard_map/ppermute | solution.py:240
  (16 other events, 89.7 us)

commit v4 on v3

--- a/solution.py
+++ b/solution.py
@@ -247,7 +247,7 @@
     return value, tuple(beside)
 
 
-def chain(chunks, produce, consume, state, gate):
+def chain(chunks, produce, consume, state, gate, eager):
     count = lax.axis_size("walker")
     me = lax.axis_index("walker")
     gaps = (2, 2)
@@ -309,7 +309,10 @@
     steps = chunks + max(late)
     for step in range(steps):
         gate, state = exchange(0, step, step - gaps[1], gate, state)
-        if step + 1 < chunks:
+        if step == 0 and eager:
+            made += [produce(chunk, gate) for chunk in range(1, chunks)]
+            *made[1:], gate = lax.optimization_barrier((*made[1:], gate))
+        if len(made) < chunks and not eager:
             made.append(produce(step + 1, gate))
             made[-1], gate, *state = lax.optimization_barrier((made[-1], gate, *state))
             state = tuple(state)
@@ -349,7 +352,7 @@
             return back_call(derivs, gate, chunk, part)
 
         state = (jnp.zeros((24, LANES), jnp.float32),)
-        (stats,) = chain(chunks, produce, consume, state, vals)
+        (stats,) = chain(chunks, produce, consume, state, vals, isinstance(residual, list))
         step = step_length(norm, first[0][part : part + 1], rows_all, dir_sq)
         return fresh, step, stats
 
@@ -372,6 +375,7 @@
     stats, (whole1, whole2, coefs) = small_sum(stats, "param", (whole1, whole2, coefs))
     share = lax.axis_index("walker").astype(jnp.int32).reshape(1)
     base, direction1, res = share_call(share, grad, whole1, whole2, coefs, rows // walkers)
+    stats, base, direction1, res = lax.optimization_barrier((stats, base, direction1, res))
 
     norm2, cross2 = stats[8:9], stats[16:17]
     beta2 = norm2 / norm1

time: 213 us -> 212 us (level)
  transfers between devices with their start and end apart: 55 -> 55, of which waited for: 32 -> 33; matrix products, arithmetic and copies ran while one was open for 2% -> 2% of each run, Pallas kernels for 7% -> 7%
where the time goes in v4:
time: 212 us; the launch traced here: 211 us
  starting transfers between devices  87.6 us (41%)
  waiting for transfers between devices  80.4 us (38%)
  Pallas kernels  26.5 us (12%)
  local copies, waits for them, and re-layouts  10.9 us (5%)
  other arithmetic  4.47 us (2%)
    ppermute x40, starting transfers between devices, exchange(): got[parity].append(lax.ppermute(own, 'walker', pairs))  72.2 us
    ppermute x40, waiting for transfers between devices, exchange(): got[parity].append(lax.ppermute(own, 'walker', pairs))  67.6 us
    ppermute x15, starting transfers between devices, small_sum(): lax.ppermute(value, axis, [(i, i ^ bit * j) for i in range(size)])  15.4 us
    ppermute x15, waiting for transfers between devices, small_sum(): lax.ppermute(value, axis, [(i, i ^ bit * j) for i in range(size)])  12.8 us
    unnamed x30, local copies, waits for them, and re-layouts  10.7 us
    pallas_call x16, Pallas kernels, back_call(): pl.pallas_call(functools.partial(back_kernel, chunk * rows), in_specs=[vm...  9.59 us
    pallas_call x1, Pallas kernels, start_call(): pl.pallas_call(functools.partial(start_kernel, copies), in_specs=[hbm(),...  8.09 us
    pallas_call x16, Pallas kernels, advance_call(): pl.pallas_call(functools.partial(advance_kernel, chunk * rows, rows_all,...  7.18 us
  transfers between devices with their start and end apart: 55, of which 33 were waited for; matrix products, arithmetic and copies ran while one was open for 2% of the time, Pallas kernels for 7%

profile of v4, /device:TPU:0, one launch (start us, length us, event | category | flops | bytes accessed | tf_op | source)
XLA Modules:
  0.0 210.8 jit_solution(14200638248482017639)
XLA Ops:
  0.0 8.1 %start_products.1 = (f32[24,128]{1,0:T(8,128)S(1)}, f32[8,622592]{1,0:T(8,128)S(1)}) custom-call(f32[8,622592]{1,0:T(8,128)} %derivs_hbm.1, f32[4864,128]{1,0:T(8,128)} %bitcast.11), custom_call_target="tpu_custom_call" | custom-call | tf_op jit(solution)/shard_map/start_products/pallas_call | solution.py:119
  9.5 2.9 %collective-permute-start.2 = (f32[24,128]{1,0:T(8,128)S(1)}, f32[24,128]{1,0:T(8,128)S(1)}, u32[]{:S(2)}, u32[]{:S(2)}) collective-permute-start(f32[24,128]{1,0:T(8,128)S(1)} %add.270), channel_id=1, source_target_pairs={{0,16},{4,20},{8,24},{12,28},{16,0},{20,4},{24,8},{28,12},{1,17},{... | collective-permute-start | bytes 36872 | tf_op jit(solution)/shard_map/ppermute | solution.py:240
  12.3 1.4 collective-permute-start.3
  14.0 2.9 %collective-permute-done.3 = f32[24,128]{1,0:T(8,128)S(1)} collective-permute-done((f32[24,128]{1,0:T(8,128)S(1)}, f32[24,128]{1,0:T(8,128)S(1)}, u32[]{:S(2)}, u32[]{:S(2)}) %collective-permute-start.3) | collective-permute-done | bytes 12320 | tf_op jit(solution)/shard_map/ppermute | solution.py:240
  18.1 3.5 %collective-permute-start.4 = (f32[616,128]{1,0:T(8,128)S(1)}, f32[616,128]{1,0:T(8,128)S(1)}, u32[]{:S(2)}, u32[]{:S(2)}) collective-permute-start(f32[616,128]{1,0:T(8,128)S(1)} %back_products.16), channel_id=1, source_target_pairs={{0,1},{3,2},{4,5},{7,6},{8,9},{11,10},{12,13},{15,14},{16,17},{19,... | collective-permute-start | bytes 946184 | tf_op jit(solution)/shard_map/ppermute | solution.py:304
  23.4 1.3 collective-permute-start.6
  24.7 4.7 %collective-permute-done.4 = f32[616,128]{1,0:T(8,128)S(1)} collective-permute-done((f32[616,128]{1,0:T(8,128)S(1)}, f32[616,128]{1,0:T(8,128)S(1)}, u32[]{:S(2)}, u32[]{:S(2)}) %collective-permute-start.4) | collective-permute-done | bytes 315424 | tf_op jit(solution)/shard_map/ppermute | solution.py:304
  30.3 7.2 %collective-permute-start.8 = (f32[616,128]{1,0:T(8,128)S(1)}, f32[616,128]{1,0:T(8,128)S(1)}, u32[]{:S(2)}, u32[]{:S(2)}) collective-permute-start(f32[616,128]{1,0:T(8,128)S(1)} %back_products.18), channel_id=1, source_target_pairs={{0,1},{3,2},{4,5},{7,6},{8,9},{11,10},{12,13},{15,14},{16,17},{19,... | collective-permute-start | bytes 946184 | tf_op jit(solution)/shard_map/ppermute | solution.py:304
  37.5 1.3 collective-permute-start.10
  38.9 6.7 %copy-done.1 = f32[8,622592]{1,0:T(8,128)S(1)} copy-done((f32[8,622592]{1,0:T(8,128)S(1)}, f32[8,622592]{1,0:T(8,128)}, u32[]{:S(2)}) %copy-start.1) | copy-done | bytes 19922968
  47.1 1.4 collective-permute-start.11
  48.6 3.6 %copy-done.2 = f32[8,622592]{1,0:T(8,128)S(1)} copy-done((f32[8,622592]{1,0:T(8,128)S(1)}, f32[8,622592]{1,0:T(8,128)}, u32[]{:S(2)}) %copy-start.2) | copy-done | bytes 19922968
  55.1 6.4 %collective-permute-start.13 = (f32[616,128]{1,0:T(8,128)S(1)}, f32[616,128]{1,0:T(8,128)S(1)}, u32[]{:S(2)}, u32[]{:S(2)}) collective-permute-start(f32[616,128]{1,0:T(8,128)S(1)} %select_add_fusion.6), channel_id=1, source_target_pairs={{0,1},{1,0},{2,3},{3,2},{4,5},{5,4},{6,7},{7,6},{8,9},{9,8},{10,11... | collective-permute-start | bytes 946184 | tf_op jit(solution)/shard_map/ppermute | solution.py:304
  62.7 3.4 %collective-permute-start.16 = (f32[616,128]{1,0:T(8,128)S(1)}, f32[616,128]{1,0:T(8,128)S(1)}, u32[]{:S(2)}, u32[]{:S(2)}) collective-permute-start(f32[616,128]{1,0:T(8,128)S(1)} %select_add_fusion.5), channel_id=1, source_target_pairs={{0,1},{1,0},{2,3},{3,2},{4,5},{5,4},{6,7},{7,6},{8,9},{9,8},{10,11... | collective-permute-start | bytes 946184 | tf_op jit(solution)/shard_map/ppermute | solution.py:304
  68.1 4.1 %collective-permute-start.14 = (f32[616,128]{1,0:T(8,128)S(1)}, f32[616,128]{1,0:T(8,128)S(1)}, u32[]{:S(2)}, u32[]{:S(2)}) collective-permute-start(f32[616,128]{1,0:T(8,128)S(1)} %select_add_fusion.4), channel_id=1, source_target_pairs={{0,1},{1,0},{2,3},{3,2},{4,5},{5,4},{6,7},{7,6},{8,9},{9,8},{10,11... | collective-permute-start | bytes 946184 | tf_op jit(solution)/shard_map/ppermute | solution.py:304
  75.0 1.3 collective-permute-start.21
  76.3 2.1 collective-permute-done.14
  81.0 6.4 %collective-permute-done.21 = f32[616,128]{1,0:T(8,128)S(1)} collective-permute-done((f32[616,128]{1,0:T(8,128)S(1)}, f32[616,128]{1,0:T(8,128)S(1)}, u32[]{:S(2)}, u32[]{:S(2)}) %collective-permute-start.21) | collective-permute-done | bytes 315424 | tf_op jit(solution)/shard_map/ppermute | solution.py:304
  87.9 1.3 collective-permute-start.23
  89.2 4.9 %collective-permute-done.19 = f32[616,128]{1,0:T(8,128)S(1)} collective-permute-done((f32[616,128]{1,0:T(8,128)S(1)}, f32[616,128]{1,0:T(8,128)S(1)}, u32[]{:S(2)}, u32[]{:S(2)}) %collective-permute-start.19) | collective-permute-done | bytes 315424 | tf_op jit(solution)/shard_map/ppermute | solution.py:304
  94.7 1.3 collective-permute-start.22
  96.0 4.9 %collective-permute-done.23 = f32[616,128]{1,0:T(8,128)S(1)} collective-permute-done((f32[616,128]{1,0:T(8,128)S(1)}, f32[616,128]{1,0:T(8,128)S(1)}, u32[]{:S(2)}, u32[]{:S(2)}) %collective-permute-start.23) | collective-permute-done | bytes 315424 | tf_op jit(solution)/shard_map/ppermute | solution.py:304
  101.4 2.9 %collective-permute-done.22 = f32[616,128]{1,0:T(8,128)S(1)} collective-permute-done((f32[616,128]{1,0:T(8,128)S(1)}, f32[616,128]{1,0:T(8,128)S(1)}, u32[]{:S(2)}, u32[]{:S(2)}) %collective-permute-start.22) | collective-permute-done | bytes 315424 | tf_op jit(solution)/shard_map/ppermute | solution.py:304
  106.1 1.8 collective-permute-start.26
  109.8 2.7 %collective-permute-done.27 = f32[24,128]{1,0:T(8,128)S(1)} collective-permute-done((f32[24,128]{1,0:T(8,128)S(1)}, f32[24,128]{1,0:T(8,128)S(1)}, u32[]{:S(2)}, u32[]{:S(2)}) %collective-permute-start.27) | collective-permute-done | bytes 12320 | tf_op jit(solution)/shard_map/ppermute | solution.py:240
  113.4 1.5 collective-permute-start.28
  119.2 1.3 collective-permute-start.30
  122.1 6.4 %collective-permute-start.32 = (f32[616,128]{1,0:T(8,128)S(1)}, f32[616,128]{1,0:T(8,128)S(1)}, u32[]{:S(2)}, u32[]{:S(2)}) collective-permute-start(f32[616,128]{1,0:T(8,128)S(1)} %back_products.26), channel_id=1, source_target_pairs={{0,1},{3,2},{4,5},{7,6},{8,9},{11,10},{12,13},{15,14},{16,17},{19,... | collective-permute-start | bytes 946184 | tf_op jit(solution)/shard_map/ppermute | solution.py:304
  128.6 4.2 %collective-permute-start.29 = (f32[616,128]{1,0:T(8,128)S(1)}, f32[616,128]{1,0:T(8,128)S(1)}, u32[]{:S(2)}, u32[]{:S(2)}) collective-permute-start(f32[616,128]{1,0:T(8,128)S(1)} %back_products.27), channel_id=1, source_target_pairs={{0,1},{3,2},{4,5},{7,6},{8,9},{11,10},{12,13},{15,14},{16,17},{19,... | collective-permute-start | bytes 946184 | tf_op jit(solution)/shard_map/ppermute | solution.py:304
  134.8 1.7 collective-permute-done.32
  137.2 6.0 %collective-permute-done.29 = f32[616,128]{1,0:T(8,128)S(1)} collective-permute-done((f32[616,128]{1,0:T(8,128)S(1)}, f32[616,128]{1,0:T(8,128)S(1)}, u32[]{:S(2)}, u32[]{:S(2)}) %collective-permute-start.29) | collective-permute-done | bytes 315424 | tf_op jit(solution)/shard_map/ppermute | solution.py:304
  143.2 2.5 %collective-permute-start.35 = (f32[616,128]{1,0:T(8,128)S(1)}, f32[616,128]{1,0:T(8,128)S(1)}, u32[]{:S(2)}, u32[]{:S(2)}) collective-permute-start(f32[616,128]{1,0:T(8,128)S(1)} %select_add_fusion.2), channel_id=1, source_target_pairs={{0,1},{1,0},{2,3},{3,2},{4,5},{5,4},{6,7},{7,6},{8,9},{9,8},{10,11... | collective-permute-start | bytes 946184 | tf_op jit(solution)/shard_map/ppermute | solution.py:304
  146.5 3.5 %collective-permute-done.36 = f32[616,128]{1,0:T(8,128)S(1)} collective-permute-done((f32[616,128]{1,0:T(8,128)S(1)}, f32[616,128]{1,0:T(8,128)S(1)}, u32[]{:S(2)}, u32[]{:S(2)}) %collective-permute-start.36) | collective-permute-done | bytes 315424 | tf_op jit(solution)/shard_map/ppermute | solution.py:304
  151.2 2.5 %collective-permute-start.40 = (f32[616,128]{1,0:T(8,128)S(1)}, f32[616,128]{1,0:T(8,128)S(1)}, u32[]{:S(2)}, u32[]{:S(2)}) collective-permute-start(f32[616,128]{1,0:T(8,128)S(1)} %select_add_fusion), channel_id=1, source_target_pairs={{0,1},{1,0},{2,3},{3,2},{4,5},{5,4},{6,7},{7,6},{8,9},{9,8},{10,11... | collective-permute-start | bytes 946184 | tf_op jit(solution)/shard_map/ppermute | solution.py:304
  154.5 2.3 %collective-permute-done.35 = f32[616,128]{1,0:T(8,128)S(1)} collective-permute-done((f32[616,128]{1,0:T(8,128)S(1)}, f32[616,128]{1,0:T(8,128)S(1)}, u32[]{:S(2)}, u32[]{:S(2)}) %collective-permute-start.35) | collective-permute-done | bytes 315424 | tf_op jit(solution)/shard_map/ppermute | solution.py:304
  157.3 2.5 %collective-permute-start.38 = (f32[616,128]{1,0:T(8,128)S(1)}, f32[616,128]{1,0:T(8,128)S(1)}, u32[]{:S(2)}, u32[]{:S(2)}) collective-permute-start(f32[616,128]{1,0:T(8,128)S(1)} %select_add_fusion.3), channel_id=1, source_target_pairs={{0,1},{1,0},{2,3},{3,2},{4,5},{5,4},{6,7},{7,6},{8,9},{9,8},{10,11... | collective-permute-start | bytes 946184 | tf_op jit(solution)/shard_map/ppermute | solution.py:304
  160.6 2.9 %collective-permute-done.40 = f32[616,128]{1,0:T(8,128)S(1)} collective-permute-done((f32[616,128]{1,0:T(8,128)S(1)}, f32[616,128]{1,0:T(8,128)S(1)}, u32[]{:S(2)}, u32[]{:S(2)}) %collective-permute-start.40) | collective-permute-done | bytes 315424 | tf_op jit(solution)/shard_map/ppermute | solution.py:304
  164.8 1.3 collective-permute-start.45
  166.1 1.5 collective-permute-done.38
  168.9 1.3 collective-permute-start.43
  170.2 9.1 %collective-permute-done.45 = f32[616,128]{1,0:T(8,128)S(1)} collective-permute-done((f32[616,128]{1,0:T(8,128)S(1)}, f32[616,128]{1,0:T(8,128)S(1)}, u32[]{:S(2)}, u32[]{:S(2)}) %collective-permute-start.45) | collective-permute-done | bytes 315424 | tf_op jit(solution)/shard_map/ppermute | solution.py:304
  181.2 4.9 %collective-permute-done.43 = f32[616,128]{1,0:T(8,128)S(1)} collective-permute-done((f32[616,128]{1,0:T(8,128)S(1)}, f32[616,128]{1,0:T(8,128)S(1)}, u32[]{:S(2)}, u32[]{:S(2)}) %collective-permute-start.43) | collective-permute-done | bytes 315424 | tf_op jit(solution)/shard_map/ppermute | solution.py:304
  188.1 4.5 %collective-permute-done.47 = f32[616,128]{1,0:T(8,128)S(1)} collective-permute-done((f32[616,128]{1,0:T(8,128)S(1)}, f32[616,128]{1,0:T(8,128)S(1)}, u32[]{:S(2)}, u32[]{:S(2)}) %collective-permute-start.47) | collective-permute-done | bytes 315424 | tf_op jit(solution)/shard_map/ppermute | solution.py:304
  192.5 3.4 %collective-permute-done.46 = f32[616,128]{1,0:T(8,128)S(1)} collective-permute-done((f32[616,128]{1,0:T(8,128)S(1)}, f32[616,128]{1,0:T(8,128)S(1)}, u32[]{:S(2)}, u32[]{:S(2)}) %collective-permute-start.46) | collective-permute-done | bytes 315424 | tf_op jit(solution)/shard_map/ppermute | solution.py:304
  199.2 1.3 collective-permute-start.51
  201.7 1.6 share_parts.1
  204.3 2.0 collective-permute-start.54
  206.3 1.5 collective-permute-start.52
  (189 shorter events, 52.0 us)
Async XLA Ops:
  9.5 4.5 %collective-permute-start.2 = (f32[24,128]{1,0:T(8,128)S(1)}, f32[24,128]{1,0:T(8,128)S(1)}, u32[]{:S(2)}, u32[]{:S(2)}) collective-permute-start(f32[24,128]{1,0:T(8,128)S(1)} %add.270), channel_id=1, source_target_pairs={{0,16},{4,20},{8,24},{12,28},{16,0},{20,4},{24,8},{28,12},{1,17},{... | collective-permute-start | bytes 36872 | tf_op jit(solution)/shard_map/ppermute | solution.py:240
  12.3 4.6 %collective-permute-start.3 = (f32[24,128]{1,0:T(8,128)S(1)}, f32[24,128]{1,0:T(8,128)S(1)}, u32[]{:S(2)}, u32[]{:S(2)}) collective-permute-start(f32[24,128]{1,0:T(8,128)S(1)} %add.270), channel_id=1, source_target_pairs={{0,24},{4,28},{8,16},{12,20},{16,8},{20,12},{24,0},{28,4},{1,25},{... | collective-permute-start | bytes 36872 | tf_op jit(solution)/shard_map/ppermute | solution.py:240
  18.1 11.4 %collective-permute-start.4 = (f32[616,128]{1,0:T(8,128)S(1)}, f32[616,128]{1,0:T(8,128)S(1)}, u32[]{:S(2)}, u32[]{:S(2)}) collective-permute-start(f32[616,128]{1,0:T(8,128)S(1)} %back_products.16), channel_id=1, source_target_pairs={{0,1},{3,2},{4,5},{7,6},{8,9},{11,10},{12,13},{15,14},{16,17},{19,... | collective-permute-start | bytes 946184 | tf_op jit(solution)/shard_map/ppermute | solution.py:304
  23.4 22.7 %collective-permute-start.6 = (f32[616,128]{1,0:T(8,128)S(1)}, f32[616,128]{1,0:T(8,128)S(1)}, u32[]{:S(2)}, u32[]{:S(2)}) collective-permute-start(f32[616,128]{1,0:T(8,128)S(1)} %back_products.17), channel_id=1, source_target_pairs={{0,1},{3,2},{4,5},{7,6},{8,9},{11,10},{12,13},{15,14},{16,17},{19,... | collective-permute-start | bytes 946184 | tf_op jit(solution)/shard_map/ppermute | solution.py:304
  29.5 17.5 %collective-permute-start.5 = (f32[616,128]{1,0:T(8,128)S(1)}, f32[616,128]{1,0:T(8,128)S(1)}, u32[]{:S(2)}, u32[]{:S(2)}) collective-permute-start(f32[616,128]{1,0:T(8,128)S(1)} %add.274), channel_id=1, source_target_pairs={{1,2},{2,1},{5,6},{6,5},{9,10},{10,9},{13,14},{14,13},{17,18},{18,... | collective-permute-start | bytes 946184 | tf_op jit(solution)/shard_map/ppermute | solution.py:304
  30.3 18.2 %collective-permute-start.8 = (f32[616,128]{1,0:T(8,128)S(1)}, f32[616,128]{1,0:T(8,128)S(1)}, u32[]{:S(2)}, u32[]{:S(2)}) collective-permute-start(f32[616,128]{1,0:T(8,128)S(1)} %back_products.18), channel_id=1, source_target_pairs={{0,1},{3,2},{4,5},{7,6},{8,9},{11,10},{12,13},{15,14},{16,17},{19,... | collective-permute-start | bytes 946184 | tf_op jit(solution)/shard_map/ppermute | solution.py:304
  37.5 16.6 %collective-permute-start.10 = (f32[616,128]{1,0:T(8,128)S(1)}, f32[616,128]{1,0:T(8,128)S(1)}, u32[]{:S(2)}, u32[]{:S(2)}) collective-permute-start(f32[616,128]{1,0:T(8,128)S(1)} %back_products.19), channel_id=1, source_target_pairs={{0,1},{3,2},{4,5},{7,6},{8,9},{11,10},{12,13},{15,14},{16,17},{19,... | collective-permute-start | bytes 946184 | tf_op jit(solution)/shard_map/ppermute | solution.py:304
  46.2 7.3 %collective-permute-start.7 = (f32[616,128]{1,0:T(8,128)S(1)}, f32[616,128]{1,0:T(8,128)S(1)}, u32[]{:S(2)}, u32[]{:S(2)}) collective-permute-start(f32[616,128]{1,0:T(8,128)S(1)} %add.276), channel_id=1, source_target_pairs={{1,2},{2,1},{5,6},{6,5},{9,10},{10,9},{13,14},{14,13},{17,18},{18,... | collective-permute-start | bytes 946184 | tf_op jit(solution)/shard_map/ppermute | solution.py:304
  47.1 14.4 %collective-permute-start.11 = (f32[616,128]{1,0:T(8,128)S(1)}, f32[616,128]{1,0:T(8,128)S(1)}, u32[]{:S(2)}, u32[]{:S(2)}) collective-permute-start(f32[616,128]{1,0:T(8,128)S(1)} %select_add_fusion.7), channel_id=1, source_target_pairs={{0,1},{1,0},{2,3},{3,2},{4,5},{5,4},{6,7},{7,6},{8,9},{9,8},{10,11... | collective-permute-start | bytes 946184 | tf_op jit(solution)/shard_map/ppermute | solution.py:304
  52.8 8.7 %collective-permute-start.9 = (f32[616,128]{1,0:T(8,128)S(1)}, f32[616,128]{1,0:T(8,128)S(1)}, u32[]{:S(2)}, u32[]{:S(2)}) collective-permute-start(f32[616,128]{1,0:T(8,128)S(1)} %add.278), channel_id=1, source_target_pairs={{1,2},{2,1},{5,6},{6,5},{9,10},{10,9},{13,14},{14,13},{17,18},{18,... | collective-permute-start | bytes 946184 | tf_op jit(solution)/shard_map/ppermute | solution.py:304
  54.2 13.3 %collective-permute-start.12 = (f32[616,128]{1,0:T(8,128)S(1)}, f32[616,128]{1,0:T(8,128)S(1)}, u32[]{:S(2)}, u32[]{:S(2)}) collective-permute-start(f32[616,128]{1,0:T(8,128)S(1)} %add.280), channel_id=1, source_target_pairs={{1,2},{2,1},{5,6},{6,5},{9,10},{10,9},{13,14},{14,13},{17,18},{18,... | collective-permute-start | bytes 946184 | tf_op jit(solution)/shard_map/ppermute | solution.py:304
  55.1 12.4 %collective-permute-start.13 = (f32[616,128]{1,0:T(8,128)S(1)}, f32[616,128]{1,0:T(8,128)S(1)}, u32[]{:S(2)}, u32[]{:S(2)}) collective-permute-start(f32[616,128]{1,0:T(8,128)S(1)} %select_add_fusion.6), channel_id=1, source_target_pairs={{0,1},{1,0},{2,3},{3,2},{4,5},{5,4},{6,7},{7,6},{8,9},{9,8},{10,11... | collective-permute-start | bytes 946184 | tf_op jit(solution)/shard_map/ppermute | solution.py:304
  62.7 11.0 %collective-permute-start.16 = (f32[616,128]{1,0:T(8,128)S(1)}, f32[616,128]{1,0:T(8,128)S(1)}, u32[]{:S(2)}, u32[]{:S(2)}) collective-permute-start(f32[616,128]{1,0:T(8,128)S(1)} %select_add_fusion.5), channel_id=1, source_target_pairs={{0,1},{1,0},{2,3},{3,2},{4,5},{5,4},{6,7},{7,6},{8,9},{9,8},{10,11... | collective-permute-start | bytes 946184 | tf_op jit(solution)/shard_map/ppermute | solution.py:304
  66.1 8.2 %collective-permute-start.17 = (f32[616,128]{1,0:T(8,128)S(1)}, f32[616,128]{1,0:T(8,128)S(1)}, u32[]{:S(2)}, u32[]{:S(2)}) collective-permute-start(f32[616,128]{1,0:T(8,128)S(1)} %get-tuple-element.227), channel_id=1, source_target_pairs={{1,2},{2,1},{5,6},{6,5},{9,10},{10,9},{13,14},{14,13},{17,18},{18,... | collective-permute-start | bytes 946184 | tf_op jit(solution)/shard_map/ppermute | solution.py:304
  68.1 10.2 %collective-permute-start.14 = (f32[616,128]{1,0:T(8,128)S(1)}, f32[616,128]{1,0:T(8,128)S(1)}, u32[]{:S(2)}, u32[]{:S(2)}) collective-permute-start(f32[616,128]{1,0:T(8,128)S(1)} %select_add_fusion.4), channel_id=1, source_target_pairs={{0,1},{1,0},{2,3},{3,2},{4,5},{5,4},{6,7},{7,6},{8,9},{9,8},{10,11... | collective-permute-start | bytes 946184 | tf_op jit(solution)/shard_map/ppermute | solution.py:304
  72.2 6.7 %collective-permute-start.15 = (f32[616,128]{1,0:T(8,128)S(1)}, f32[616,128]{1,0:T(8,128)S(1)}, u32[]{:S(2)}, u32[]{:S(2)}) collective-permute-start(f32[616,128]{1,0:T(8,128)S(1)} %get-tuple-element.225), channel_id=1, source_target_pairs={{1,2},{2,1},{5,6},{6,5},{9,10},{10,9},{13,14},{14,13},{17,18},{18,... | collective-permute-start | bytes 946184 | tf_op jit(solution)/shard_map/ppermute | solution.py:304
  74.3 13.6 %collective-permute-start.20 = (f32[616,128]{1,0:T(8,128)S(1)}, f32[616,128]{1,0:T(8,128)S(1)}, u32[]{:S(2)}, u32[]{:S(2)}) collective-permute-start(f32[616,128]{1,0:T(8,128)S(1)} %get-tuple-element.236), channel_id=1, source_target_pairs={{1,2},{2,1},{5,6},{6,5},{9,10},{10,9},{13,14},{14,13},{17,18},{18,... | collective-permute-start | bytes 946184 | tf_op jit(solution)/shard_map/ppermute | solution.py:304
  75.0 12.4 %collective-permute-start.21 = (f32[616,128]{1,0:T(8,128)S(1)}, f32[616,128]{1,0:T(8,128)S(1)}, u32[]{:S(2)}, u32[]{:S(2)}) collective-permute-start(f32[616,128]{1,0:T(8,128)S(1)} %add.293), channel_id=1, source_target_pairs={{1,0},{2,3},{5,4},{6,7},{9,8},{10,11},{13,12},{14,15},{17,16},{18,... | collective-permute-start | bytes 946184 | tf_op jit(solution)/shard_map/ppermute | solution.py:304
  79.0 15.1 %collective-permute-start.19 = (f32[616,128]{1,0:T(8,128)S(1)}, f32[616,128]{1,0:T(8,128)S(1)}, u32[]{:S(2)}, u32[]{:S(2)}) collective-permute-start(f32[616,128]{1,0:T(8,128)S(1)} %add.289), channel_id=1, source_target_pairs={{1,0},{2,3},{5,4},{6,7},{9,8},{10,11},{13,12},{14,15},{17,16},{18,... | collective-permute-start | bytes 946184 | tf_op jit(solution)/shard_map/ppermute | solution.py:304
  80.3 14.3 %collective-permute-start.18 = (f32[616,128]{1,0:T(8,128)S(1)}, f32[616,128]{1,0:T(8,128)S(1)}, u32[]{:S(2)}, u32[]{:S(2)}) collective-permute-start(f32[616,128]{1,0:T(8,128)S(1)} %get-tuple-element.234), channel_id=1, source_target_pairs={{1,2},{2,1},{5,6},{6,5},{9,10},{10,9},{13,14},{14,13},{17,18},{18,... | collective-permute-start | bytes 946184 | tf_op jit(solution)/shard_map/ppermute | solution.py:304
  87.9 12.9 %collective-permute-start.23 = (f32[616,128]{1,0:T(8,128)S(1)}, f32[616,128]{1,0:T(8,128)S(1)}, u32[]{:S(2)}, u32[]{:S(2)}) collective-permute-start(f32[616,128]{1,0:T(8,128)S(1)} %add.299), channel_id=1, source_target_pairs={{1,0},{2,3},{5,4},{6,7},{9,8},{10,11},{13,12},{14,15},{17,16},{18,... | collective-permute-start | bytes 946184 | tf_op jit(solution)/shard_map/ppermute | solution.py:304
  94.7 9.6 %collective-permute-start.22 = (f32[616,128]{1,0:T(8,128)S(1)}, f32[616,128]{1,0:T(8,128)S(1)}, u32[]{:S(2)}, u32[]{:S(2)}) collective-permute-start(f32[616,128]{1,0:T(8,128)S(1)} %add.296), channel_id=1, source_target_pairs={{1,0},{2,3},{5,4},{6,7},{9,8},{10,11},{13,12},{14,15},{17,16},{18,... | collective-permute-start | bytes 946184 | tf_op jit(solution)/shard_map/ppermute | solution.py:304
  107.9 4.6 %collective-permute-start.27 = (f32[24,128]{1,0:T(8,128)S(1)}, f32[24,128]{1,0:T(8,128)S(1)}, u32[]{:S(2)}, u32[]{:S(2)}) collective-permute-start(f32[24,128]{1,0:T(8,128)S(1)} %add.306), channel_id=1, source_target_pairs={{0,24},{4,28},{8,16},{12,20},{16,8},{20,12},{24,0},{28,4},{1,25},{... | collective-permute-start | bytes 36872 | tf_op jit(solution)/shard_map/ppermute | solution.py:240
  113.4 7.9 %collective-permute-start.28 = (f32[616,128]{1,0:T(8,128)S(1)}, f32[616,128]{1,0:T(8,128)S(1)}, u32[]{:S(2)}, u32[]{:S(2)}) collective-permute-start(f32[616,128]{1,0:T(8,128)S(1)} %back_products.24), channel_id=1, source_target_pairs={{0,1},{3,2},{4,5},{7,6},{8,9},{11,10},{12,13},{15,14},{16,17},{19,... | collective-permute-start | bytes 946184 | tf_op jit(solution)/shard_map/ppermute | solution.py:304
  119.2 9.4 %collective-permute-start.30 = (f32[616,128]{1,0:T(8,128)S(1)}, f32[616,128]{1,0:T(8,128)S(1)}, u32[]{:S(2)}, u32[]{:S(2)}) collective-permute-start(f32[616,128]{1,0:T(8,128)S(1)} %back_products.25), channel_id=1, source_target_pairs={{0,1},{3,2},{4,5},{7,6},{8,9},{11,10},{12,13},{15,14},{16,17},{19,... | collective-permute-start | bytes 946184 | tf_op jit(solution)/shard_map/ppermute | solution.py:304
  121.4 12.1 %collective-permute-start.33 = (f32[616,128]{1,0:T(8,128)S(1)}, f32[616,128]{1,0:T(8,128)S(1)}, u32[]{:S(2)}, u32[]{:S(2)}) collective-permute-start(f32[616,128]{1,0:T(8,128)S(1)} %add.311), channel_id=1, source_target_pairs={{1,2},{2,1},{5,6},{6,5},{9,10},{10,9},{13,14},{14,13},{17,18},{18,... | collective-permute-start | bytes 946184 | tf_op jit(solution)/shard_map/ppermute | solution.py:304
  122.1 14.3 %collective-permute-start.32 = (f32[616,128]{1,0:T(8,128)S(1)}, f32[616,128]{1,0:T(8,128)S(1)}, u32[]{:S(2)}, u32[]{:S(2)}) collective-permute-start(f32[616,128]{1,0:T(8,128)S(1)} %back_products.26), channel_id=1, source_target_pairs={{0,1},{3,2},{4,5},{7,6},{8,9},{11,10},{12,13},{15,14},{16,17},{19,... | collective-permute-start | bytes 946184 | tf_op jit(solution)/shard_map/ppermute | solution.py:304
  128.6 14.6 %collective-permute-start.29 = (f32[616,128]{1,0:T(8,128)S(1)}, f32[616,128]{1,0:T(8,128)S(1)}, u32[]{:S(2)}, u32[]{:S(2)}) collective-permute-start(f32[616,128]{1,0:T(8,128)S(1)} %back_products.27), channel_id=1, source_target_pairs={{0,1},{3,2},{4,5},{7,6},{8,9},{11,10},{12,13},{15,14},{16,17},{19,... | collective-permute-start | bytes 946184 | tf_op jit(solution)/shard_map/ppermute | solution.py:304
  132.8 4.4 %collective-permute-start.31 = (f32[616,128]{1,0:T(8,128)S(1)}, f32[616,128]{1,0:T(8,128)S(1)}, u32[]{:S(2)}, u32[]{:S(2)}) collective-permute-start(f32[616,128]{1,0:T(8,128)S(1)} %add.313), channel_id=1, source_target_pairs={{1,2},{2,1},{5,6},{6,5},{9,10},{10,9},{13,14},{14,13},{17,18},{18,... | collective-permute-start | bytes 946184 | tf_op jit(solution)/shard_map/ppermute | solution.py:304
  133.6 16.4 %collective-permute-start.36 = (f32[616,128]{1,0:T(8,128)S(1)}, f32[616,128]{1,0:T(8,128)S(1)}, u32[]{:S(2)}, u32[]{:S(2)}) collective-permute-start(f32[616,128]{1,0:T(8,128)S(1)} %select_add_fusion.1), channel_id=1, source_target_pairs={{0,1},{1,0},{2,3},{3,2},{4,5},{5,4},{6,7},{7,6},{8,9},{9,8},{10,11... | collective-permute-start | bytes 946184 | tf_op jit(solution)/shard_map/ppermute | solution.py:304
  136.5 13.6 %collective-permute-start.37 = (f32[616,128]{1,0:T(8,128)S(1)}, f32[616,128]{1,0:T(8,128)S(1)}, u32[]{:S(2)}, u32[]{:S(2)}) collective-permute-start(f32[616,128]{1,0:T(8,128)S(1)} %add.315), channel_id=1, source_target_pairs={{1,2},{2,1},{5,6},{6,5},{9,10},{10,9},{13,14},{14,13},{17,18},{18,... | collective-permute-start | bytes 946184 | tf_op jit(solution)/shard_map/ppermute | solution.py:304
  143.2 13.5 %collective-permute-start.35 = (f32[616,128]{1,0:T(8,128)S(1)}, f32[616,128]{1,0:T(8,128)S(1)}, u32[]{:S(2)}, u32[]{:S(2)}) collective-permute-start(f32[616,128]{1,0:T(8,128)S(1)} %select_add_fusion.2), channel_id=1, source_target_pairs={{0,1},{1,0},{2,3},{3,2},{4,5},{5,4},{6,7},{7,6},{8,9},{9,8},{10,11... | collective-permute-start | bytes 946184 | tf_op jit(solution)/shard_map/ppermute | solution.py:304
  145.8 11.0 %collective-permute-start.34 = (f32[616,128]{1,0:T(8,128)S(1)}, f32[616,128]{1,0:T(8,128)S(1)}, u32[]{:S(2)}, u32[]{:S(2)}) collective-permute-start(f32[616,128]{1,0:T(8,128)S(1)} %add.312), channel_id=1, source_target_pairs={{1,2},{2,1},{5,6},{6,5},{9,10},{10,9},{13,14},{14,13},{17,18},{18,... | collective-permute-start | bytes 946184 | tf_op jit(solution)/shard_map/ppermute | solution.py:304
  151.2 12.2 %collective-permute-start.40 = (f32[616,128]{1,0:T(8,128)S(1)}, f32[616,128]{1,0:T(8,128)S(1)}, u32[]{:S(2)}, u32[]{:S(2)}) collective-permute-start(f32[616,128]{1,0:T(8,128)S(1)} %select_add_fusion), channel_id=1, source_target_pairs={{0,1},{1,0},{2,3},{3,2},{4,5},{5,4},{6,7},{7,6},{8,9},{9,8},{10,11... | collective-permute-start | bytes 946184 | tf_op jit(solution)/shard_map/ppermute | solution.py:304
  153.8 10.3 %collective-permute-start.41 = (f32[616,128]{1,0:T(8,128)S(1)}, f32[616,128]{1,0:T(8,128)S(1)}, u32[]{:S(2)}, u32[]{:S(2)}) collective-permute-start(f32[616,128]{1,0:T(8,128)S(1)} %get-tuple-element.291), channel_id=1, source_target_pairs={{1,2},{2,1},{5,6},{6,5},{9,10},{10,9},{13,14},{14,13},{17,18},{18,... | collective-permute-start | bytes 946184 | tf_op jit(solution)/shard_map/ppermute | solution.py:304
  157.3 10.2 %collective-permute-start.38 = (f32[616,128]{1,0:T(8,128)S(1)}, f32[616,128]{1,0:T(8,128)S(1)}, u32[]{:S(2)}, u32[]{:S(2)}) collective-permute-start(f32[616,128]{1,0:T(8,128)S(1)} %select_add_fusion.3), channel_id=1, source_target_pairs={{0,1},{1,0},{2,3},{3,2},{4,5},{5,4},{6,7},{7,6},{8,9},{9,8},{10,11... | collective-permute-start | bytes 946184 | tf_op jit(solution)/shard_map/ppermute | solution.py:304
  159.9 8.2 %collective-permute-start.39 = (f32[616,128]{1,0:T(8,128)S(1)}, f32[616,128]{1,0:T(8,128)S(1)}, u32[]{:S(2)}, u32[]{:S(2)}) collective-permute-start(f32[616,128]{1,0:T(8,128)S(1)} %get-tuple-element.288), channel_id=1, source_target_pairs={{1,2},{2,1},{5,6},{6,5},{9,10},{10,9},{13,14},{14,13},{17,18},{18,... | collective-permute-start | bytes 946184 | tf_op jit(solution)/shard_map/ppermute | solution.py:304
  164.1 15.7 %collective-permute-start.44 = (f32[616,128]{1,0:T(8,128)S(1)}, f32[616,128]{1,0:T(8,128)S(1)}, u32[]{:S(2)}, u32[]{:S(2)}) collective-permute-start(f32[616,128]{1,0:T(8,128)S(1)} %get-tuple-element.302), channel_id=1, source_target_pairs={{1,2},{2,1},{5,6},{6,5},{9,10},{10,9},{13,14},{14,13},{17,18},{18,... | collective-permute-start | bytes 946184 | tf_op jit(solution)/shard_map/ppermute | solution.py:304
  164.8 14.5 %collective-permute-start.45 = (f32[616,128]{1,0:T(8,128)S(1)}, f32[616,128]{1,0:T(8,128)S(1)}, u32[]{:S(2)}, u32[]{:S(2)}) collective-permute-start(f32[616,128]{1,0:T(8,128)S(1)} %add.332), channel_id=1, source_target_pairs={{1,0},{2,3},{5,4},{6,7},{9,8},{10,11},{13,12},{14,15},{17,16},{18,... | collective-permute-start | bytes 946184 | tf_op jit(solution)/shard_map/ppermute | solution.py:304
  168.2 18.4 %collective-permute-start.42 = (f32[616,128]{1,0:T(8,128)S(1)}, f32[616,128]{1,0:T(8,128)S(1)}, u32[]{:S(2)}, u32[]{:S(2)}) collective-permute-start(f32[616,128]{1,0:T(8,128)S(1)} %get-tuple-element.299), channel_id=1, source_target_pairs={{1,2},{2,1},{5,6},{6,5},{9,10},{10,9},{13,14},{14,13},{17,18},{18,... | collective-permute-start | bytes 946184 | tf_op jit(solution)/shard_map/ppermute | solution.py:304
  168.9 17.2 %collective-permute-start.43 = (f32[616,128]{1,0:T(8,128)S(1)}, f32[616,128]{1,0:T(8,128)S(1)}, u32[]{:S(2)}, u32[]{:S(2)}) collective-permute-start(f32[616,128]{1,0:T(8,128)S(1)} %add.328), channel_id=1, source_target_pairs={{1,0},{2,3},{5,4},{6,7},{9,8},{10,11},{13,12},{14,15},{17,16},{18,... | collective-permute-start | bytes 946184 | tf_op jit(solution)/shard_map/ppermute | solution.py:304
  179.9 12.7 %collective-permute-start.47 = (f32[616,128]{1,0:T(8,128)S(1)}, f32[616,128]{1,0:T(8,128)S(1)}, u32[]{:S(2)}, u32[]{:S(2)}) collective-permute-start(f32[616,128]{1,0:T(8,128)S(1)} %add.338), channel_id=1, source_target_pairs={{1,0},{2,3},{5,4},{6,7},{9,8},{10,11},{13,12},{14,15},{17,16},{18,... | collective-permute-start | bytes 946184 | tf_op jit(solution)/shard_map/ppermute | solution.py:304
  186.7 9.2 %collective-permute-start.46 = (f32[616,128]{1,0:T(8,128)S(1)}, f32[616,128]{1,0:T(8,128)S(1)}, u32[]{:S(2)}, u32[]{:S(2)}) collective-permute-start(f32[616,128]{1,0:T(8,128)S(1)} %add.335), channel_id=1, source_target_pairs={{1,0},{2,3},{5,4},{6,7},{9,8},{10,11},{13,12},{14,15},{17,16},{18,... | collective-permute-start | bytes 946184 | tf_op jit(solution)/shard_map/ppermute | solution.py:304
  198.2 5.1 %collective-permute-start.50 = (f32[24,128]{1,0:T(8,128)S(1)}, f32[24,128]{1,0:T(8,128)S(1)}, u32[]{:S(2)}, u32[]{:S(2)}) collective-permute-start(f32[24,128]{1,0:T(8,128)S(1)} %add.345), channel_id=1, source_target_pairs={{0,16},{4,20},{8,24},{12,28},{16,0},{20,4},{24,8},{28,12},{1,17},{... | collective-permute-start | bytes 36872 | tf_op jit(solution)/shard_map/ppermute | solution.py:240
  199.2 4.6 %collective-permute-start.51 = (f32[24,128]{1,0:T(8,128)S(1)}, f32[24,128]{1,0:T(8,128)S(1)}, u32[]{:S(2)}, u32[]{:S(2)}) collective-permute-start(f32[24,128]{1,0:T(8,128)S(1)} %add.345), channel_id=1, source_target_pairs={{0,24},{4,28},{8,16},{12,20},{16,8},{20,12},{24,0},{28,4},{1,25},{... | collective-permute-start | bytes 36872 | tf_op jit(solution)/shard_map/ppermute | solution.py:240
  200.5 3.7 %collective-permute-start.49 = (f32[24,128]{1,0:T(8,128)S(1)}, f32[24,128]{1,0:T(8,128)S(1)}, u32[]{:S(2)}, u32[]{:S(2)}) collective-permute-start(f32[24,128]{1,0:T(8,128)S(1)} %add.345), channel_id=1, source_target_pairs={{0,8},{4,12},{8,0},{12,4},{16,24},{20,28},{24,16},{28,20},{1,9},{5... | collective-permute-start | bytes 36872 | tf_op jit(solution)/shard_map/ppermute | solution.py:240
  204.3 4.5 %collective-permute-start.53 = (f32[1,128]{1,0:T(1,128)S(1)}, f32[1,128]{1,0:T(1,128)S(1)}, u32[]{:S(2)}, u32[]{:S(2)}) collective-permute-start(f32[1,128]{1,0:T(1,128)S(1)} %bitcast.40), channel_id=1, source_target_pairs={{0,2},{1,3},{2,0},{3,1},{4,6},{5,7},{6,4},{7,5},{8,10},{9,11},{10,... | collective-permute-start | bytes 1544 | tf_op jit(solution)/shard_map/ppermute | solution.py:240
  204.3 5.4 %collective-permute-start.54 = (f32[1,128]{1,0:T(1,128)S(1)}, f32[1,128]{1,0:T(1,128)S(1)}, u32[]{:S(2)}, u32[]{:S(2)}) collective-permute-start(f32[1,128]{1,0:T(1,128)S(1)} %bitcast.41), channel_id=1, source_target_pairs={{0,3},{1,2},{2,1},{3,0},{4,7},{5,6},{6,5},{7,4},{8,11},{9,10},{10,... | collective-permute-start | bytes 1544 | tf_op jit(solution)/shard_map/ppermute | solution.py:240
  (16 other events, 97.9 us)

commit v5 on v4

--- a/solution.py
+++ b/solution.py
@@ -310,10 +310,10 @@
     for step in range(steps):
         gate, state = exchange(0, step, step - gaps[1], gate, state)
         if step == 0 and eager:
-            made += [produce(chunk, gate) for chunk in range(1, chunks)]
+            made += [produce(chunk, gate) for chunk in range(1, min(6, chunks))]
             *made[1:], gate = lax.optimization_barrier((*made[1:], gate))
-        if len(made) < chunks and not eager:
-            made.append(produce(step + 1, gate))
+        if len(made) < chunks and (step or not eager):
+            made.append(produce(len(made), gate))
             made[-1], gate, *state = lax.optimization_barrier((made[-1], gate, *state))
             state = tuple(state)
         gate, state = exchange(1, step, step - gaps[0], gate, state)

time: 212 us -> 212 us (level)
  no operation moved by 1% of the time
where the time goes in v5:
time: 212 us; the launch traced here: 211 us
  starting transfers between devices  87.6 us (41%)
  waiting for transfers between devices  80.4 us (38%)
  Pallas kernels  26.5 us (12%)
  local copies, waits for them, and re-layouts  10.9 us (5%)
  other arithmetic  4.47 us (2%)
    ppermute x40, starting transfers between devices, exchange(): got[parity].append(lax.ppermute(own, 'walker', pairs))  72.2 us
    ppermute x40, waiting for transfers between devices, exchange(): got[parity].append(lax.ppermute(own, 'walker', pairs))  67.6 us
    ppermute x15, starting transfers between devices, small_sum(): lax.ppermute(value, axis, [(i, i ^ bit * j) for i in range(size)])  15.4 us
    ppermute x15, waiting for transfers between devices, small_sum(): lax.ppermute(value, axis, [(i, i ^ bit * j) for i in range(size)])  12.8 us
    unnamed x30, local copies, waits for them, and re-layouts  10.7 us
    pallas_call x16, Pallas kernels, back_call(): pl.pallas_call(functools.partial(back_kernel, chunk * rows), in_specs=[vm...  9.59 us
    pallas_call x1, Pallas kernels, start_call(): pl.pallas_call(functools.partial(start_kernel, copies), in_specs=[hbm(),...  8.09 us
    pallas_call x16, Pallas kernels, advance_call(): pl.pallas_call(functools.partial(advance_kernel, chunk * rows, rows_all,...  7.18 us
  transfers between devices with their start and end apart: 55, of which 33 were waited for; matrix products, arithmetic and copies ran while one was open for 2% of the time, Pallas kernels for 7%

profile of v5, /device:TPU:0, one launch (start us, length us, event | category | flops | bytes accessed | tf_op | source)
XLA Modules:
  0.0 210.8 jit_solution(14200638248482017639)
XLA Ops:
  0.0 8.1 %start_products.1 = (f32[24,128]{1,0:T(8,128)S(1)}, f32[8,622592]{1,0:T(8,128)S(1)}) custom-call(f32[8,622592]{1,0:T(8,128)} %derivs_hbm.1, f32[4864,128]{1,0:T(8,128)} %bitcast.11), custom_call_target="tpu_custom_call" | custom-call | tf_op jit(solution)/shard_map/start_products/pallas_call | solution.py:119
  9.5 2.9 %collective-permute-start.2 = (f32[24,128]{1,0:T(8,128)S(1)}, f32[24,128]{1,0:T(8,128)S(1)}, u32[]{:S(2)}, u32[]{:S(2)}) collective-permute-start(f32[24,128]{1,0:T(8,128)S(1)} %add.270), channel_id=1, source_target_pairs={{0,16},{4,20},{8,24},{12,28},{16,0},{20,4},{24,8},{28,12},{1,17},{... | collective-permute-start | bytes 36872 | tf_op jit(solution)/shard_map/ppermute | solution.py:240
  12.3 1.4 collective-permute-start.3
  14.0 2.9 %collective-permute-done.3 = f32[24,128]{1,0:T(8,128)S(1)} collective-permute-done((f32[24,128]{1,0:T(8,128)S(1)}, f32[24,128]{1,0:T(8,128)S(1)}, u32[]{:S(2)}, u32[]{:S(2)}) %collective-permute-start.3) | collective-permute-done | bytes 12320 | tf_op jit(solution)/shard_map/ppermute | solution.py:240
  18.1 3.5 %collective-permute-start.4 = (f32[616,128]{1,0:T(8,128)S(1)}, f32[616,128]{1,0:T(8,128)S(1)}, u32[]{:S(2)}, u32[]{:S(2)}) collective-permute-start(f32[616,128]{1,0:T(8,128)S(1)} %back_products.16), channel_id=1, source_target_pairs={{0,1},{3,2},{4,5},{7,6},{8,9},{11,10},{12,13},{15,14},{16,17},{19,... | collective-permute-start | bytes 946184 | tf_op jit(solution)/shard_map/ppermute | solution.py:304
  23.4 1.3 collective-permute-start.6
  24.7 4.7 %collective-permute-done.4 = f32[616,128]{1,0:T(8,128)S(1)} collective-permute-done((f32[616,128]{1,0:T(8,128)S(1)}, f32[616,128]{1,0:T(8,128)S(1)}, u32[]{:S(2)}, u32[]{:S(2)}) %collective-permute-start.4) | collective-permute-done | bytes 315424 | tf_op jit(solution)/shard_map/ppermute | solution.py:304
  30.3 7.2 %collective-permute-start.8 = (f32[616,128]{1,0:T(8,128)S(1)}, f32[616,128]{1,0:T(8,128)S(1)}, u32[]{:S(2)}, u32[]{:S(2)}) collective-permute-start(f32[616,128]{1,0:T(8,128)S(1)} %back_products.18), channel_id=1, source_target_pairs={{0,1},{3,2},{4,5},{7,6},{8,9},{11,10},{12,13},{15,14},{16,17},{19,... | collective-permute-start | bytes 946184 | tf_op jit(solution)/shard_map/ppermute | solution.py:304
  37.5 1.3 collective-permute-start.10
  38.9 6.7 %copy-done.1 = f32[8,622592]{1,0:T(8,128)S(1)} copy-done((f32[8,622592]{1,0:T(8,128)S(1)}, f32[8,622592]{1,0:T(8,128)}, u32[]{:S(2)}) %copy-start.1) | copy-done | bytes 19922968
  47.1 1.4 collective-permute-start.11
  48.6 3.6 %copy-done.2 = f32[8,622592]{1,0:T(8,128)S(1)} copy-done((f32[8,622592]{1,0:T(8,128)S(1)}, f32[8,622592]{1,0:T(8,128)}, u32[]{:S(2)}) %copy-start.2) | copy-done | bytes 19922968
  55.1 6.4 %collective-permute-start.13 = (f32[616,128]{1,0:T(8,128)S(1)}, f32[616,128]{1,0:T(8,128)S(1)}, u32[]{:S(2)}, u32[]{:S(2)}) collective-permute-start(f32[616,128]{1,0:T(8,128)S(1)} %select_add_fusion.6), channel_id=1, source_target_pairs={{0,1},{1,0},{2,3},{3,2},{4,5},{5,4},{6,7},{7,6},{8,9},{9,8},{10,11... | collective-permute-start | bytes 946184 | tf_op jit(solution)/shard_map/ppermute | solution.py:304
  62.7 3.4 %collective-permute-start.16 = (f32[616,128]{1,0:T(8,128)S(1)}, f32[616,128]{1,0:T(8,128)S(1)}, u32[]{:S(2)}, u32[]{:S(2)}) collective-permute-start(f32[616,128]{1,0:T(8,128)S(1)} %select_add_fusion.5), channel_id=1, source_target_pairs={{0,1},{1,0},{2,3},{3,2},{4,5},{5,4},{6,7},{7,6},{8,9},{9,8},{10,11... | collective-permute-start | bytes 946184 | tf_op jit(solution)/shard_map/ppermute | solution.py:304
  68.1 4.1 %collective-permute-start.14 = (f32[616,128]{1,0:T(8,128)S(1)}, f32[616,128]{1,0:T(8,128)S(1)}, u32[]{:S(2)}, u32[]{:S(2)}) collective-permute-start(f32[616,128]{1,0:T(8,128)S(1)} %select_add_fusion.4), channel_id=1, source_target_pairs={{0,1},{1,0},{2,3},{3,2},{4,5},{5,4},{6,7},{7,6},{8,9},{9,8},{10,11... | collective-permute-start | bytes 946184 | tf_op jit(solution)/shard_map/ppermute | solution.py:304
  75.0 1.3 collective-permute-start.21
  76.3 2.1 collective-permute-done.14
  81.0 6.4 %collective-permute-done.21 = f32[616,128]{1,0:T(8,128)S(1)} collective-permute-done((f32[616,128]{1,0:T(8,128)S(1)}, f32[616,128]{1,0:T(8,128)S(1)}, u32[]{:S(2)}, u32[]{:S(2)}) %collective-permute-start.21) | collective-permute-done | bytes 315424 | tf_op jit(solution)/shard_map/ppermute | solution.py:304
  87.9 1.3 collective-permute-start.23
  89.2 4.9 %collective-permute-done.19 = f32[616,128]{1,0:T(8,128)S(1)} collective-permute-done((f32[616,128]{1,0:T(8,128)S(1)}, f32[616,128]{1,0:T(8,128)S(1)}, u32[]{:S(2)}, u32[]{:S(2)}) %collective-permute-start.19) | collective-permute-done | bytes 315424 | tf_op jit(solution)/shard_map/ppermute | solution.py:304
  94.7 1.3 collective-permute-start.22
  96.0 4.9 %collective-permute-done.23 = f32[616,128]{1,0:T(8,128)S(1)} collective-permute-done((f32[616,128]{1,0:T(8,128)S(1)}, f32[616,128]{1,0:T(8,128)S(1)}, u32[]{:S(2)}, u32[]{:S(2)}) %collective-permute-start.23) | collective-permute-done | bytes 315424 | tf_op jit(solution)/shard_map/ppermute | solution.py:304
  101.4 2.9 %collective-permute-done.22 = f32[616,128]{1,0:T(8,128)S(1)} collective-permute-done((f32[616,128]{1,0:T(8,128)S(1)}, f32[616,128]{1,0:T(8,128)S(1)}, u32[]{:S(2)}, u32[]{:S(2)}) %collective-permute-start.22) | collective-permute-done | bytes 315424 | tf_op jit(solution)/shard_map/ppermute | solution.py:304
  106.1 1.8 collective-permute-start.26
  109.8 2.7 %collective-permute-done.27 = f32[24,128]{1,0:T(8,128)S(1)} collective-permute-done((f32[24,128]{1,0:T(8,128)S(1)}, f32[24,128]{1,0:T(8,128)S(1)}, u32[]{:S(2)}, u32[]{:S(2)}) %collective-permute-start.27) | collective-permute-done | bytes 12320 | tf_op jit(solution)/shard_map/ppermute | solution.py:240
  113.4 1.5 collective-permute-start.28
  119.2 1.3 collective-permute-start.30
  122.1 6.4 %collective-permute-start.32 = (f32[616,128]{1,0:T(8,128)S(1)}, f32[616,128]{1,0:T(8,128)S(1)}, u32[]{:S(2)}, u32[]{:S(2)}) collective-permute-start(f32[616,128]{1,0:T(8,128)S(1)} %back_products.26), channel_id=1, source_target_pairs={{0,1},{3,2},{4,5},{7,6},{8,9},{11,10},{12,13},{15,14},{16,17},{19,... | collective-permute-start | bytes 946184 | tf_op jit(solution)/shard_map/ppermute | solution.py:304
  128.6 4.2 %collective-permute-start.29 = (f32[616,128]{1,0:T(8,128)S(1)}, f32[616,128]{1,0:T(8,128)S(1)}, u32[]{:S(2)}, u32[]{:S(2)}) collective-permute-start(f32[616,128]{1,0:T(8,128)S(1)} %back_products.27), channel_id=1, source_target_pairs={{0,1},{3,2},{4,5},{7,6},{8,9},{11,10},{12,13},{15,14},{16,17},{19,... | collective-permute-start | bytes 946184 | tf_op jit(solution)/shard_map/ppermute | solution.py:304
  134.8 1.7 collective-permute-done.32
  137.2 6.0 %collective-permute-done.29 = f32[616,128]{1,0:T(8,128)S(1)} collective-permute-done((f32[616,128]{1,0:T(8,128)S(1)}, f32[616,128]{1,0:T(8,128)S(1)}, u32[]{:S(2)}, u32[]{:S(2)}) %collective-permute-start.29) | collective-permute-done | bytes 315424 | tf_op jit(solution)/shard_map/ppermute | solution.py:304
  143.2 2.5 %collective-permute-start.35 = (f32[616,128]{1,0:T(8,128)S(1)}, f32[616,128]{1,0:T(8,128)S(1)}, u32[]{:S(2)}, u32[]{:S(2)}) collective-permute-start(f32[616,128]{1,0:T(8,128)S(1)} %select_add_fusion.2), channel_id=1, source_target_pairs={{0,1},{1,0},{2,3},{3,2},{4,5},{5,4},{6,7},{7,6},{8,9},{9,8},{10,11... | collective-permute-start | bytes 946184 | tf_op jit(solution)/shard_map/ppermute | solution.py:304
  146.5 3.5 %collective-permute-done.36 = f32[616,128]{1,0:T(8,128)S(1)} collective-permute-done((f32[616,128]{1,0:T(8,128)S(1)}, f32[616,128]{1,0:T(8,128)S(1)}, u32[]{:S(2)}, u32[]{:S(2)}) %collective-permute-start.36) | collective-permute-done | bytes 315424 | tf_op jit(solution)/shard_map/ppermute | solution.py:304
  151.2 2.5 %collective-permute-start.40 = (f32[616,128]{1,0:T(8,128)S(1)}, f32[616,128]{1,0:T(8,128)S(1)}, u32[]{:S(2)}, u32[]{:S(2)}) collective-permute-start(f32[616,128]{1,0:T(8,128)S(1)} %select_add_fusion), channel_id=1, source_target_pairs={{0,1},{1,0},{2,3},{3,2},{4,5},{5,4},{6,7},{7,6},{8,9},{9,8},{10,11... | collective-permute-start | bytes 946184 | tf_op jit(solution)/shard_map/ppermute | solution.py:304
  154.5 2.3 %collective-permute-done.35 = f32[616,128]{1,0:T(8,128)S(1)} collective-permute-done((f32[616,128]{1,0:T(8,128)S(1)}, f32[616,128]{1,0:T(8,128)S(1)}, u32[]{:S(2)}, u32[]{:S(2)}) %collective-permute-start.35) | collective-permute-done | bytes 315424 | tf_op jit(solution)/shard_map/ppermute | solution.py:304
  157.3 2.5 %collective-permute-start.38 = (f32[616,128]{1,0:T(8,128)S(1)}, f32[616,128]{1,0:T(8,128)S(1)}, u32[]{:S(2)}, u32[]{:S(2)}) collective-permute-start(f32[616,128]{1,0:T(8,128)S(1)} %select_add_fusion.3), channel_id=1, source_target_pairs={{0,1},{1,0},{2,3},{3,2},{4,5},{5,4},{6,7},{7,6},{8,9},{9,8},{10,11... | collective-permute-start | bytes 946184 | tf_op jit(solution)/shard_map/ppermute | solution.py:304
  160.6 2.9 %collective-permute-done.40 = f32[616,128]{1,0:T(8,128)S(1)} collective-permute-done((f32[616,128]{1,0:T(8,128)S(1)}, f32[616,128]{1,0:T(8,128)S(1)}, u32[]{:S(2)}, u32[]{:S(2)}) %collective-permute-start.40) | collective-permute-done | bytes 315424 | tf_op jit(solution)/shard_map/ppermute | solution.py:304
  164.8 1.3 collective-permute-start.45
  166.1 1.5 collective-permute-done.38
  168.9 1.3 collective-permute-start.43
  170.2 9.1 %collective-permute-done.45 = f32[616,128]{1,0:T(8,128)S(1)} collective-permute-done((f32[616,128]{1,0:T(8,128)S(1)}, f32[616,128]{1,0:T(8,128)S(1)}, u32[]{:S(2)}, u32[]{:S(2)}) %collective-permute-start.45) | collective-permute-done | bytes 315424 | tf_op jit(solution)/shard_map/ppermute | solution.py:304
  181.2 4.9 %collective-permute-done.43 = f32[616,128]{1,0:T(8,128)S(1)} collective-permute-done((f32[616,128]{1,0:T(8,128)S(1)}, f32[616,128]{1,0:T(8,128)S(1)}, u32[]{:S(2)}, u32[]{:S(2)}) %collective-permute-start.43) | collective-permute-done | bytes 315424 | tf_op jit(solution)/shard_map/ppermute | solution.py:304
  188.1 4.5 %collective-permute-done.47 = f32[616,128]{1,0:T(8,128)S(1)} collective-permute-done((f32[616,128]{1,0:T(8,128)S(1)}, f32[616,128]{1,0:T(8,128)S(1)}, u32[]{:S(2)}, u32[]{:S(2)}) %collective-permute-start.47) | collective-permute-done | bytes 315424 | tf_op jit(solution)/shard_map/ppermute | solution.py:304
  192.5 3.4 %collective-permute-done.46 = f32[616,128]{1,0:T(8,128)S(1)} collective-permute-done((f32[616,128]{1,0:T(8,128)S(1)}, f32[616,128]{1,0:T(8,128)S(1)}, u32[]{:S(2)}, u32[]{:S(2)}) %collective-permute-start.46) | collective-permute-done | bytes 315424 | tf_op jit(solution)/shard_map/ppermute | solution.py:304
  199.2 1.3 collective-permute-start.51
  201.7 1.6 share_parts.1
  204.3 2.0 collective-permute-start.54
  206.3 1.5 collective-permute-start.52
  (189 shorter events, 52.0 us)
Async XLA Ops:
  9.5 4.5 %collective-permute-start.2 = (f32[24,128]{1,0:T(8,128)S(1)}, f32[24,128]{1,0:T(8,128)S(1)}, u32[]{:S(2)}, u32[]{:S(2)}) collective-permute-start(f32[24,128]{1,0:T(8,128)S(1)} %add.270), channel_id=1, source_target_pairs={{0,16},{4,20},{8,24},{12,28},{16,0},{20,4},{24,8},{28,12},{1,17},{... | collective-permute-start | bytes 36872 | tf_op jit(solution)/shard_map/ppermute | solution.py:240
  12.3 4.6 %collective-permute-start.3 = (f32[24,128]{1,0:T(8,128)S(1)}, f32[24,128]{1,0:T(8,128)S(1)}, u32[]{:S(2)}, u32[]{:S(2)}) collective-permute-start(f32[24,128]{1,0:T(8,128)S(1)} %add.270), channel_id=1, source_target_pairs={{0,24},{4,28},{8,16},{12,20},{16,8},{20,12},{24,0},{28,4},{1,25},{... | collective-permute-start | bytes 36872 | tf_op jit(solution)/shard_map/ppermute | solution.py:240
  18.1 11.4 %collective-permute-start.4 = (f32[616,128]{1,0:T(8,128)S(1)}, f32[616,128]{1,0:T(8,128)S(1)}, u32[]{:S(2)}, u32[]{:S(2)}) collective-permute-start(f32[616,128]{1,0:T(8,128)S(1)} %back_products.16), channel_id=1, source_target_pairs={{0,1},{3,2},{4,5},{7,6},{8,9},{11,10},{12,13},{15,14},{16,17},{19,... | collective-permute-start | bytes 946184 | tf_op jit(solution)/shard_map/ppermute | solution.py:304
  23.4 22.7 %collective-permute-start.6 = (f32[616,128]{1,0:T(8,128)S(1)}, f32[616,128]{1,0:T(8,128)S(1)}, u32[]{:S(2)}, u32[]{:S(2)}) collective-permute-start(f32[616,128]{1,0:T(8,128)S(1)} %back_products.17), channel_id=1, source_target_pairs={{0,1},{3,2},{4,5},{7,6},{8,9},{11,10},{12,13},{15,14},{16,17},{19,... | collective-permute-start | bytes 946184 | tf_op jit(solution)/shard_map/ppermute | solution.py:304
  29.5 17.5 %collective-permute-start.5 = (f32[616,128]{1,0:T(8,128)S(1)}, f32[616,128]{1,0:T(8,128)S(1)}, u32[]{:S(2)}, u32[]{:S(2)}) collective-permute-start(f32[616,128]{1,0:T(8,128)S(1)} %add.274), channel_id=1, source_target_pairs={{1,2},{2,1},{5,6},{6,5},{9,10},{10,9},{13,14},{14,13},{17,18},{18,... | collective-permute-start | bytes 946184 | tf_op jit(solution)/shard_map/ppermute | solution.py:304
  30.3 18.2 %collective-permute-start.8 = (f32[616,128]{1,0:T(8,128)S(1)}, f32[616,128]{1,0:T(8,128)S(1)}, u32[]{:S(2)}, u32[]{:S(2)}) collective-permute-start(f32[616,128]{1,0:T(8,128)S(1)} %back_products.18), channel_id=1, source_target_pairs={{0,1},{3,2},{4,5},{7,6},{8,9},{11,10},{12,13},{15,14},{16,17},{19,... | collective-permute-start | bytes 946184 | tf_op jit(solution)/shard_map/ppermute | solution.py:304
  37.5 16.6 %collective-permute-start.10 = (f32[616,128]{1,0:T(8,128)S(1)}, f32[616,128]{1,0:T(8,128)S(1)}, u32[]{:S(2)}, u32[]{:S(2)}) collective-permute-start(f32[616,128]{1,0:T(8,128)S(1)} %back_products.19), channel_id=1, source_target_pairs={{0,1},{3,2},{4,5},{7,6},{8,9},{11,10},{12,13},{15,14},{16,17},{19,... | collective-permute-start | bytes 946184 | tf_op jit(solution)/shard_map/ppermute | solution.py:304
  46.2 7.3 %collective-permute-start.7 = (f32[616,128]{1,0:T(8,128)S(1)}, f32[616,128]{1,0:T(8,128)S(1)}, u32[]{:S(2)}, u32[]{:S(2)}) collective-permute-start(f32[616,128]{1,0:T(8,128)S(1)} %add.276), channel_id=1, source_target_pairs={{1,2},{2,1},{5,6},{6,5},{9,10},{10,9},{13,14},{14,13},{17,18},{18,... | collective-permute-start | bytes 946184 | tf_op jit(solution)/shard_map/ppermute | solution.py:304
  47.1 14.4 %collective-permute-start.11 = (f32[616,128]{1,0:T(8,128)S(1)}, f32[616,128]{1,0:T(8,128)S(1)}, u32[]{:S(2)}, u32[]{:S(2)}) collective-permute-start(f32[616,128]{1,0:T(8,128)S(1)} %select_add_fusion.7), channel_id=1, source_target_pairs={{0,1},{1,0},{2,3},{3,2},{4,5},{5,4},{6,7},{7,6},{8,9},{9,8},{10,11... | collective-permute-start | bytes 946184 | tf_op jit(solution)/shard_map/ppermute | solution.py:304
  52.8 8.7 %collective-permute-start.9 = (f32[616,128]{1,0:T(8,128)S(1)}, f32[616,128]{1,0:T(8,128)S(1)}, u32[]{:S(2)}, u32[]{:S(2)}) collective-permute-start(f32[616,128]{1,0:T(8,128)S(1)} %add.278), channel_id=1, source_target_pairs={{1,2},{2,1},{5,6},{6,5},{9,10},{10,9},{13,14},{14,13},{17,18},{18,... | collective-permute-start | bytes 946184 | tf_op jit(solution)/shard_map/ppermute | solution.py:304
  54.2 13.3 %collective-permute-start.12 = (f32[616,128]{1,0:T(8,128)S(1)}, f32[616,128]{1,0:T(8,128)S(1)}, u32[]{:S(2)}, u32[]{:S(2)}) collective-permute-start(f32[616,128]{1,0:T(8,128)S(1)} %add.280), channel_id=1, source_target_pairs={{1,2},{2,1},{5,6},{6,5},{9,10},{10,9},{13,14},{14,13},{17,18},{18,... | collective-permute-start | bytes 946184 | tf_op jit(solution)/shard_map/ppermute | solution.py:304
  55.1 12.4 %collective-permute-start.13 = (f32[616,128]{1,0:T(8,128)S(1)}, f32[616,128]{1,0:T(8,128)S(1)}, u32[]{:S(2)}, u32[]{:S(2)}) collective-permute-start(f32[616,128]{1,0:T(8,128)S(1)} %select_add_fusion.6), channel_id=1, source_target_pairs={{0,1},{1,0},{2,3},{3,2},{4,5},{5,4},{6,7},{7,6},{8,9},{9,8},{10,11... | collective-permute-start | bytes 946184 | tf_op jit(solution)/shard_map/ppermute | solution.py:304
  62.7 11.0 %collective-permute-start.16 = (f32[616,128]{1,0:T(8,128)S(1)}, f32[616,128]{1,0:T(8,128)S(1)}, u32[]{:S(2)}, u32[]{:S(2)}) collective-permute-start(f32[616,128]{1,0:T(8,128)S(1)} %select_add_fusion.5), channel_id=1, source_target_pairs={{0,1},{1,0},{2,3},{3,2},{4,5},{5,4},{6,7},{7,6},{8,9},{9,8},{10,11... | collective-permute-start | bytes 946184 | tf_op jit(solution)/shard_map/ppermute | solution.py:304
  66.1 8.2 %collective-permute-start.17 = (f32[616,128]{1,0:T(8,128)S(1)}, f32[616,128]{1,0:T(8,128)S(1)}, u32[]{:S(2)}, u32[]{:S(2)}) collective-permute-start(f32[616,128]{1,0:T(8,128)S(1)} %get-tuple-element.231), channel_id=1, source_target_pairs={{1,2},{2,1},{5,6},{6,5},{9,10},{10,9},{13,14},{14,13},{17,18},{18,... | collective-permute-start | bytes 946184 | tf_op jit(solution)/shard_map/ppermute | solution.py:304
  68.1 10.2 %collective-permute-start.14 = (f32[616,128]{1,0:T(8,128)S(1)}, f32[616,128]{1,0:T(8,128)S(1)}, u32[]{:S(2)}, u32[]{:S(2)}) collective-permute-start(f32[616,128]{1,0:T(8,128)S(1)} %select_add_fusion.4), channel_id=1, source_target_pairs={{0,1},{1,0},{2,3},{3,2},{4,5},{5,4},{6,7},{7,6},{8,9},{9,8},{10,11... | collective-permute-start | bytes 946184 | tf_op jit(solution)/shard_map/ppermute | solution.py:304
  72.2 6.7 %collective-permute-start.15 = (f32[616,128]{1,0:T(8,128)S(1)}, f32[616,128]{1,0:T(8,128)S(1)}, u32[]{:S(2)}, u32[]{:S(2)}) collective-permute-start(f32[616,128]{1,0:T(8,128)S(1)} %get-tuple-element.229), channel_id=1, source_target_pairs={{1,2},{2,1},{5,6},{6,5},{9,10},{10,9},{13,14},{14,13},{17,18},{18,... | collective-permute-start | bytes 946184 | tf_op jit(solution)/shard_map/ppermute | solution.py:304
  74.3 13.6 %collective-permute-start.20 = (f32[616,128]{1,0:T(8,128)S(1)}, f32[616,128]{1,0:T(8,128)S(1)}, u32[]{:S(2)}, u32[]{:S(2)}) collective-permute-start(f32[616,128]{1,0:T(8,128)S(1)} %get-tuple-element.240), channel_id=1, source_target_pairs={{1,2},{2,1},{5,6},{6,5},{9,10},{10,9},{13,14},{14,13},{17,18},{18,... | collective-permute-start | bytes 946184 | tf_op jit(solution)/shard_map/ppermute | solution.py:304
  75.0 12.4 %collective-permute-start.21 = (f32[616,128]{1,0:T(8,128)S(1)}, f32[616,128]{1,0:T(8,128)S(1)}, u32[]{:S(2)}, u32[]{:S(2)}) collective-permute-start(f32[616,128]{1,0:T(8,128)S(1)} %add.293), channel_id=1, source_target_pairs={{1,0},{2,3},{5,4},{6,7},{9,8},{10,11},{13,12},{14,15},{17,16},{18,... | collective-permute-start | bytes 946184 | tf_op jit(solution)/shard_map/ppermute | solution.py:304
  79.0 15.1 %collective-permute-start.19 = (f32[616,128]{1,0:T(8,128)S(1)}, f32[616,128]{1,0:T(8,128)S(1)}, u32[]{:S(2)}, u32[]{:S(2)}) collective-permute-start(f32[616,128]{1,0:T(8,128)S(1)} %add.289), channel_id=1, source_target_pairs={{1,0},{2,3},{5,4},{6,7},{9,8},{10,11},{13,12},{14,15},{17,16},{18,... | collective-permute-start | bytes 946184 | tf_op jit(solution)/shard_map/ppermute | solution.py:304
  80.3 14.3 %collective-permute-start.18 = (f32[616,128]{1,0:T(8,128)S(1)}, f32[616,128]{1,0:T(8,128)S(1)}, u32[]{:S(2)}, u32[]{:S(2)}) collective-permute-start(f32[616,128]{1,0:T(8,128)S(1)} %get-tuple-element.238), channel_id=1, source_target_pairs={{1,2},{2,1},{5,6},{6,5},{9,10},{10,9},{13,14},{14,13},{17,18},{18,... | collective-permute-start | bytes 946184 | tf_op jit(solution)/shard_map/ppermute | solution.py:304
  87.9 12.9 %collective-permute-start.23 = (f32[616,128]{1,0:T(8,128)S(1)}, f32[616,128]{1,0:T(8,128)S(1)}, u32[]{:S(2)}, u32[]{:S(2)}) collective-permute-start(f32[616,128]{1,0:T(8,128)S(1)} %add.299), channel_id=1, source_target_pairs={{1,0},{2,3},{5,4},{6,7},{9,8},{10,11},{13,12},{14,15},{17,16},{18,... | collective-permute-start | bytes 946184 | tf_op jit(solution)/shard_map/ppermute | solution.py:304
  94.7 9.6 %collective-permute-start.22 = (f32[616,128]{1,0:T(8,128)S(1)}, f32[616,128]{1,0:T(8,128)S(1)}, u32[]{:S(2)}, u32[]{:S(2)}) collective-permute-start(f32[616,128]{1,0:T(8,128)S(1)} %add.296), channel_id=1, source_target_pairs={{1,0},{2,3},{5,4},{6,7},{9,8},{10,11},{13,12},{14,15},{17,16},{18,... | collective-permute-start | bytes 946184 | tf_op jit(solution)/shard_map/ppermute | solution.py:304
  107.9 4.6 %collective-permute-start.27 = (f32[24,128]{1,0:T(8,128)S(1)}, f32[24,128]{1,0:T(8,128)S(1)}, u32[]{:S(2)}, u32[]{:S(2)}) collective-permute-start(f32[24,128]{1,0:T(8,128)S(1)} %add.306), channel_id=1, source_target_pairs={{0,24},{4,28},{8,16},{12,20},{16,8},{20,12},{24,0},{28,4},{1,25},{... | collective-permute-start | bytes 36872 | tf_op jit(solution)/shard_map/ppermute | solution.py:240
  113.4 7.9 %collective-permute-start.28 = (f32[616,128]{1,0:T(8,128)S(1)}, f32[616,128]{1,0:T(8,128)S(1)}, u32[]{:S(2)}, u32[]{:S(2)}) collective-permute-start(f32[616,128]{1,0:T(8,128)S(1)} %back_products.24), channel_id=1, source_target_pairs={{0,1},{3,2},{4,5},{7,6},{8,9},{11,10},{12,13},{15,14},{16,17},{19,... | collective-permute-start | bytes 946184 | tf_op jit(solution)/shard_map/ppermute | solution.py:304
  119.2 9.4 %collective-permute-start.30 = (f32[616,128]{1,0:T(8,128)S(1)}, f32[616,128]{1,0:T(8,128)S(1)}, u32[]{:S(2)}, u32[]{:S(2)}) collective-permute-start(f32[616,128]{1,0:T(8,128)S(1)} %back_products.25), channel_id=1, source_target_pairs={{0,1},{3,2},{4,5},{7,6},{8,9},{11,10},{12,13},{15,14},{16,17},{19,... | collective-permute-start | bytes 946184 | tf_op jit(solution)/shard_map/ppermute | solution.py:304
  121.4 12.1 %collective-permute-start.33 = (f32[616,128]{1,0:T(8,128)S(1)}, f32[616,128]{1,0:T(8,128)S(1)}, u32[]{:S(2)}, u32[]{:S(2)}) collective-permute-start(f32[616,128]{1,0:T(8,128)S(1)} %add.311), channel_id=1, source_target_pairs={{1,2},{2,1},{5,6},{6,5},{9,10},{10,9},{13,14},{14,13},{17,18},{18,... | collective-permute-start | bytes 946184 | tf_op jit(solution)/shard_map/ppermute | solution.py:304
  122.1 14.3 %collective-permute-start.32 = (f32[616,128]{1,0:T(8,128)S(1)}, f32[616,128]{1,0:T(8,128)S(1)}, u32[]{:S(2)}, u32[]{:S(2)}) collective-permute-start(f32[616,128]{1,0:T(8,128)S(1)} %back_products.26), channel_id=1, source_target_pairs={{0,1},{3,2},{4,5},{7,6},{8,9},{11,10},{12,13},{15,14},{16,17},{19,... | collective-permute-start | bytes 946184 | tf_op jit(solution)/shard_map/ppermute | solution.py:304
  128.6 14.6 %collective-permute-start.29 = (f32[616,128]{1,0:T(8,128)S(1)}, f32[616,128]{1,0:T(8,128)S(1)}, u32[]{:S(2)}, u32[]{:S(2)}) collective-permute-start(f32[616,128]{1,0:T(8,128)S(1)} %back_products.27), channel_id=1, source_target_pairs={{0,1},{3,2},{4,5},{7,6},{8,9},{11,10},{12,13},{15,14},{16,17},{19,... | collective-permute-start | bytes 946184 | tf_op jit(solution)/shard_map/ppermute | solution.py:304
  132.8 4.4 %collective-permute-start.31 = (f32[616,128]{1,0:T(8,128)S(1)}, f32[616,128]{1,0:T(8,128)S(1)}, u32[]{:S(2)}, u32[]{:S(2)}) collective-permute-start(f32[616,128]{1,0:T(8,128)S(1)} %add.313), channel_id=1, source_target_pairs={{1,2},{2,1},{5,6},{6,5},{9,10},{10,9},{13,14},{14,13},{17,18},{18,... | collective-permute-start | bytes 946184 | tf_op jit(solution)/shard_map/ppermute | solution.py:304
  133.6 16.4 %collective-permute-start.36 = (f32[616,128]{1,0:T(8,128)S(1)}, f32[616,128]{1,0:T(8,128)S(1)}, u32[]{:S(2)}, u32[]{:S(2)}) collective-permute-start(f32[616,128]{1,0:T(8,128)S(1)} %select_add_fusion.1), channel_id=1, source_target_pairs={{0,1},{1,0},{2,3},{3,2},{4,5},{5,4},{6,7},{7,6},{8,9},{9,8},{10,11... | collective-permute-start | bytes 946184 | tf_op jit(solution)/shard_map/ppermute | solution.py:304
  136.5 13.6 %collective-permute-start.37 = (f32[616,128]{1,0:T(8,128)S(1)}, f32[616,128]{1,0:T(8,128)S(1)}, u32[]{:S(2)}, u32[]{:S(2)}) collective-permute-start(f32[616,128]{1,0:T(8,128)S(1)} %add.315), channel_id=1, source_target_pairs={{1,2},{2,1},{5,6},{6,5},{9,10},{10,9},{13,14},{14,13},{17,18},{18,... | collective-permute-start | bytes 946184 | tf_op jit(solution)/shard_map/ppermute | solution.py:304
  143.2 13.5 %collective-permute-start.35 = (f32[616,128]{1,0:T(8,128)S(1)}, f32[616,128]{1,0:T(8,128)S(1)}, u32[]{:S(2)}, u32[]{:S(2)}) collective-permute-start(f32[616,128]{1,0:T(8,128)S(1)} %select_add_fusion.2), channel_id=1, source_target_pairs={{0,1},{1,0},{2,3},{3,2},{4,5},{5,4},{6,7},{7,6},{8,9},{9,8},{10,11... | collective-permute-start | bytes 946184 | tf_op jit(solution)/shard_map/ppermute | solution.py:304
  145.8 11.0 %collective-permute-start.34 = (f32[616,128]{1,0:T(8,128)S(1)}, f32[616,128]{1,0:T(8,128)S(1)}, u32[]{:S(2)}, u32[]{:S(2)}) collective-permute-start(f32[616,128]{1,0:T(8,128)S(1)} %add.312), channel_id=1, source_target_pairs={{1,2},{2,1},{5,6},{6,5},{9,10},{10,9},{13,14},{14,13},{17,18},{18,... | collective-permute-start | bytes 946184 | tf_op jit(solution)/shard_map/ppermute | solution.py:304
  151.2 12.2 %collective-permute-start.40 = (f32[616,128]{1,0:T(8,128)S(1)}, f32[616,128]{1,0:T(8,128)S(1)}, u32[]{:S(2)}, u32[]{:S(2)}) collective-permute-start(f32[616,128]{1,0:T(8,128)S(1)} %select_add_fusion), channel_id=1, source_target_pairs={{0,1},{1,0},{2,3},{3,2},{4,5},{5,4},{6,7},{7,6},{8,9},{9,8},{10,11... | collective-permute-start | bytes 946184 | tf_op jit(solution)/shard_map/ppermute | solution.py:304
  153.8 10.3 %collective-permute-start.41 = (f32[616,128]{1,0:T(8,128)S(1)}, f32[616,128]{1,0:T(8,128)S(1)}, u32[]{:S(2)}, u32[]{:S(2)}) collective-permute-start(f32[616,128]{1,0:T(8,128)S(1)} %get-tuple-element.299), channel_id=1, source_target_pairs={{1,2},{2,1},{5,6},{6,5},{9,10},{10,9},{13,14},{14,13},{17,18},{18,... | collective-permute-start | bytes 946184 | tf_op jit(solution)/shard_map/ppermute | solution.py:304
  157.3 10.2 %collective-permute-start.38 = (f32[616,128]{1,0:T(8,128)S(1)}, f32[616,128]{1,0:T(8,128)S(1)}, u32[]{:S(2)}, u32[]{:S(2)}) collective-permute-start(f32[616,128]{1,0:T(8,128)S(1)} %select_add_fusion.3), channel_id=1, source_target_pairs={{0,1},{1,0},{2,3},{3,2},{4,5},{5,4},{6,7},{7,6},{8,9},{9,8},{10,11... | collective-permute-start | bytes 946184 | tf_op jit(solution)/shard_map/ppermute | solution.py:304
  159.9 8.2 %collective-permute-start.39 = (f32[616,128]{1,0:T(8,128)S(1)}, f32[616,128]{1,0:T(8,128)S(1)}, u32[]{:S(2)}, u32[]{:S(2)}) collective-permute-start(f32[616,128]{1,0:T(8,128)S(1)} %get-tuple-element.296), channel_id=1, source_target_pairs={{1,2},{2,1},{5,6},{6,5},{9,10},{10,9},{13,14},{14,13},{17,18},{18,... | collective-permute-start | bytes 946184 | tf_op jit(solution)/shard_map/ppermute | solution.py:304
  164.1 15.7 %collective-permute-start.44 = (f32[616,128]{1,0:T(8,128)S(1)}, f32[616,128]{1,0:T(8,128)S(1)}, u32[]{:S(2)}, u32[]{:S(2)}) collective-permute-start(f32[616,128]{1,0:T(8,128)S(1)} %get-tuple-element.310), channel_id=1, source_target_pairs={{1,2},{2,1},{5,6},{6,5},{9,10},{10,9},{13,14},{14,13},{17,18},{18,... | collective-permute-start | bytes 946184 | tf_op jit(solution)/shard_map/ppermute | solution.py:304
  164.8 14.5 %collective-permute-start.45 = (f32[616,128]{1,0:T(8,128)S(1)}, f32[616,128]{1,0:T(8,128)S(1)}, u32[]{:S(2)}, u32[]{:S(2)}) collective-permute-start(f32[616,128]{1,0:T(8,128)S(1)} %add.332), channel_id=1, source_target_pairs={{1,0},{2,3},{5,4},{6,7},{9,8},{10,11},{13,12},{14,15},{17,16},{18,... | collective-permute-start | bytes 946184 | tf_op jit(solution)/shard_map/ppermute | solution.py:304
  168.2 18.4 %collective-permute-start.42 = (f32[616,128]{1,0:T(8,128)S(1)}, f32[616,128]{1,0:T(8,128)S(1)}, u32[]{:S(2)}, u32[]{:S(2)}) collective-permute-start(f32[616,128]{1,0:T(8,128)S(1)} %get-tuple-element.307), channel_id=1, source_target_pairs={{1,2},{2,1},{5,6},{6,5},{9,10},{10,9},{13,14},{14,13},{17,18},{18,... | collective-permute-start | bytes 946184 | tf_op jit(solution)/shard_map/ppermute | solution.py:304
  168.9 17.2 %collective-permute-start.43 = (f32[616,128]{1,0:T(8,128)S(1)}, f32[616,128]{1,0:T(8,128)S(1)}, u32[]{:S(2)}, u32[]{:S(2)}) collective-permute-start(f32[616,128]{1,0:T(8,128)S(1)} %add.328), channel_id=1, source_target_pairs={{1,0},{2,3},{5,4},{6,7},{9,8},{10,11},{13,12},{14,15},{17,16},{18,... | collective-permute-start | bytes 946184 | tf_op jit(solution)/shard_map/ppermute | solution.py:304
  179.9 12.7 %collective-permute-start.47 = (f32[616,128]{1,0:T(8,128)S(1)}, f32[616,128]{1,0:T(8,128)S(1)}, u32[]{:S(2)}, u32[]{:S(2)}) collective-permute-start(f32[616,128]{1,0:T(8,128)S(1)} %add.338), channel_id=1, source_target_pairs={{1,0},{2,3},{5,4},{6,7},{9,8},{10,11},{13,12},{14,15},{17,16},{18,... | collective-permute-start | bytes 946184 | tf_op jit(solution)/shard_map/ppermute | solution.py:304
  186.7 9.2 %collective-permute-start.46 = (f32[616,128]{1,0:T(8,128)S(1)}, f32[616,128]{1,0:T(8,128)S(1)}, u32[]{:S(2)}, u32[]{:S(2)}) collective-permute-start(f32[616,128]{1,0:T(8,128)S(1)} %add.335), channel_id=1, source_target_pairs={{1,0},{2,3},{5,4},{6,7},{9,8},{10,11},{13,12},{14,15},{17,16},{18,... | collective-permute-start | bytes 946184 | tf_op jit(solution)/shard_map/ppermute | solution.py:304
  198.2 5.1 %collective-permute-start.50 = (f32[24,128]{1,0:T(8,128)S(1)}, f32[24,128]{1,0:T(8,128)S(1)}, u32[]{:S(2)}, u32[]{:S(2)}) collective-permute-start(f32[24,128]{1,0:T(8,128)S(1)} %add.345), channel_id=1, source_target_pairs={{0,16},{4,20},{8,24},{12,28},{16,0},{20,4},{24,8},{28,12},{1,17},{... | collective-permute-start | bytes 36872 | tf_op jit(solution)/shard_map/ppermute | solution.py:240
  199.2 4.6 %collective-permute-start.51 = (f32[24,128]{1,0:T(8,128)S(1)}, f32[24,128]{1,0:T(8,128)S(1)}, u32[]{:S(2)}, u32[]{:S(2)}) collective-permute-start(f32[24,128]{1,0:T(8,128)S(1)} %add.345), channel_id=1, source_target_pairs={{0,24},{4,28},{8,16},{12,20},{16,8},{20,12},{24,0},{28,4},{1,25},{... | collective-permute-start | bytes 36872 | tf_op jit(solution)/shard_map/ppermute | solution.py:240
  200.5 3.7 %collective-permute-start.49 = (f32[24,128]{1,0:T(8,128)S(1)}, f32[24,128]{1,0:T(8,128)S(1)}, u32[]{:S(2)}, u32[]{:S(2)}) collective-permute-start(f32[24,128]{1,0:T(8,128)S(1)} %add.345), channel_id=1, source_target_pairs={{0,8},{4,12},{8,0},{12,4},{16,24},{20,28},{24,16},{28,20},{1,9},{5... | collective-permute-start | bytes 36872 | tf_op jit(solution)/shard_map/ppermute | solution.py:240
  204.3 4.5 %collective-permute-start.53 = (f32[1,128]{1,0:T(1,128)S(1)}, f32[1,128]{1,0:T(1,128)S(1)}, u32[]{:S(2)}, u32[]{:S(2)}) collective-permute-start(f32[1,128]{1,0:T(1,128)S(1)} %bitcast.40), channel_id=1, source_target_pairs={{0,2},{1,3},{2,0},{3,1},{4,6},{5,7},{6,4},{7,5},{8,10},{9,11},{10,... | collective-permute-start | bytes 1544 | tf_op jit(solution)/shard_map/ppermute | solution.py:240
  204.3 5.4 %collective-permute-start.54 = (f32[1,128]{1,0:T(1,128)S(1)}, f32[1,128]{1,0:T(1,128)S(1)}, u32[]{:S(2)}, u32[]{:S(2)}) collective-permute-start(f32[1,128]{1,0:T(1,128)S(1)} %bitcast.41), channel_id=1, source_target_pairs={{0,3},{1,2},{2,1},{3,0},{4,7},{5,6},{6,5},{7,4},{8,11},{9,10},{10,... | collective-permute-start | bytes 1544 | tf_op jit(solution)/shard_map/ppermute | solution.py:240
  (16 other events, 97.9 us)
